TPU v7x, 32 devices: a whole 2x2x4 slice. The times are simulated.
32 devices in a mesh: scene: 2 (over x), img: 16 (over z, y, core).
Axes of the slice: x: 2, y: 2, z: 4, core: 2. Of those that a mesh axis runs over, the one named last changes fastest.
Arguments:
- enc_tokens: bfloat16 [1024, 16, 1024], P(('scene', 'img')), parts along dimension 0, may hold values from -6 to 6
- pair_list: int32 [2048, 2], P(('scene', 'img')), parts along dimension 0, may hold values from -1 to 511, as said below
- w_embed: bfloat16 [1024, 768], replicated, may hold values from -0.1875 to 0.1875
- w_query: bfloat16 [768, 768], replicated, may hold values from -0.21875 to 0.21875
- w_key: bfloat16 [768, 768], replicated, may hold values from -0.21875 to 0.21875
- w_value: bfloat16 [768, 768], replicated, may hold values from -0.21875 to 0.21875
- w_out: bfloat16 [768, 768], replicated, may hold values from -0.21875 to 0.21875
- w_head: bfloat16 [768, 28], replicated, may hold values from -0.21875 to 0.21875
Outputs:
- points: float32 [1024, 3, 16], P(('scene', 'img')), parts along dimension 0
- descriptors: float32 [1024, 24, 16], P(('scene', 'img')), parts along dimension 0
- confidence: float32 [1024, 16], P(('scene', 'img')), parts along dimension 0
There are 2 independent parts, one for each index of `scene`. A program takes and returns all parts, laid end to end along the dimension named above; an argument that names none is the same for every part. Nothing has to cross between parts.
Inputs may be any that keep to these rules, and one draw needn't show every extreme that they name: `pair_list`: the 64 rows of one executor (index of img) name in column 0 an image held by that executor and in column 1 a partner image held by another executor; the used rows come first and the rest hold -1 in both columns. Every executor uses 64 - 64 // 4 rows or more, and some executor uses all. The partners that one executor names on one image owner are distinct and at most 5; some executor names 5 on one owner, and some image owner is named 5 times by every other executor.
All inputs are finite; a program needn't handle non-finite values.
Results may differ from a plain program's by a relative error of at most 0.0055.
Values may be sent and summed in bfloat16 or wider, within the bound.
No kernel may reach another device: no remote copies, remote signals or barrier semaphores. Data moves between devices by JAX's collectives and lax.ppermute only.
A program may use at most 128 MiB of HBM per device.

v0:
```python
import jax
import jax.numpy as jnp
from jax import lax
from jax.sharding import PartitionSpec as P

HEADS = 12


def layer_norm(field):
    average = jnp.mean(field, axis=-1, keepdims=True)
    centred = field - average
    variance = jnp.mean(centred * centred, axis=-1, keepdims=True)
    return centred * lax.rsqrt(variance + 1e-06)


def project(matrix_rows, weight):
    return jnp.dot(matrix_rows, weight, preferred_element_type=jnp.float32).astype(jnp.bfloat16)


def decode_terms(query_rows, key_part, value_part, base_rows, live, w_out, w_head):
    count, patches, model_width = query_rows.shape
    head_count = HEADS
    head_dim = model_width // head_count
    channels = w_head.shape[1]
    score_scale = 1.0 / head_dim**0.5
    query_heads = query_rows.reshape(count, patches, head_count, head_dim)
    key_heads = key_part.reshape(count, patches, head_count, head_dim)
    value_heads = value_part.reshape(count, patches, head_count, head_dim)
    scores = (
        jnp.einsum("bqhd,bkhd->bhqk", query_heads, key_heads, preferred_element_type=jnp.float32)
        * score_scale
    )
    exponent = jnp.exp(scores)
    weights = (exponent / jnp.sum(exponent, axis=-1, keepdims=True)).astype(jnp.bfloat16)
    attended = jnp.einsum(
        "bhqk,bkhd->bqhd", weights, value_heads, preferred_element_type=jnp.float32
    ).astype(jnp.bfloat16)
    attended = attended.reshape(count * patches, model_width)
    updated = base_rows.reshape(count * patches, model_width).astype(jnp.float32) + jnp.dot(
        attended, w_out, preferred_element_type=jnp.float32
    )
    head_input = layer_norm(updated).astype(jnp.bfloat16)
    head_out = jnp.dot(head_input, w_head, preferred_element_type=jnp.float32).reshape(
        count, patches, channels
    )
    confidence_weight = 1.0 + jnp.exp(head_out[..., 3:4])
    weighted = jnp.concatenate(
        [
            confidence_weight * head_out[..., 0:3],
            confidence_weight * head_out[..., 4:],
            confidence_weight,
        ],
        axis=-1,
    )
    weighted = weighted * live.astype(jnp.float32)[:, None, None]
    return jnp.transpose(weighted, (0, 2, 1)).reshape(count, channels * patches)


def per_device(enc_tokens, pair_list, w_embed, w_query, w_key, w_value, w_out, w_head):
    groups = lax.axis_size("img")
    position = lax.axis_index("img")
    img_dev, patches, enc_width = enc_tokens.shape
    model_width = w_query.shape[0]
    channels = w_head.shape[1]
    pair_dev = pair_list.shape[0]
    per_owner = (pair_dev + groups - 2) // (groups - 1)
    slot_count = groups * per_owner
    embedded = project(enc_tokens.reshape(img_dev * patches, enc_width), w_embed)
    normed = layer_norm(embedded.astype(jnp.float32)).astype(jnp.bfloat16)
    embedded_rows = embedded.reshape(img_dev, patches, model_width)
    partner = pair_list[:, 1]
    in_use = partner >= 0
    local_image = jnp.clip(pair_list[:, 0] - position * img_dev, 0, img_dev - 1)
    owner_index = jnp.where(in_use, partner // img_dev, groups)
    position_list = jnp.arange(pair_dev, dtype=jnp.int32)
    earlier = (owner_index[:, None] == owner_index[None, :]) & (
        position_list[None, :] < position_list[:, None]
    )
    order_rank = jnp.sum(earlier.astype(jnp.int32), axis=1)
    slot_index = jnp.where(in_use, owner_index * per_owner + order_rank, slot_count)
    slot_ids = jnp.arange(slot_count, dtype=jnp.int32)
    slot_match = slot_index[None, :] == slot_ids[:, None]
    wanted = jnp.sum(jnp.where(slot_match, (partner % img_dev + 1)[None, :], 0), axis=1) - 1
    own_ids = jnp.arange(img_dev, dtype=jnp.int32)
    key_rows = project(normed, w_key).reshape(img_dev, patches, model_width)
    value_rows = project(normed, w_value).reshape(img_dev, patches, model_width)
    requested = lax.all_to_all(
        wanted.reshape(groups, per_owner), "img", split_axis=0, concat_axis=0, tiled=True
    )
    requested_flat = requested.reshape(slot_count)
    served_mask = (requested_flat >= 0)[:, None, None]
    chosen_rows = jnp.clip(requested_flat, 0, img_dev - 1)
    send_tokens = jnp.where(served_mask, embedded_rows[chosen_rows], jnp.zeros((), jnp.bfloat16))
    send_tokens = send_tokens.reshape(groups, per_owner, patches, model_width)
    fetch_index = jnp.clip(slot_index, 0, slot_count - 1)
    queries = project(normed, w_query).reshape(img_dev, patches, model_width)
    send_queries = jnp.where(served_mask, queries[chosen_rows], jnp.zeros((), jnp.bfloat16))
    send_queries = send_queries.reshape(groups, per_owner, patches, model_width)
    got_tokens, got_queries = (
        lax.all_to_all(send_tokens, "img", split_axis=0, concat_axis=0, tiled=True),
        lax.all_to_all(send_queries, "img", split_axis=0, concat_axis=0, tiled=True),
    )
    fetched = got_tokens.reshape(slot_count, patches, model_width)[fetch_index]
    fetched_queries = got_queries.reshape(slot_count, patches, model_width)[fetch_index]
    weighted = decode_terms(
        fetched_queries,
        key_rows[local_image],
        value_rows[local_image],
        fetched,
        in_use,
        w_out,
        w_head,
    )
    slot_terms = jnp.dot(slot_match.astype(jnp.float32), weighted, precision=lax.Precision.HIGHEST)
    returned = lax.all_to_all(
        slot_terms.reshape(groups, per_owner, channels * patches),
        "img",
        split_axis=0,
        concat_axis=0,
        tiled=True,
    )
    owned_match = (requested_flat[None, :] == own_ids[:, None]).astype(jnp.float32)
    totals = jnp.dot(
        owned_match,
        returned.reshape(slot_count, channels * patches),
        precision=lax.Precision.HIGHEST,
    )
    totals = totals.reshape(img_dev, channels, patches)
    confidence = totals[:, channels - 1, :]
    divisor = 1.0 + confidence[:, None, :]
    points = totals[:, 0:3, :] / divisor
    descriptors = totals[:, 3 : channels - 1, :] / divisor
    return (points, descriptors, confidence)


def solution(mesh):
    return jax.shard_map(
        per_device,
        mesh=mesh,
        in_specs=(
            P(("scene", "img"), None, None),
            P(("scene", "img"), None),
            P(),
            P(),
            P(),
            P(),
            P(),
            P(),
        ),
        out_specs=(
            P(("scene", "img"), None, None),
            P(("scene", "img"), None, None),
            P(("scene", "img"), None),
        ),
        check_vma=False,
    )
```

profile of v0, /device:TPU:0, one launch (start us, length us, event | category | flops | bytes accessed | tf_op | source)
XLA Modules:
  0.0 157.5 jit_solution(4008299377462764272)
XLA Ops:
  0.7 0.8 fusion.31
  1.5 0.8 fusion.30
  2.4 0.3 copy-done.9
  2.7 0.7 fusion.27
  3.4 0.6 copy-done.7
  4.1 0.7 sub.40
  4.8 7.4 %all-to-all-start = ((s32[16,1,5]{2,1,0:T(1,128)}), s32[16,1,5]{2,1,0:T(1,128)S(1)}, u32[]{:S(2)}, u32[]{:S(2)}) async-start(s32[16,1,5]{2,1,0:T(1,128)} %bitcast.2), calls=%async_computation | async-start | bytes 16384 | tf_op jit(solution)/shard_map/all_to_all | solution.py:87
  12.2 2.4 %convert_reduce_fusion = (f32[512]{0:T(512)S(1)}, bf16[512,768]{1,0:T(8,128)(2,1)S(1)}) fusion(bf16[512,1024]{1,0:T(8,128)(2,1)} %bitcast.94, bf16[1024,768]{1,0:T(8,128)(2,1)S(1)} %copy-done), kind=kOutput, calls=%fused_computation.19 | convolution fusion | flops 806485504 | bytes 3409920 | tf_op jit(solution)/shard_map/dot_general | solution.py:17
  14.6 0.4 fusion.11
  15.0 0.8 convolution_convert_fusion.1
  15.8 2.7 %all-to-all-done = s32[16,1,5]{2,1,0:T(1,128)S(1)} async-done(((s32[16,1,5]{2,1,0:T(1,128)}), s32[16,1,5]{2,1,0:T(1,128)S(1)}, u32[]{:S(2)}, u32[]{:S(2)}) %all-to-all-start) | async-done | bytes 352 | tf_op jit(solution)/shard_map/all_to_all | solution.py:87
  18.8 2.1 %gather_fusion.3 = bf16[80,16,768]{2,1,0:T(8,128)(2,1)} fusion(bf16[32,16,768]{2,1,0:T(8,128)(2,1)S(1)} %bitcast.84, s32[1024]{0:T(1024)S(1)} %pad_clamp_fusion.2), kind=kCustom, calls=%fused_computation.3 | custom fusion | bytes 3932480 | tf_op jit(solution)/shard_map/gather | solution.py:97
  21.0 2.1 %gather_fusion = bf16[80,16,768]{2,1,0:T(8,128)(2,1)} fusion(bf16[32,16,768]{2,1,0:T(8,128)(2,1)S(1)} %bitcast.77, s32[1024]{0:T(1024)S(1)} %pad_clamp_fusion.2), kind=kCustom, calls=%fused_computation | custom fusion | bytes 3932480 | tf_op jit(solution)/shard_map/gather | solution.py:93
  23.1 3.8 %broadcast_select_fusion = (bf16[16,5,16,768]{3,2,1,0:T(8,128)(2,1)S(1)}, bf16[16,5,16,768]{3,2,1,0:T(8,128)(2,1)}) fusion(bf16[16,5,16,768]{3,2,1,0:T(8,128)(2,1)} %bitcast.81, pred[16,5]{1,0:T(8,128)(4,1)S(1)} %copy.102, bf16[16,5,16,768]{3,2,1,0:T(8,128)(2,1)} %bitcast.82), kind=kLoop, calls=%fused_computation.20 | loop fusion | flops 1966080 | bytes 7864400 | tf_op jit(solution)/shard_map/jit(_where)/select_n | solution.py:97
  26.9 48.3 %all_to_all.21 = bf16[16,5,16,768]{3,2,1,0:T(8,128)(2,1)} all-to-all(bf16[16,5,16,768]{3,2,1,0:T(8,128)(2,1)S(1)} %get-tuple-element.27), channel_id=1, replica_groups=mesh['scene'=2,'img'=16] {'img'}, dimensions={0} | all-to-all | bytes 3932160 | tf_op jit(solution)/shard_map/all_to_all | solution.py:101
  75.2 4.8 %all-to-all-start.1 = ((bf16[16,5,16,768]{3,2,1,0:T(8,128)(2,1)}), bf16[16,5,16,768]{3,2,1,0:T(8,128)(2,1)}, u32[]{:S(2)}, u32[]{:S(2)}) async-start(bf16[16,5,16,768]{3,2,1,0:T(8,128)(2,1)} %get-tuple-element.28), calls=%async_computation.1 | async-start | bytes 3932160 | tf_op jit(solution)/shard_map/all_to_all | solution.py:100
  80.0 0.8 convolution_convert_fusion
  80.8 0.6 gather_fusion.5
  81.5 3.9 %reshape.242 = bf16[64,16,12,64]{3,2,1,0:T(8,128)(2,1)} reshape(bf16[64,16,768]{2,1,0:T(8,128)(2,1)S(1)} %gather_fusion.5) | data formatting | bytes 3145728 | tf_op jit(solution)/shard_map/reshape | solution.py:27
  85.4 2.1 %convolution_convert_fusion.2 = bf16[512,768]{1,0:T(8,128)(2,1)S(1)} fusion(bf16[768,768]{1,0:T(8,128)(2,1)} %param.13, bf16[512,768]{1,0:T(8,128)(2,1)S(1)} %get-tuple-element.32, f32[512]{0:T(512)S(1)} %add_rsqrt_fusion.1, f32[512]{0:T(512)S(1)} %broadcast_multiply_fusion.1), kind=kOutput, calls=%fused_computation.33 | convolution fusion | flops 605945856 | bytes 2756608 | tf_op jit(solution)/shard_map/dot_general | solution.py:17
  87.5 0.6 gather_fusion.2
  88.2 3.9 %reshape.237 = bf16[64,16,12,64]{3,2,1,0:T(8,128)(2,1)} reshape(bf16[64,16,768]{2,1,0:T(8,128)(2,1)S(1)} %gather_fusion.2) | data formatting | bytes 3145728 | tf_op jit(solution)/shard_map/reshape | solution.py:28
  92.0 0.7 fusion.29
  92.7 1.2 fusion.32
  93.9 0.6 gather_fusion.4
  94.6 3.9 %reshape.240 = bf16[64,16,12,64]{3,2,1,0:T(8,128)(2,1)} reshape(bf16[64,16,768]{2,1,0:T(8,128)(2,1)S(1)} %gather_fusion.4) | data formatting | bytes 3145728 | tf_op jit(solution)/shard_map/reshape | solution.py:26
  98.5 6.2 %fusion = (f32[64,12,16]{2,1,0:T(8,128)S(1)}, f32[64,12,16,16]{2,3,1,0:T(8,128)S(1)}) fusion(bf16[64,16,12,64]{3,2,1,0:T(8,128)(2,1)} %reshape.242, bf16[64,16,12,64]{3,2,1,0:T(8,128)(2,1)} %reshape.240), kind=kOutput, calls=%fused_computation.8 | convolution fusion | flops 25546752 | bytes 3981312 | tf_op jit(solution)/shard_map/bqhd,bkhd->bhqk/dot_general | solution.py:30
  104.7 2.1 %convert_bitcast_fusion = bf16[64,16,12,64]{3,1,2,0:T(8,128)(2,1)S(1)} fusion(f32[64,12,16,16]{2,3,1,0:T(8,128)S(1)} %get-tuple-element.34, f32[64,12,16]{2,1,0:T(8,128)S(1)} %get-tuple-element.33, bf16[64,16,12,64]{3,2,1,0:T(8,128)(2,1)S(1)} %copy-done.3), kind=kOutput, calls=%fused_computation.16 | convolution fusion | flops 26542080 | bytes 3981312 | tf_op jit(solution)/shard_map/bhqk,bkhd->bqhd/dot_general | solution.py:35
  106.8 3.1 %copy.109 = bf16[64,16,12,64]{3,2,1,0:T(8,128)(2,1)} copy(bf16[64,16,12,64]{3,1,2,0:T(8,128)(2,1)S(1)} %convert_bitcast_fusion) | data formatting | bytes 3145728 | tf_op jit(solution)/shard_map/convert_element_type | solution.py:37
  109.9 5.2 %reshape.243 = bf16[1024,768]{1,0:T(8,128)(2,1)S(1)} reshape(bf16[64,16,12,64]{3,2,1,0:T(8,128)(2,1)} %copy.109) | data formatting | bytes 3145728 | tf_op jit(solution)/shard_map/reshape | solution.py:38
  115.1 3.6 %all-to-all-done.1 = bf16[16,5,16,768]{3,2,1,0:T(8,128)(2,1)} async-done(((bf16[16,5,16,768]{3,2,1,0:T(8,128)(2,1)}), bf16[16,5,16,768]{3,2,1,0:T(8,128)(2,1)}, u32[]{:S(2)}, u32[]{:S(2)}) %all-to-all-start.1) | async-done | bytes 1966112 | tf_op jit(solution)/shard_map/all_to_all | solution.py:100
  118.7 2.2 %gather_fusion.1 = bf16[64,16,768]{2,1,0:T(8,128)(2,1)S(1)} fusion(bf16[80,16,768]{2,1,0:T(8,128)(2,1)} %bitcast.9, s32[1024]{0:T(1024)S(1)} %pad_clamp_fusion.1), kind=kCustom, calls=%fused_computation.1 | custom fusion | bytes 3145984 | tf_op jit(solution)/shard_map/gather | solution.py:103
  120.9 2.0 %bitcast_convert_fusion = f32[1024,768]{1,0:T(8,128)} fusion(bf16[64,16,768]{2,1,0:T(8,128)(2,1)S(1)} %gather_fusion.1), kind=kLoop, calls=%fused_computation.28 | loop fusion | flops 786432 | bytes 4718592 | tf_op jit(solution)/shard_map/convert_element_type | solution.py:39
  122.9 3.6 %copy.110 = f32[1024,768]{0,1:T(8,128)} copy(f32[1024,768]{1,0:T(8,128)} %bitcast_convert_fusion) | data formatting | bytes 6291456 | tf_op jit(solution)/shard_map/convert_element_type | solution.py:39
  126.5 3.4 %fusion.39 = (f32[1024]{0:T(1024)S(1)}, f32[1024,768]{0,1:T(8,128)S(1)}) fusion(f32[1024,768]{0,1:T(8,128)} %copy.110, bf16[1024,768]{1,0:T(8,128)(2,1)S(1)} %reshape.243, bf16[768,768]{1,0:T(8,128)(2,1)S(1)} %copy-done.4), kind=kOutput, calls=%fused_computation.95 | convolution fusion | flops 1209531392 | bytes 9048064 | tf_op jit(solution)/shard_map/dot_general | solution.py:39
  129.9 0.4 multiply_reduce_fusion
  130.3 0.4 copy-done.5
  130.7 0.6 fusion.13
  132.1 0.3 slice_multiply_fusion
  133.1 0.3 fusion.18
  133.4 0.8 copy.118
  134.2 10.8 %all-to-all-start.3 = ((f32[16,5,448]{2,1,0:T(8,128)}), f32[16,5,448]{2,1,0:T(8,128)S(1)}, u32[]{:S(2)}, u32[]{:S(2)}) async-start(f32[16,5,448]{2,1,0:T(8,128)} %copy.118), calls=%async_computation.3 | async-start | bytes 524288 | tf_op jit(solution)/shard_map/all_to_all | solution.py:115
  145.0 0.5 broadcast.324
  145.5 0.7 reduce.3
  146.3 8.8 %all-to-all-done.3 = f32[16,5,448]{2,1,0:T(8,128)S(1)} async-done(((f32[16,5,448]{2,1,0:T(8,128)}), f32[16,5,448]{2,1,0:T(8,128)S(1)}, u32[]{:S(2)}, u32[]{:S(2)}) %all-to-all-start.3) | async-done | bytes 143392 | tf_op jit(solution)/shard_map/all_to_all | solution.py:115
  155.5 0.6 fusion.38
  156.2 0.7 copy.122
  156.9 0.6 copy.121
  (57 shorter events, 2.7 us)
Async XLA Ops:
  0.6 11.6 %copy-start = (bf16[1024,768]{1,0:T(8,128)(2,1)S(1)}, bf16[1024,768]{1,0:T(8,128)(2,1)}, u32[]{:S(2)}) copy-start(bf16[1024,768]{1,0:T(8,128)(2,1)} %param.10) | copy-start | bytes 4718596
  2.2 0.5 copy-start.9
  2.7 1.4 copy-start.10
  3.4 0.6 copy-start.7
  4.8 13.7 %all-to-all-start = ((s32[16,1,5]{2,1,0:T(1,128)}), s32[16,1,5]{2,1,0:T(1,128)S(1)}, u32[]{:S(2)}, u32[]{:S(2)}) async-start(s32[16,1,5]{2,1,0:T(1,128)} %bitcast.2), calls=%async_computation | async-start | bytes 16384 | tf_op jit(solution)/shard_map/all_to_all | solution.py:87
  12.2 2.8 %copy-start.12 = (bf16[768,768]{1,0:T(8,128)(2,1)S(1)}, bf16[768,768]{1,0:T(8,128)(2,1)}, u32[]{:S(2)}) copy-start(bf16[768,768]{1,0:T(8,128)(2,1)} %param.11) | copy-start | bytes 3538948
  75.2 4.8 %copy-start.13 = (bf16[768,768]{1,0:T(8,128)(2,1)S(1)}, bf16[768,768]{1,0:T(8,128)(2,1)}, u32[]{:S(2)}) copy-start(bf16[768,768]{1,0:T(8,128)(2,1)} %param.12) | copy-start | bytes 3538948
  75.2 43.5 %all-to-all-start.1 = ((bf16[16,5,16,768]{3,2,1,0:T(8,128)(2,1)}), bf16[16,5,16,768]{3,2,1,0:T(8,128)(2,1)}, u32[]{:S(2)}, u32[]{:S(2)}) async-start(bf16[16,5,16,768]{3,2,1,0:T(8,128)(2,1)} %get-tuple-element.28), calls=%async_computation.1 | async-start | bytes 3932160 | tf_op jit(solution)/shard_map/all_to_all | solution.py:100
  88.1 3.9 %copy-start.6 = (s32[64,2]{0,1:T(2,128)S(1)}, s32[64,2]{0,1:T(2,128)}, u32[]{:S(2)}) copy-start(s32[64,2]{0,1:T(2,128)} %param.9) | copy-start | bytes 1540
  88.1 5.8 %copy-start.2 = (bf16[16,5,16,768]{3,2,1,0:T(8,128)(2,1)S(1)}, bf16[16,5,16,768]{3,2,1,0:T(8,128)(2,1)}, u32[]{:S(2)}) copy-start(bf16[16,5,16,768]{3,2,1,0:T(8,128)(2,1)} %all_to_all.21) | copy-start | bytes 5898244
  98.5 6.2 %copy-start.3 = (bf16[64,16,12,64]{3,2,1,0:T(8,128)(2,1)S(1)}, bf16[64,16,12,64]{3,2,1,0:T(8,128)(2,1)}, u32[]{:S(2)}) copy-start(bf16[64,16,12,64]{3,2,1,0:T(8,128)(2,1)} %reshape.237) | copy-start | bytes 4718596
  122.9 3.7 %copy-start.4 = (bf16[768,768]{1,0:T(8,128)(2,1)S(1)}, bf16[768,768]{1,0:T(8,128)(2,1)}, u32[]{:S(2)}) copy-start(bf16[768,768]{1,0:T(8,128)(2,1)} %param.14) | copy-start | bytes 3538948
  129.9 0.8 copy-start.5
  131.5 1.5 copy-start.11
  131.8 1.2 copy-start.8
  133.0 24.5 %copy-start.1 = (bf16[1024,768]{1,0:T(8,128)(2,1)S(1)}, bf16[1024,768]{1,0:T(8,128)(2,1)}, u32[]{:S(2)}) copy-start(bf16[1024,768]{1,0:T(8,128)(2,1)} %param.10) | copy-start | bytes 4718596
  134.2 20.8 %all-to-all-start.3 = ((f32[16,5,448]{2,1,0:T(8,128)}), f32[16,5,448]{2,1,0:T(8,128)S(1)}, u32[]{:S(2)}, u32[]{:S(2)}) async-start(f32[16,5,448]{2,1,0:T(8,128)} %copy.118), calls=%async_computation.3 | async-start | bytes 524288 | tf_op jit(solution)/shard_map/all_to_all | solution.py:115
where the time goes:
time: 158 us
  blocking collectives  48.3 us (31%)
  local copies, waits for them, and re-layouts  38.3 us (24%)
  starting transfers between devices  22.9 us (14%)
  matrix products  19.1 us (12%)
  waiting for transfers between devices  15 us (9%)
  other arithmetic  12.9 us (8%)
    all_to_all x1, blocking collectives, per_device(): lax.all_to_all(send_queries, 'img', split_axis=0, concat_axis=0, tiled=True)  48.3 us
    all_to_all x1, starting transfers between devices, per_device(): lax.all_to_all(slot_terms.reshape(groups, per_owner, channels * patches),...  10.8 us
    all_to_all x1, waiting for transfers between devices, per_device(): lax.all_to_all(slot_terms.reshape(groups, per_owner, channels * patches),...  8.77 us
    all_to_all x1, starting transfers between devices, per_device(): lax.all_to_all(wanted.reshape(groups, per_owner), 'img', split_axis=0, co...  7.39 us
    dot_general x1, matrix products, decode_terms(): jnp.einsum('bqhd,bkhd->bhqk', query_heads, key_heads, preferred_element_t...  6.22 us
    dot_general x4, matrix products, project(): jnp.dot(matrix_rows, weight, preferred_element_type=jnp.float32)  6.16 us
    reshape x1, local copies, waits for them, and re-layouts, decode_terms(): attended = attended.reshape(count * patches, model_width)  5.21 us
    all_to_all x1, starting transfers between devices, per_device(): lax.all_to_all(send_tokens, 'img', split_axis=0, concat_axis=0, tiled=True)  4.75 us
  transfers between devices with their start and end apart: 3, of which 3 were waited for; matrix products, arithmetic and copies ran while one was open for 25% of the time, Pallas kernels for 0%

commit v1 on v0

v1 whole, which is shorter than its diff:
```python
import functools
import math

import jax
import jax.numpy as jnp
from jax import lax
from jax.experimental import pallas as pl
from jax.experimental.pallas import tpu as pltpu
from jax.sharding import PartitionSpec as P

HEADS = 12
BF16 = jnp.bfloat16
F32 = jnp.float32
VMEM_LIMIT = 40 * 1024 * 1024


def layer_norm(field):
    average = jnp.mean(field, axis=-1, keepdims=True)
    centred = field - average
    variance = jnp.mean(centred * centred, axis=-1, keepdims=True)
    return centred * lax.rsqrt(variance + 1e-06)


def step_to(owner, position, groups):
    if groups & (groups - 1) == 0:
        return owner ^ position
    return lax.rem(owner - position + groups, groups)


def source_of(step, position, groups):
    if groups & (groups - 1) == 0:
        return step ^ position
    return lax.rem(position - step + groups, groups)


def embed_kernel(groups, per_owner, patches, pairs_ref, enc_ref, w_ref, emb_ref, normed_ref, *rest):
    sends, (slots,) = rest[:-1], rest[-1:]
    img_dev = enc_ref.shape[0] // patches
    position = pairs_ref[0, 0] // img_dev

    @pl.loop(0, groups * per_owner)
    def _(slot):
        slots[slot] = 0

    @pl.loop(0, groups)
    def _(owner):
        slots[groups * per_owner + owner] = 0

    @pl.loop(0, pairs_ref.shape[0])
    def _(row):
        partner = pairs_ref[row, 1]

        @pl.when(partner >= 0)
        def _():
            owner = partner // img_dev
            rank = slots[groups * per_owner + owner]
            slots[groups * per_owner + owner] = rank + 1
            step = step_to(owner, position, groups) if len(sends) > 1 else owner
            slots[step * per_owner + rank] = lax.rem(pairs_ref[row, 0], img_dev)

    embedded = jnp.dot(enc_ref[...], w_ref[...], preferred_element_type=F32).astype(BF16)
    emb_ref[...] = embedded
    normed_ref[...] = layer_norm(embedded.astype(F32)).astype(BF16)

    def image(slot):
        at = pl.multiple_of(slots[slot] * patches, patches)
        return normed_ref[pl.ds(at, patches), :]

    if len(sends) == 1:

        @pl.loop(0, groups * per_owner)
        def _(slot):
            sends[0][pl.ds(pl.multiple_of(slot * patches, patches), patches), :] = image(slot)

    else:
        for step, send in enumerate(sends, 1):
            for rank in range(per_owner):
                send[rank * patches : (rank + 1) * patches, :] = image(step * per_owner + rank)


def query_kernel(scale, normed_ref, w_ref, out_ref):
    rows = jnp.dot(normed_ref[...], w_ref[...], preferred_element_type=F32).astype(BF16)
    out_ref[...] = rows * jnp.asarray(scale, BF16)


def decode_kernel(
    steps, per_owner, patches, table_ref, query_ref, emb_ref, wk_ref, wv_ref, wo_ref, wh_ref, totals_ref, *rest,
):
    blocks, (out_ref, q_rows, e_rows) = rest[:-3], rest[-3:]
    span = per_owner * patches
    width = wk_ref.shape[0]
    pair = 2 * (width // HEADS)

    def partner(step, rank):
        return table_ref[step * per_owner + rank]

    for n, step in enumerate(steps):
        for rank in range(per_owner):
            at = pl.multiple_of(jnp.maximum(partner(step, rank), 0) * patches, patches)
            to = n * span + rank * patches
            q_rows[to : to + patches, :] = query_ref[pl.ds(at, patches), :]
            e_rows[to : to + patches, :] = emb_ref[pl.ds(at, patches), :]

    x = jnp.concatenate([b[...] for b in blocks], axis=0) if len(blocks) > 1 else blocks[0][...]
    keys = jnp.dot(x, wk_ref[...], preferred_element_type=F32).astype(BF16)
    values = jnp.dot(x, wv_ref[...], preferred_element_type=F32).astype(BF16)
    first = lax.broadcasted_iota(jnp.int32, (span, pair), 1) < pair // 2
    at_row = lax.rem(lax.broadcasted_iota(jnp.int32, (2 * span, span), 0), span) // patches
    at_col = lax.broadcasted_iota(jnp.int32, (2 * span, span), 1) // patches
    same = at_row == at_col
    zero = jnp.zeros((), BF16)
    attended = []
    for n in range(len(steps)):
        cut = slice(n * span, (n + 1) * span)
        parts = []
        for p in range(HEADS // 2):
            cols = slice(p * pair, (p + 1) * pair)
            q = q_rows[cut, cols]
            both = jnp.concatenate([jnp.where(first, q, zero), jnp.where(first, zero, q)], axis=0)
            scores = lax.dot_general(
                both, keys[cut, cols], (((1,), (1,)), ((), ())), preferred_element_type=F32
            )
            exponent = jnp.exp(jnp.where(same, scores, -jnp.inf))
            weights = (exponent / jnp.sum(exponent, axis=-1, keepdims=True)).astype(BF16)
            mixed = jnp.dot(weights, values[cut, cols], preferred_element_type=F32)
            parts.append(jnp.where(first, mixed[:span], mixed[span:]).astype(BF16))
        attended.append(jnp.concatenate(parts, axis=1))
    attended = jnp.concatenate(attended, axis=0) if len(attended) > 1 else attended[0]
    updated = e_rows[...].astype(F32) + jnp.dot(attended, wo_ref[...], preferred_element_type=F32)
    head_input = layer_norm(updated).astype(BF16)
    head_out = jnp.dot(head_input, wh_ref[...], preferred_element_type=F32)
    weight = 1.0 + jnp.exp(head_out[:, 3:4])
    column = lax.broadcasted_iota(jnp.int32, head_out.shape, 1)
    terms = jnp.where(column == 3, weight, weight * head_out)
    out_ref[...] = totals_ref[...]
    for n, step in enumerate(steps):
        for rank in range(per_owner):
            image = partner(step, rank)
            to = n * span + rank * patches

            @pl.when(image >= 0)
            def _():
                at = pl.ds(pl.multiple_of(image * patches, patches), patches)
                out_ref[at, :] = out_ref[at, :] + terms[to : to + patches, :]


def vmem():
    return pl.BlockSpec(memory_space=pltpu.VMEM)


def smem():
    return pl.BlockSpec(memory_space=pltpu.SMEM)


def cost(flops, moved):
    return pl.CostEstimate(flops=int(flops), bytes_accessed=int(moved), transcendentals=0)


def per_device(enc_tokens, pair_list, w_embed, w_query, w_key, w_value, w_out, w_head):
    groups = lax.axis_size("img")
    position = lax.axis_index("img")
    img_dev, patches, enc_width = enc_tokens.shape
    width = w_query.shape[0]
    channels = w_head.shape[1]
    pair_dev = pair_list.shape[0]
    per_owner = (pair_dev + groups - 2) // (groups - 1)
    span = per_owner * patches
    own_rows = img_dev * patches
    params = pltpu.CompilerParams(vmem_limit_bytes=VMEM_LIMIT)
    by_permute = groups <= 32

    partners = lax.all_gather(pair_list[:, 1], "img", axis=0)
    mine = (partners // img_dev == position) & (partners >= 0)
    before = jnp.cumsum(mine.astype(jnp.int32), axis=1) - 1
    ranks = jnp.arange(per_owner, dtype=jnp.int32)
    hit = mine[:, None, :] & (before[:, None, :] == ranks[None, :, None])
    table = jnp.sum(jnp.where(hit, (partners % img_dev + 1)[:, None, :], 0), axis=2) - 1
    if by_permute:
        table = table[source_of(jnp.arange(groups, dtype=jnp.int32), position, groups)]
    table = table.reshape(groups * per_owner)

    if by_permute:
        send_shapes = [jax.ShapeDtypeStruct((span, width), BF16)] * (groups - 1)
    else:
        send_shapes = [jax.ShapeDtypeStruct((groups * span, width), BF16)]
    embedded, normed, *sends = pl.pallas_call(
        functools.partial(embed_kernel, groups, per_owner, patches),
        out_shape=[jax.ShapeDtypeStruct((own_rows, width), BF16)] * 2 + send_shapes,
        in_specs=[smem(), vmem(), vmem()],
        out_specs=[vmem()] * (2 + len(send_shapes)),
        scratch_shapes=[pltpu.SMEM((groups * per_owner + groups,), jnp.int32)],
        compiler_params=params,
        cost_estimate=cost(2 * own_rows * enc_width * width, 6e6),
        name="embed",
    )(pair_list, enc_tokens.reshape(own_rows, enc_width), w_embed)

    queries = pl.pallas_call(
        functools.partial(query_kernel, 1.0 / math.sqrt(width // HEADS)),
        out_shape=jax.ShapeDtypeStruct((own_rows, width), BF16),
        in_specs=[vmem(), vmem()],
        out_specs=vmem(),
        compiler_params=params,
        cost_estimate=cost(2 * own_rows * width * width, 3e6),
        name="queries",
    )(normed, w_query)

    def decode(totals, table, steps, blocks):
        count = span * len(steps)
        return pl.pallas_call(
            functools.partial(decode_kernel, steps, per_owner, patches),
            out_shape=jax.ShapeDtypeStruct((own_rows, channels), F32),
            in_specs=[smem()] + [vmem()] * (7 + len(blocks)),
            out_specs=vmem(),
            scratch_shapes=[pltpu.VMEM((count, width), BF16)] * 2,
            compiler_params=params,
            cost_estimate=cost(6 * count * width * width, 6e6),
            name="decode",
        )(table, queries, embedded, w_key, w_value, w_out, w_head, totals, *blocks)

    totals = jnp.zeros((own_rows, channels), F32)
    if by_permute:
        pairs_of = lambda s: [(i, i ^ s if groups & (groups - 1) == 0 else (i + s) % groups) for i in range(groups)]
        half = groups // 2
        near = list(range(2, half)) + [1]
        far = list(range(half, groups))
        got = {}

        def chain(order, window):
            for n, s in enumerate(order):
                v = sends[s - 1]
                if n >= window:
                    back = order[n - window]
                    v, got[back] = lax.optimization_barrier((v, got[back]))
                got[s] = lax.ppermute(v, "img", pairs_of(s))

        chain(far, 3)
        chain(near, 2)
        order = []
        for k in range(half):
            order += far[k : k + 1] + near[k : k + 1]
        for k in range(0, len(order), 2):
            steps = tuple(order[k : k + 2])
            totals = decode(totals, table, steps, [got[s] for s in steps])
    else:
        got = lax.all_to_all(sends[0].reshape(groups, span, width), "img", 0, 0, tiled=True)
        some = math.gcd(groups, max(1, 128 // span))

        def body(k, totals):
            part = lax.dynamic_slice_in_dim(table, k * some * per_owner, some * per_owner)
            block = lax.dynamic_slice_in_dim(got, k * some, some).reshape(some * span, width)
            return decode(totals, part, tuple(range(some)), [block])

        totals = lax.fori_loop(0, groups // some, body, totals)
    totals = jnp.transpose(totals.reshape(img_dev, patches, channels), (0, 2, 1))
    confidence = totals[:, 3, :]
    divisor = 1.0 + confidence[:, None, :]
    return (totals[:, 0:3, :] / divisor, totals[:, 4:, :] / divisor, confidence)


def solution(mesh):
    rows = P(("scene", "img"))
    return jax.shard_map(
        per_device,
        mesh=mesh,
        in_specs=(rows, rows, P(), P(), P(), P(), P(), P()),
        out_specs=(rows, rows, rows),
        check_vma=False,
    )
```

time: 158 us -> 96.5 us (0.61)
  blocking collectives: 48.3 us -> 9.88 us
  Pallas kernels: 0 us -> 26 us
  matrix products: 19.1 us -> 0 us
  waiting for transfers between devices: 15 us -> 0.04 us
  other arithmetic: 12.9 us -> 2.36 us
  local copies, waits for them, and re-layouts: 38.3 us -> 30.2 us
  starting transfers between devices: 22.9 us -> 25.7 us
    all_to_all x1 -> x0, blocking collectives: 48.3 us -> none  [per_device(): lax.all_to_all(send_queries, 'img', split_axis=0, concat_axis=0, tiled=True)]
    pallas_call x0 -> x10, Pallas kernels: none -> 26 us  [the longest x8 20.2 us: decode(): pl.pallas_call(functools.partial(decode_kernel, steps, per_owner, patches...]
    ppermute x0 -> x15, starting transfers between devices: none -> 25.7 us  [chain(): got[s] = lax.ppermute(v, 'img', pairs_of(s))]
    unnamed x31 -> x83, local copies, waits for them, and re-layouts: 2.94 us -> 27 us
    all_to_all x3 -> x0, starting transfers between devices: 22.9 us -> none  [the longest x1 10.8 us: per_device(): lax.all_to_all(slot_terms.reshape(groups, per_owner, channels * patches),...]
    dot_general x10 -> x0, matrix products: 19.1 us -> none  [the longest x1 6.22 us: decode_terms(): jnp.einsum('bqhd,bkhd->bhqk', query_heads, key_heads, preferred_element_t...]
    all_to_all x3 -> x0, waiting for transfers between devices: 15 us -> none  [the longest x1 8.77 us: per_device(): lax.all_to_all(slot_terms.reshape(groups, per_owner, channels * patches),...]
    reshape x5 -> x2, local copies, waits for them, and re-layouts: 16.9 us -> 1.93 us  [the longest x1 1.15 us: per_device(): totals.reshape(img_dev, patches, channels)]
  transfers between devices with their start and end apart: 3 -> 15, of which waited for: 3 -> 0; matrix products, arithmetic and copies ran while one was open for 25% -> 5% of each run, Pallas kernels for 0% -> 20%
where the time goes in v1:
time: 96.5 us; the launch traced here: 95.8 us
  local copies, waits for them, and re-layouts  30.2 us (31%)
  Pallas kernels  26 us (27%)
  starting transfers between devices  25.7 us (27%)
  blocking collectives  9.88 us (10%)
  other arithmetic  2.36 us (2%)
  between operations  1.65 us (2%)
    unnamed x83, local copies, waits for them, and re-layouts  27 us
    ppermute x15, starting transfers between devices, chain(): got[s] = lax.ppermute(v, 'img', pairs_of(s))  25.7 us
    pallas_call x8, Pallas kernels, decode(): pl.pallas_call(functools.partial(decode_kernel, steps, per_owner, patches...  20.2 us
    unnamed x1, blocking collectives  9.88 us
    pallas_call x1, Pallas kernels, per_device(): pl.pallas_call(functools.partial(embed_kernel, groups, per_owner, patches...  5.03 us
  transfers between devices with their start and end apart: 15, of which 0 were waited for; matrix products, arithmetic and copies ran while one was open for 5% of the time, Pallas kernels for 20%

profile of v1, /device:TPU:0, one launch (start us, length us, event | category | flops | bytes accessed | tf_op | source)
XLA Modules:
  0.0 95.8 jit_solution(8204261195731850193)
XLA Ops:
  0.6 1.4 %copy.43.pairs_ref = s32[64,2]{1,0:T(8,128)} copy(s32[64,2]{0,1:T(2,128)} %param.9) | data formatting | bytes 1024 | tf_op args[1]
  2.0 0.8 copy-done.20
  2.8 1.4 %copy-done.21 = bf16[1024,768]{1,0:T(8,128)(2,1)S(1)} copy-done((bf16[1024,768]{1,0:T(8,128)(2,1)S(1)}, bf16[1024,768]{1,0:T(8,128)(2,1)}, u32[]{:S(2)}) %copy-start.21) | copy-done | bytes 1572888
  4.2 1.2 %copy-done.22 = bf16[32,16,1024]{2,1,0:T(8,128)(2,1)S(1)} copy-done((bf16[32,16,1024]{2,1,0:T(8,128)(2,1)S(1)}, bf16[32,16,1024]{2,1,0:T(8,128)(2,1)}, u32[]{:S(2)}) %copy-start.22) | copy-done | bytes 1048600
  5.4 5.0 %embed.1 = (bf16[512,768]{1,0:T(8,128)(2,1)S(1)}, bf16[512,768]{1,0:T(8,128)(2,1)S(1)}, bf16[80,768]{1,0:T(8,128)(2,1)S(1)}, bf16[80,768]{1,0:T(8,128)(2,1)}, bf...) custom-call(s32[64,2]{1,0:T(8,128)S(1)} %copy-done.20, ...), custom_call_target="tpu_custom_call" | custom-call | flops 805306368 | bytes 6000000 | tf_op jit(solution)/shard_map/embed/pallas_call | solution.py:186
  10.4 0.9 copy-done.5
  11.3 0.9 copy-done.10
  12.9 0.7 copy-done.25
  13.5 0.6 copy-done.27
  14.2 0.6 copy-done.29
  14.8 0.6 copy-done.31
  18.1 0.6 copy-done.36
  18.7 4.0 %collective-permute-start = (bf16[80,768]{1,0:T(8,128)(2,1)}, bf16[80,768]{1,0:T(8,128)(2,1)S(1)}, u32[]{:S(2)}, u32[]{:S(2)}) collective-permute-start(bf16[80,768]{1,0:T(8,128)(2,1)} %get-tuple-element.43), channel_id=1, source_target_pairs={{0,8},{1,9},{2,10},{3,11},{4,12},{5,13},{6,14},{7,15},{8,0},{9,1},... | collective-permute-start | bytes 368648 | tf_op jit(solution)/shard_map/ppermute | solution.py:234
  22.8 1.5 %collective-permute-start.1 = (bf16[80,768]{1,0:T(8,128)(2,1)}, bf16[80,768]{1,0:T(8,128)(2,1)S(1)}, u32[]{:S(2)}, u32[]{:S(2)}) collective-permute-start(bf16[80,768]{1,0:T(8,128)(2,1)} %get-tuple-element.46), channel_id=1, source_target_pairs={{0,2},{1,3},{2,0},{3,1},{4,6},{5,7},{6,4},{7,5},{8,10},{9,11},{10,... | collective-permute-start | bytes 368648 | tf_op jit(solution)/shard_map/ppermute | solution.py:234
  24.5 3.9 %collective-permute-start.4 = (bf16[80,768]{1,0:T(8,128)(2,1)}, bf16[80,768]{1,0:T(8,128)(2,1)}, u32[]{:S(2)}, u32[]{:S(2)}) collective-permute-start(bf16[80,768]{1,0:T(8,128)(2,1)} %get-tuple-element.55), channel_id=1, source_target_pairs={{0,10},{1,11},{2,8},{3,9},{4,14},{5,15},{6,12},{7,13},{8,2},{9,3},... | collective-permute-start | bytes 368648 | tf_op jit(solution)/shard_map/ppermute | solution.py:234
  29.8 9.9 %all-reduce = s32[1024]{0:T(1024)S(1)} all-reduce(s32[1024]{0:T(1024)S(1)} %bitcast_dynamic-update-slice_fusion), channel_id=2, replica_groups=mesh['scene'=2,'img'=16] {'img'}, use_global_device_ids=true, to_apply=%add | all-reduce | flops 1024 | bytes 8192
  40.8 0.8 collective-permute-start.5
  42.2 0.7 copy-done.16
  42.9 0.7 copy-done.18
  43.6 3.8 %collective-permute-start.6 = (bf16[80,768]{1,0:T(8,128)(2,1)}, bf16[80,768]{1,0:T(8,128)(2,1)}, u32[]{:S(2)}, u32[]{:S(2)}) collective-permute-start(bf16[80,768]{1,0:T(8,128)(2,1)} %copy-done.35), channel_id=1, source_target_pairs={{0,11},{1,10},{2,9},{3,8},{4,15},{5,14},{6,13},{7,12},{8,3},{9,2},... | collective-permute-start | bytes 368648 | tf_op jit(solution)/shard_map/ppermute | solution.py:234
  47.7 1.0 %collective-permute-start.8 = (bf16[80,768]{1,0:T(8,128)(2,1)}, bf16[80,768]{1,0:T(8,128)(2,1)}, u32[]{:S(2)}, u32[]{:S(2)}) collective-permute-start(bf16[80,768]{1,0:T(8,128)(2,1)} %copy-done.33), channel_id=1, source_target_pairs={{0,12},{1,13},{2,14},{3,15},{4,8},{5,9},{6,10},{7,11},{8,4},{9,5},... | collective-permute-start | bytes 368648 | tf_op jit(solution)/shard_map/ppermute | solution.py:234
  48.6 1.3 %copy-done.8 = bf16[768,768]{1,0:T(8,128)(2,1)S(1)} copy-done((bf16[768,768]{1,0:T(8,128)(2,1)S(1)}, bf16[768,768]{1,0:T(8,128)(2,1)}, u32[]{:S(2)}) %copy-start.8) | copy-done | bytes 1179672
  49.9 1.1 %copy-done.11 = bf16[512,768]{1,0:T(8,128)(2,1)S(1)} copy-done((bf16[512,768]{1,0:T(8,128)(2,1)S(1)}, bf16[512,768]{1,0:T(8,128)(2,1)}, u32[]{:S(2)}) %copy-start.11) | copy-done | bytes 786456
  51.1 0.8 queries.1.query_ref
  51.9 0.9 copy-done.3
  52.8 1.1 %gather_fusion = s32[16,5]{1,0:T(8,128)} fusion(s32[16,5]{1,0:T(8,128)S(1)} %copy.42, s32[1024]{0:T(1024)S(1)} %pad_clamp_fusion), kind=kCustom, calls=%fused_computation | custom fusion | bytes 704 | tf_op jit(solution)/shard_map/gather | solution.py:179
  54.0 0.8 reshape.40.table_ref
  54.8 1.6 %copy.51.wh_ref = bf16[768,28]{1,0:T(8,128)(2,1)} copy(bf16[768,28]{0,1:T(8,128)(2,1)} %param.15) | data formatting | bytes 86016 | tf_op args[7]
  56.4 2.5 %collective-permute-start.10 = (bf16[80,768]{1,0:T(8,128)(2,1)}, bf16[80,768]{1,0:T(8,128)(2,1)S(1)}, u32[]{:S(2)}, u32[]{:S(2)}) collective-permute-start(bf16[80,768]{1,0:T(8,128)(2,1)} %copy-done.31), channel_id=1, source_target_pairs={{0,13},{1,12},{2,15},{3,14},{4,9},{5,8},{6,11},{7,10},{8,5},{9,4},... | collective-permute-start | bytes 368648 | tf_op jit(solution)/shard_map/ppermute | solution.py:234
  59.0 1.1 %copy-done.4 = bf16[512,768]{1,0:T(8,128)(2,1)S(1)} copy-done((bf16[512,768]{1,0:T(8,128)(2,1)S(1)}, bf16[512,768]{1,0:T(8,128)(2,1)}, u32[]{:S(2)}) %copy-start.4) | copy-done | bytes 786456
  60.1 1.1 %copy-done.6 = bf16[512,768]{1,0:T(8,128)(2,1)S(1)} copy-done((bf16[512,768]{1,0:T(8,128)(2,1)S(1)}, bf16[512,768]{1,0:T(8,128)(2,1)}, u32[]{:S(2)}) %copy-start.6) | copy-done | bytes 786456
  61.2 0.9 copy-done.7
  62.1 0.9 copy-done.13
  63.0 0.9 copy-done.15
  64.0 2.4 %decode.8.totals_ref = f32[512,28]{1,0:T(8,128)S(1)} custom-call(s32[80]{0:T(128)S(1)} %reshape.40.table_ref, bf16[512,768]{1,0:T(8,128)(2,1)S(1)} %copy-done.4, bf16[512,768]{1,0:T(8,128)(2,1)S(1)} %copy-done.6, bf16[768,768]{1,0:T(8,128)(2,1)S(1)} %copy-done, bf16[768,768]{1,0:T(8,128)(2,1)S(1)} %copy-done.1, bf16[768,768]{1,0:T(8,128)(2,1)S(1)} %copy-done.2, ...), custom_call_target="tpu_custom_call" | custom-call | flops 566231040 | bytes 6000000 | tf_op jit(solution)/shard_map/decode/pallas_call | solution.py:209
  66.4 2.4 %decode.9.totals_ref = f32[512,28]{1,0:T(8,128)S(1)} custom-call(s32[80]{0:T(128)S(1)} %reshape.40.table_ref, bf16[512,768]{1,0:T(8,128)(2,1)S(1)} %copy-done.4, bf16[512,768]{1,0:T(8,128)(2,1)S(1)} %copy-done.6, bf16[768,768]{1,0:T(8,128)(2,1)S(1)} %copy-done, bf16[768,768]{1,0:T(8,128)(2,1)S(1)} %copy-done.1, bf16[768,768]{1,0:T(8,128)(2,1)S(1)} %copy-done.2, ...), custom_call_target="tpu_custom_call" | custom-call | flops 566231040 | bytes 6000000 | tf_op jit(solution)/shard_map/decode/pallas_call | solution.py:209
  68.8 2.8 %collective-permute-start.11 = (bf16[80,768]{1,0:T(8,128)(2,1)S(1)}, bf16[80,768]{1,0:T(8,128)(2,1)S(1)}, u32[]{:S(2)}, u32[]{:S(2)}) collective-permute-start(bf16[80,768]{1,0:T(8,128)(2,1)S(1)} %copy-done.30), channel_id=1, source_target_pairs={{0,7},{1,6},{2,5},{3,4},{4,3},{5,2},{6,1},{7,0},{8,15},{9,14},{10,... | collective-permute-start | bytes 368648 | tf_op jit(solution)/shard_map/ppermute | solution.py:234
  71.6 1.2 %collective-permute-start.12 = (bf16[80,768]{1,0:T(8,128)(2,1)S(1)}, bf16[80,768]{1,0:T(8,128)(2,1)S(1)}, u32[]{:S(2)}, u32[]{:S(2)}) collective-permute-start(bf16[80,768]{1,0:T(8,128)(2,1)S(1)} %copy-done.28), channel_id=1, source_target_pairs={{0,14},{1,15},{2,12},{3,13},{4,10},{5,11},{6,8},{7,9},{8,6},{9,7},... | collective-permute-start | bytes 368648 | tf_op jit(solution)/shard_map/ppermute | solution.py:234
  72.8 3.2 %collective-permute-start.14 = (bf16[80,768]{1,0:T(8,128)(2,1)S(1)}, bf16[80,768]{1,0:T(8,128)(2,1)S(1)}, u32[]{:S(2)}, u32[]{:S(2)}) collective-permute-start(bf16[80,768]{1,0:T(8,128)(2,1)S(1)} %copy-done.24), channel_id=1, source_target_pairs={{0,15},{1,14},{2,13},{3,12},{4,11},{5,10},{6,9},{7,8},{8,7},{9,6},... | collective-permute-start | bytes 368648 | tf_op jit(solution)/shard_map/ppermute | solution.py:234
  76.0 2.8 %decode.10.totals_ref = f32[512,28]{1,0:T(8,128)S(1)} custom-call(s32[80]{0:T(128)S(1)} %reshape.40.table_ref, bf16[512,768]{1,0:T(8,128)(2,1)S(1)} %copy-done.4, bf16[512,768]{1,0:T(8,128)(2,1)S(1)} %copy-done.6, bf16[768,768]{1,0:T(8,128)(2,1)S(1)} %copy-done, bf16[768,768]{1,0:T(8,128)(2,1)S(1)} %copy-done.1, bf16[768,768]{1,0:T(8,128)(2,1)S(1)} %copy-done.2, ...), custom_call_target="tpu_custom_call" | custom-call | flops 566231040 | bytes 6000000 | tf_op jit(solution)/shard_map/decode/pallas_call | solution.py:209
  79.3 2.8 %decode.11.totals_ref = f32[512,28]{1,0:T(8,128)S(1)} custom-call(s32[80]{0:T(128)S(1)} %reshape.40.table_ref, bf16[512,768]{1,0:T(8,128)(2,1)S(1)} %copy-done.4, bf16[512,768]{1,0:T(8,128)(2,1)S(1)} %copy-done.6, bf16[768,768]{1,0:T(8,128)(2,1)S(1)} %copy-done, bf16[768,768]{1,0:T(8,128)(2,1)S(1)} %copy-done.1, bf16[768,768]{1,0:T(8,128)(2,1)S(1)} %copy-done.2, ...), custom_call_target="tpu_custom_call" | custom-call | flops 566231040 | bytes 6000000 | tf_op jit(solution)/shard_map/decode/pallas_call | solution.py:209
  82.1 2.9 %decode.12.totals_ref = f32[512,28]{1,0:T(8,128)S(1)} custom-call(s32[80]{0:T(128)S(1)} %reshape.40.table_ref, bf16[512,768]{1,0:T(8,128)(2,1)S(1)} %copy-done.4, bf16[512,768]{1,0:T(8,128)(2,1)S(1)} %copy-done.6, bf16[768,768]{1,0:T(8,128)(2,1)S(1)} %copy-done, bf16[768,768]{1,0:T(8,128)(2,1)S(1)} %copy-done.1, bf16[768,768]{1,0:T(8,128)(2,1)S(1)} %copy-done.2, ...), custom_call_target="tpu_custom_call" | custom-call | flops 566231040 | bytes 6000000 | tf_op jit(solution)/shard_map/decode/pallas_call | solution.py:209
  85.1 2.4 %decode.13.totals_ref = f32[512,28]{1,0:T(8,128)S(1)} custom-call(s32[80]{0:T(128)S(1)} %reshape.40.table_ref, bf16[512,768]{1,0:T(8,128)(2,1)S(1)} %copy-done.4, bf16[512,768]{1,0:T(8,128)(2,1)S(1)} %copy-done.6, bf16[768,768]{1,0:T(8,128)(2,1)S(1)} %copy-done, bf16[768,768]{1,0:T(8,128)(2,1)S(1)} %copy-done.1, bf16[768,768]{1,0:T(8,128)(2,1)S(1)} %copy-done.2, ...), custom_call_target="tpu_custom_call" | custom-call | flops 566231040 | bytes 6000000 | tf_op jit(solution)/shard_map/decode/pallas_call | solution.py:209
  87.5 2.4 %decode.14.totals_ref = f32[512,28]{1,0:T(8,128)S(1)} custom-call(s32[80]{0:T(128)S(1)} %reshape.40.table_ref, bf16[512,768]{1,0:T(8,128)(2,1)S(1)} %copy-done.4, bf16[512,768]{1,0:T(8,128)(2,1)S(1)} %copy-done.6, bf16[768,768]{1,0:T(8,128)(2,1)S(1)} %copy-done, bf16[768,768]{1,0:T(8,128)(2,1)S(1)} %copy-done.1, bf16[768,768]{1,0:T(8,128)(2,1)S(1)} %copy-done.2, ...), custom_call_target="tpu_custom_call" | custom-call | flops 566231040 | bytes 6000000 | tf_op jit(solution)/shard_map/decode/pallas_call | solution.py:209
  89.9 2.1 %decode.15 = f32[512,28]{1,0:T(8,128)S(1)} custom-call(s32[80]{0:T(128)S(1)} %reshape.40.table_ref, bf16[512,768]{1,0:T(8,128)(2,1)S(1)} %copy-done.4, bf16[512,768]{1,0:T(8,128)(2,1)S(1)} %copy-done.6, bf16[768,768]{1,0:T(8,128)(2,1)S(1)} %copy-done, bf16[768,768]{1,0:T(8,128)(2,1)S(1)} %copy-done.1, bf16[768,768]{1,0:T(8,128)(2,1)S(1)} %copy-done.2, ...), custom_call_target="tpu_custom_call" | custom-call | flops 283115520 | bytes 6000000 | tf_op jit(solution)/shard_map/decode/pallas_call | solution.py:209
  92.1 0.7 copy-done.9
  92.8 1.1 %copy.52 = f32[32,16,28]{0,1,2:T(8,128)S(1)} copy(f32[32,16,28]{2,1,0:T(8,128)} %bitcast.12) | data formatting | bytes 114688 | tf_op jit(solution)/shard_map/reshape | solution.py:254
  95.1 0.7 slice_divide_fusion
  (92 shorter events, 8.2 us)
Async XLA Ops:
  2.0 0.8 copy-start.20
  2.8 1.4 %copy-start.21 = (bf16[1024,768]{1,0:T(8,128)(2,1)S(1)}, bf16[1024,768]{1,0:T(8,128)(2,1)}, u32[]{:S(2)}) copy-start(bf16[1024,768]{1,0:T(8,128)(2,1)} %w_ref.2) | copy-start | bytes 4718596
  4.2 1.2 %copy-start.22 = (bf16[32,16,1024]{2,1,0:T(8,128)(2,1)S(1)}, bf16[32,16,1024]{2,1,0:T(8,128)(2,1)}, u32[]{:S(2)}) copy-start(bf16[32,16,1024]{2,1,0:T(8,128)(2,1)} %param.8) | copy-start | bytes 3145732
  5.4 23.0 %copy-start.38 = (u32[32]{0:T(128)S(1)}, u32[32]{0:T(128)}, u32[]{:S(2)}) copy-start(u32[32]{0:T(128)} %constant.50) | copy-start | bytes 388
  5.4 24.2 %copy-start.37 = (s32[64,2]{0,1:T(2,128)S(1)}, s32[64,2]{0,1:T(2,128)}, u32[]{:S(2)}) copy-start(s32[64,2]{0,1:T(2,128)} %param.9) | copy-start | bytes 1540
  5.4 53.5 %copy-start.2 = (bf16[768,768]{1,0:T(8,128)(2,1)S(1)}, bf16[768,768]{1,0:T(8,128)(2,1)}, u32[]{:S(2)}) copy-start(bf16[768,768]{1,0:T(8,128)(2,1)} %wo_ref.15) | copy-start | bytes 3538948
  10.4 0.9 copy-start.5
  11.3 0.9 copy-start.10
  12.9 0.7 copy-start.25
  13.5 0.7 copy-start.27
  14.2 0.7 copy-start.29
  14.8 0.6 copy-start.31
  18.1 0.6 copy-start.36
  18.7 22.9 %collective-permute-start = (bf16[80,768]{1,0:T(8,128)(2,1)}, bf16[80,768]{1,0:T(8,128)(2,1)S(1)}, u32[]{:S(2)}, u32[]{:S(2)}) collective-permute-start(bf16[80,768]{1,0:T(8,128)(2,1)} %get-tuple-element.43), channel_id=1, source_target_pairs={{0,8},{1,9},{2,10},{3,11},{4,12},{5,13},{6,14},{7,15},{8,0},{9,1},... | collective-permute-start | bytes 368648 | tf_op jit(solution)/shard_map/ppermute | solution.py:234
  22.8 17.4 %collective-permute-start.1 = (bf16[80,768]{1,0:T(8,128)(2,1)}, bf16[80,768]{1,0:T(8,128)(2,1)S(1)}, u32[]{:S(2)}, u32[]{:S(2)}) collective-permute-start(bf16[80,768]{1,0:T(8,128)(2,1)} %get-tuple-element.46), channel_id=1, source_target_pairs={{0,2},{1,3},{2,0},{3,1},{4,6},{5,7},{6,4},{7,5},{8,10},{9,11},{10,... | collective-permute-start | bytes 368648 | tf_op jit(solution)/shard_map/ppermute | solution.py:234
  24.3 18.0 %collective-permute-start.2 = (bf16[80,768]{1,0:T(8,128)(2,1)}, bf16[80,768]{1,0:T(8,128)(2,1)S(1)}, u32[]{:S(2)}, u32[]{:S(2)}) collective-permute-start(bf16[80,768]{1,0:T(8,128)(2,1)} %get-tuple-element.49), channel_id=1, source_target_pairs={{0,9},{1,8},{2,11},{3,10},{4,13},{5,12},{6,15},{7,14},{8,1},{9,0},... | collective-permute-start | bytes 368648 | tf_op jit(solution)/shard_map/ppermute | solution.py:234
  24.3 18.6 %collective-permute-start.3 = (bf16[80,768]{1,0:T(8,128)(2,1)}, bf16[80,768]{1,0:T(8,128)(2,1)S(1)}, u32[]{:S(2)}, u32[]{:S(2)}) collective-permute-start(bf16[80,768]{1,0:T(8,128)(2,1)} %get-tuple-element.52), channel_id=1, source_target_pairs={{0,3},{1,2},{2,1},{3,0},{4,7},{5,6},{6,5},{7,4},{8,11},{9,10},{10,... | collective-permute-start | bytes 368648 | tf_op jit(solution)/shard_map/ppermute | solution.py:234
  24.5 31.9 %collective-permute-start.4 = (bf16[80,768]{1,0:T(8,128)(2,1)}, bf16[80,768]{1,0:T(8,128)(2,1)}, u32[]{:S(2)}, u32[]{:S(2)}) collective-permute-start(bf16[80,768]{1,0:T(8,128)(2,1)} %get-tuple-element.55), channel_id=1, source_target_pairs={{0,10},{1,11},{2,8},{3,9},{4,14},{5,15},{6,12},{7,13},{8,2},{9,3},... | collective-permute-start | bytes 368648 | tf_op jit(solution)/shard_map/ppermute | solution.py:234
  40.8 18.1 %collective-permute-start.5 = (bf16[80,768]{1,0:T(8,128)(2,1)}, bf16[80,768]{1,0:T(8,128)(2,1)}, u32[]{:S(2)}, u32[]{:S(2)}) collective-permute-start(bf16[80,768]{1,0:T(8,128)(2,1)} %copy-done.36), channel_id=1, source_target_pairs={{0,4},{1,5},{2,6},{3,7},{4,0},{5,1},{6,2},{7,3},{8,12},{9,13},{10,... | collective-permute-start | bytes 368648 | tf_op jit(solution)/shard_map/ppermute | solution.py:234
  41.6 0.6 copy-start.12
  42.2 0.7 copy-start.16
  42.9 0.7 copy-start.18
  43.6 25.2 %collective-permute-start.6 = (bf16[80,768]{1,0:T(8,128)(2,1)}, bf16[80,768]{1,0:T(8,128)(2,1)}, u32[]{:S(2)}, u32[]{:S(2)}) collective-permute-start(bf16[80,768]{1,0:T(8,128)(2,1)} %copy-done.35), channel_id=1, source_target_pairs={{0,11},{1,10},{2,9},{3,8},{4,15},{5,14},{6,13},{7,12},{8,3},{9,2},... | collective-permute-start | bytes 368648 | tf_op jit(solution)/shard_map/ppermute | solution.py:234
  47.3 21.5 %collective-permute-start.7 = (bf16[80,768]{1,0:T(8,128)(2,1)}, bf16[80,768]{1,0:T(8,128)(2,1)}, u32[]{:S(2)}, u32[]{:S(2)}) collective-permute-start(bf16[80,768]{1,0:T(8,128)(2,1)} %copy-done.34), channel_id=1, source_target_pairs={{0,5},{1,4},{2,7},{3,6},{4,1},{5,0},{6,3},{7,2},{8,13},{9,12},{10,... | collective-permute-start | bytes 368648 | tf_op jit(solution)/shard_map/ppermute | solution.py:234
  47.7 21.2 %collective-permute-start.8 = (bf16[80,768]{1,0:T(8,128)(2,1)}, bf16[80,768]{1,0:T(8,128)(2,1)}, u32[]{:S(2)}, u32[]{:S(2)}) collective-permute-start(bf16[80,768]{1,0:T(8,128)(2,1)} %copy-done.33), channel_id=1, source_target_pairs={{0,12},{1,13},{2,14},{3,15},{4,8},{5,9},{6,10},{7,11},{8,4},{9,5},... | collective-permute-start | bytes 368648 | tf_op jit(solution)/shard_map/ppermute | solution.py:234
  48.6 1.3 %copy-start.8 = (bf16[768,768]{1,0:T(8,128)(2,1)S(1)}, bf16[768,768]{1,0:T(8,128)(2,1)}, u32[]{:S(2)}) copy-start(bf16[768,768]{1,0:T(8,128)(2,1)} %w_ref.3) | copy-start | bytes 3538948
  49.9 1.1 %copy-start.11 = (bf16[512,768]{1,0:T(8,128)(2,1)S(1)}, bf16[512,768]{1,0:T(8,128)(2,1)}, u32[]{:S(2)}) copy-start(bf16[512,768]{1,0:T(8,128)(2,1)} %copy-done.10) | copy-start | bytes 2359300
  51.1 7.9 %copy-start = (bf16[768,768]{1,0:T(8,128)(2,1)S(1)}, bf16[768,768]{1,0:T(8,128)(2,1)}, u32[]{:S(2)}) copy-start(bf16[768,768]{1,0:T(8,128)(2,1)} %wk_ref.15) | copy-start | bytes 3538948
  51.1 7.9 %copy-start.1 = (bf16[768,768]{1,0:T(8,128)(2,1)S(1)}, bf16[768,768]{1,0:T(8,128)(2,1)}, u32[]{:S(2)}) copy-start(bf16[768,768]{1,0:T(8,128)(2,1)} %wv_ref.15) | copy-start | bytes 3538948
  51.8 0.9 copy-start.3
  56.4 28.7 %collective-permute-start.10 = (bf16[80,768]{1,0:T(8,128)(2,1)}, bf16[80,768]{1,0:T(8,128)(2,1)S(1)}, u32[]{:S(2)}, u32[]{:S(2)}) collective-permute-start(bf16[80,768]{1,0:T(8,128)(2,1)} %copy-done.31), channel_id=1, source_target_pairs={{0,13},{1,12},{2,15},{3,14},{4,9},{5,8},{6,11},{7,10},{8,5},{9,4},... | collective-permute-start | bytes 368648 | tf_op jit(solution)/shard_map/ppermute | solution.py:234
  58.9 19.9 %collective-permute-start.9 = (bf16[80,768]{1,0:T(8,128)(2,1)}, bf16[80,768]{1,0:T(8,128)(2,1)S(1)}, u32[]{:S(2)}, u32[]{:S(2)}) collective-permute-start(bf16[80,768]{1,0:T(8,128)(2,1)} %copy-done.32), channel_id=1, source_target_pairs={{0,6},{1,7},{2,4},{3,5},{4,2},{5,3},{6,0},{7,1},{8,14},{9,15},{10,... | collective-permute-start | bytes 368648 | tf_op jit(solution)/shard_map/ppermute | solution.py:234
  58.9 1.1 %copy-start.4 = (bf16[512,768]{1,0:T(8,128)(2,1)S(1)}, bf16[512,768]{1,0:T(8,128)(2,1)}, u32[]{:S(2)}) copy-start(bf16[512,768]{1,0:T(8,128)(2,1)} %copy-done.3) | copy-start | bytes 2359300
  60.1 1.1 %copy-start.6 = (bf16[512,768]{1,0:T(8,128)(2,1)S(1)}, bf16[512,768]{1,0:T(8,128)(2,1)}, u32[]{:S(2)}) copy-start(bf16[512,768]{1,0:T(8,128)(2,1)} %copy-done.5) | copy-start | bytes 2359300
  61.2 0.9 copy-start.7
  62.1 0.9 copy-start.13
  63.0 0.9 copy-start.15
  63.9 2.4 %copy-start.17 = (bf16[80,768]{1,0:T(8,128)(2,1)S(1)}, bf16[80,768]{1,0:T(8,128)(2,1)}, u32[]{:S(2)}) copy-start(bf16[80,768]{1,0:T(8,128)(2,1)} %copy-done.16) | copy-start | bytes 368644
  63.9 2.4 %copy-start.19 = (bf16[80,768]{1,0:T(8,128)(2,1)S(1)}, bf16[80,768]{1,0:T(8,128)(2,1)}, u32[]{:S(2)}) copy-start(bf16[80,768]{1,0:T(8,128)(2,1)} %copy-done.18) | copy-start | bytes 368644
  66.4 2.5 %copy-start.30 = (bf16[80,768]{1,0:T(8,128)(2,1)S(1)}, bf16[80,768]{1,0:T(8,128)(2,1)}, u32[]{:S(2)}) copy-start(bf16[80,768]{1,0:T(8,128)(2,1)} %copy-done.29) | copy-start | bytes 368644
  66.4 5.2 %copy-start.28 = (bf16[80,768]{1,0:T(8,128)(2,1)S(1)}, bf16[80,768]{1,0:T(8,128)(2,1)}, u32[]{:S(2)}) copy-start(bf16[80,768]{1,0:T(8,128)(2,1)} %copy-done.27) | copy-start | bytes 368644
  66.4 6.4 %copy-start.24 = (bf16[80,768]{1,0:T(8,128)(2,1)S(1)}, bf16[80,768]{1,0:T(8,128)(2,1)}, u32[]{:S(2)}) copy-start(bf16[80,768]{1,0:T(8,128)(2,1)} %copy-done.23) | copy-start | bytes 368644
  68.8 10.0 %copy-start.26 = (bf16[80,768]{1,0:T(8,128)(2,1)S(1)}, bf16[80,768]{1,0:T(8,128)(2,1)}, u32[]{:S(2)}) copy-start(bf16[80,768]{1,0:T(8,128)(2,1)} %copy-done.25) | copy-start | bytes 368644
  68.8 16.3 %collective-permute-start.11 = (bf16[80,768]{1,0:T(8,128)(2,1)S(1)}, bf16[80,768]{1,0:T(8,128)(2,1)S(1)}, u32[]{:S(2)}, u32[]{:S(2)}) collective-permute-start(bf16[80,768]{1,0:T(8,128)(2,1)S(1)} %copy-done.30), channel_id=1, source_target_pairs={{0,7},{1,6},{2,5},{3,4},{4,3},{5,2},{6,1},{7,0},{8,15},{9,14},{10,... | collective-permute-start | bytes 368648 | tf_op jit(solution)/shard_map/ppermute | solution.py:234
  71.6 15.9 %collective-permute-start.12 = (bf16[80,768]{1,0:T(8,128)(2,1)S(1)}, bf16[80,768]{1,0:T(8,128)(2,1)S(1)}, u32[]{:S(2)}, u32[]{:S(2)}) collective-permute-start(bf16[80,768]{1,0:T(8,128)(2,1)S(1)} %copy-done.28), channel_id=1, source_target_pairs={{0,14},{1,15},{2,12},{3,13},{4,10},{5,11},{6,8},{7,9},{8,6},{9,7},... | collective-permute-start | bytes 368648 | tf_op jit(solution)/shard_map/ppermute | solution.py:234
  72.8 17.1 %collective-permute-start.14 = (bf16[80,768]{1,0:T(8,128)(2,1)S(1)}, bf16[80,768]{1,0:T(8,128)(2,1)S(1)}, u32[]{:S(2)}, u32[]{:S(2)}) collective-permute-start(bf16[80,768]{1,0:T(8,128)(2,1)S(1)} %copy-done.24), channel_id=1, source_target_pairs={{0,15},{1,14},{2,13},{3,12},{4,11},{5,10},{6,9},{7,8},{8,7},{9,6},... | collective-permute-start | bytes 368648 | tf_op jit(solution)/shard_map/ppermute | solution.py:234
  78.8 8.7 %collective-permute-start.13 = (bf16[80,768]{1,0:T(8,128)(2,1)S(1)}, bf16[80,768]{1,0:T(8,128)(2,1)S(1)}, u32[]{:S(2)}, u32[]{:S(2)}) collective-permute-start(bf16[80,768]{1,0:T(8,128)(2,1)S(1)} %copy-done.26), channel_id=1, source_target_pairs={{0,1},{1,0},{2,3},{3,2},{4,5},{5,4},{6,7},{7,6},{8,9},{9,8},{10,11... | collective-permute-start | bytes 368648 | tf_op jit(solution)/shard_map/ppermute | solution.py:234
  92.1 0.7 copy-start.9
  (6 other events, 3.8 us)

commit v2 on v1

v2 whole, which is shorter than its diff:
```python
import functools
import math

import jax
import jax.numpy as jnp
from jax import lax
from jax.experimental import pallas as pl
from jax.experimental.pallas import tpu as pltpu
from jax.sharding import PartitionSpec as P

HEADS = 12
LOGIT = 3
BF16 = jnp.bfloat16
F32 = jnp.float32
VMEM_LIMIT = 12 * 1024 * 1024
LARGE_LIMIT = 56 * 1024 * 1024
MOST_GROUPS = 32
LANES = 128
TILE = 16


def layer_norm(field):
    average = jnp.mean(field, axis=-1, keepdims=True)
    centred = field - average
    variance = jnp.mean(centred * centred, axis=-1, keepdims=True)
    return centred * lax.rsqrt(variance + 1e-06)


def block_rows(slots, patches, width):
    return slots * patches * (width // LANES) + TILE


def embed_kernel(
    groups, per_owner, patches, steps, send_rows, pairs_hbm, enc_hbm, w_hbm, emb_hbm, normed_hbm, *rest
):
    sends = rest[: len(send_rows)]
    pairs, slots, ids, ranks, enc, w, emb, normed, filled, in_sem, out_sem = rest[len(send_rows) :]
    img_dev = enc.shape[0] // patches
    width = w.shape[1]
    loads = [
        pltpu.make_async_copy(pairs_hbm, pairs, in_sem.at[0]),
        pltpu.make_async_copy(w_hbm, w, in_sem.at[1]),
        pltpu.make_async_copy(enc_hbm, enc, in_sem.at[2]),
    ]
    for load in loads:
        load.start()
    position = lax.axis_index("img")
    for owner in range(groups):
        ranks[owner] = 0
        for rank in range(per_owner):
            slots[owner * per_owner + rank] = 0
            ids[owner * per_owner + rank] = 0
    loads[0].wait()
    unused = groups * per_owner

    @pl.loop(0, pairs.shape[1], unroll=4)
    def _(row):
        partner = pairs[1, row]
        live = partner >= 0
        owner = jnp.where(live, lax.div(partner, img_dev), groups)
        rank = jnp.where(live, ranks[owner], 0)
        ranks[owner] = rank + 1
        step = owner ^ position if len(send_rows) > 1 else owner
        at = jnp.where(live, step * per_owner + rank, unused)
        slots[at] = lax.rem(jnp.maximum(pairs[0, row], 0), img_dev) * patches
        ids[at] = lax.rem(jnp.maximum(partner, 0), img_dev) + 1

    loads[1].wait()
    loads[2].wait()
    embedded = jnp.dot(enc[...], w[...], preferred_element_type=F32).astype(BF16)
    emb[...] = embedded
    stores = [pltpu.make_async_copy(emb, emb_hbm, out_sem.at[0])]
    stores[-1].start()
    normed[...] = layer_norm(embedded.astype(F32)).astype(BF16)
    stores.append(pltpu.make_async_copy(normed, normed_hbm, out_sem.at[1]))
    stores[-1].start()

    span = per_owner * patches
    tall = block_rows(per_owner, patches, width)
    tile_row = lax.broadcasted_iota(jnp.int32, (TILE, LANES), 0)
    place = {}
    base = 0
    for n, rows in enumerate(send_rows):
        place[(base + rows) // tall - 1] = (n, base, rows)
        base += rows
    for block, step in enumerate(steps):
        top = block * tall
        marks = jnp.zeros((TILE, LANES), F32)
        for rank in range(per_owner):
            slot = step * per_owner + rank
            image = normed[pl.ds(pl.multiple_of(slots[slot], patches), patches), :]
            for f in range(width // LANES):
                to = top + f * span + rank * patches
                filled[to : to + patches, :] = image[:, f * LANES : (f + 1) * LANES]
            marks = jnp.where(tile_row == rank, ids[slot].astype(F32), marks)
        filled[top + tall - TILE : top + tall, :] = marks.astype(BF16)
        if block in place:
            n, base, rows = place[block]
            stores.append(pltpu.make_async_copy(filled.at[pl.ds(base, rows)], sends[n], out_sem.at[2 + n]))
            stores[-1].start()
    for store in stores:
        store.wait()


def join_kernel(copies, *refs):
    *refs, sem = refs
    moves = []
    for n, (source, at, target, to, rows) in enumerate(copies):
        part = refs[source].at[pl.ds(at, rows)]
        moves.append(pltpu.make_async_copy(part, refs[2 + target].at[pl.ds(to, rows)], sem.at[n]))
        moves[-1].start()
    for move in moves:
        move.wait()


def query_kernel(scale, normed_ref, w_ref, out_ref):
    rows = jnp.dot(normed_ref[...], w_ref[...], preferred_element_type=F32).astype(BF16)
    out_ref[...] = rows * jnp.asarray(scale, BF16)


def decode_kernel(
    parts, per_owner, patches, first_call, last_call, query_ref, emb_ref, wk_ref, wv_ref, wo_ref, wh_ref, *rest
):
    rest = list(rest)
    totals_in = None if first_call else rest.pop(0)
    operands = [rest.pop(0) for _ in range(1 + max(n for n, _ in parts))]
    if last_call:
        points_ref, descriptors_ref, confidence_ref, q_rows, e_rows, marks, ids, sem, totals_ref = rest
    else:
        totals_ref, q_rows, e_rows, marks, ids, sem = rest
    width = wk_ref.shape[0]
    pair = 2 * (width // HEADS)
    span = per_owner * patches
    tall = block_rows(per_owner, patches, width)

    rows = []
    for k, (n, block) in enumerate(parts):
        top = block * tall
        mark = operands[n][top + tall - TILE : top + tall, :]
        marks[k * TILE : (k + 1) * TILE, :] = mark.astype(F32).astype(jnp.int32)
        pieces = [operands[n][top + f * span : top + (f + 1) * span, :] for f in range(width // LANES)]
        rows.append(jnp.concatenate(pieces, axis=1))
    to_scalars = pltpu.make_async_copy(marks, ids, sem)
    to_scalars.start()
    x = jnp.concatenate(rows, axis=0) if len(rows) > 1 else rows[0]
    keys = jnp.dot(x, wk_ref[...], preferred_element_type=F32).astype(BF16)
    values = jnp.dot(x, wv_ref[...], preferred_element_type=F32).astype(BF16)

    to_scalars.wait()
    slots = [ids[k * TILE + rank, 0] for k in range(len(parts)) for rank in range(per_owner)]
    for n, mark in enumerate(slots):
        at = pl.ds(pl.multiple_of(jnp.maximum(mark - 1, 0) * patches, patches), patches)
        to = slice(n * patches, (n + 1) * patches)
        q_rows[to, :] = query_ref[at, :]
        e_rows[to, :] = emb_ref[at, :]

    zero = jnp.zeros((), BF16)
    attended = []
    some = span * max(1, LANES // span)
    for start in range(0, x.shape[0], some):
        cut = slice(start, min(start + some, x.shape[0]))
        size = cut.stop - cut.start
        first = lax.broadcasted_iota(jnp.int32, (size, pair), 1) < pair // 2
        at_row = lax.rem(lax.broadcasted_iota(jnp.int32, (2 * size, size), 0), size) // patches
        same = at_row == lax.broadcasted_iota(jnp.int32, (2 * size, size), 1) // patches
        found = []
        for p in range(HEADS // 2):
            cols = slice(p * pair, (p + 1) * pair)
            q = q_rows[cut, cols]
            both = jnp.concatenate([jnp.where(first, q, zero), jnp.where(first, zero, q)], axis=0)
            scores = lax.dot_general(
                both, keys[cut, cols], (((1,), (1,)), ((), ())), preferred_element_type=F32
            )
            exponent = jnp.exp(jnp.where(same, scores, -jnp.inf))
            weights = (exponent / jnp.sum(exponent, axis=-1, keepdims=True)).astype(BF16)
            mixed = jnp.dot(weights, values[cut, cols], preferred_element_type=F32)
            found.append(jnp.where(first, mixed[:size], mixed[size:]).astype(BF16))
        attended.append(jnp.concatenate(found, axis=1))
    attended = jnp.concatenate(attended, axis=0) if len(attended) > 1 else attended[0]
    updated = e_rows[...].astype(F32) + jnp.dot(attended, wo_ref[...], preferred_element_type=F32)
    head_input = layer_norm(updated).astype(BF16)
    head_out = lax.dot_general(
        head_input, wh_ref[...], (((1,), (1,)), ((), ())), preferred_element_type=F32
    )
    weight = 1.0 + jnp.exp(head_out[:, LOGIT : LOGIT + 1])
    column = lax.broadcasted_iota(jnp.int32, head_out.shape, 1)
    terms = jnp.where(column == LOGIT, weight, weight * head_out)
    totals_ref[...] = jnp.zeros(totals_ref.shape, F32) if first_call else totals_in[...]
    for n, mark in enumerate(slots):

        @pl.when(mark > 0)
        def _():
            at = pl.ds(pl.multiple_of((mark - 1) * patches, patches), patches)
            totals_ref[at, :] = totals_ref[at, :] + terms[n * patches : (n + 1) * patches, :]

    if last_call:
        img_dev = confidence_ref.shape[1]
        for token in range(patches):
            rows = jnp.transpose(totals_ref[pl.ds(token, img_dev, stride=patches), :])
            confidence = rows[LOGIT : LOGIT + 1]
            ratio = rows / (1.0 + confidence)
            confidence_ref[token : token + 1, :] = confidence
            for channel in range(LOGIT):
                points_ref[channel, token : token + 1, :] = ratio[channel : channel + 1]
            for channel in range(LOGIT + 1, rows.shape[0]):
                descriptors_ref[channel - LOGIT - 1, token : token + 1, :] = ratio[channel : channel + 1]


def vmem():
    return pl.BlockSpec(memory_space=pltpu.VMEM)


def smem():
    return pl.BlockSpec(memory_space=pltpu.SMEM)


def hbm():
    return pl.BlockSpec(memory_space=pltpu.HBM)


LITTLE = pl.CostEstimate(flops=1, bytes_accessed=1, transcendentals=0)


def per_device(enc_tokens, pair_list, w_embed, w_query, w_key, w_value, w_out, w_head):
    groups = lax.axis_size("img")
    img_dev, patches, enc_width = enc_tokens.shape
    width = w_query.shape[0]
    channels = w_head.shape[1]
    pair_dev = pair_list.shape[0]
    per_owner = (pair_dev + groups - 2) // (groups - 1)
    span = per_owner * patches
    own_rows = img_dev * patches
    params = pltpu.CompilerParams(vmem_limit_bytes=VMEM_LIMIT)
    large = pltpu.CompilerParams(vmem_limit_bytes=LARGE_LIMIT)
    by_permute = groups <= MOST_GROUPS and groups >= 8 and groups & (groups - 1) == 0
    tall = block_rows(per_owner, patches, width)

    def rows_of(count):
        return jax.ShapeDtypeStruct((count, width), BF16)

    def blocks_of(count):
        return jax.ShapeDtypeStruct((count * tall, LANES), BF16)

    chips = groups // 2
    far, near = list(range(chips // 2, chips)), list(range(1, chips // 2))
    if by_permute:
        steps = [2 * t for t in far + near] + [2 * t + 1 for t in range(chips)]
        counts = [chips - 1, chips]
    else:
        steps = list(range(groups))
        counts = [groups]
    embedded, normed, *sends = pl.pallas_call(
        functools.partial(embed_kernel, groups, per_owner, patches, steps, [c * tall for c in counts]),
        out_shape=[rows_of(own_rows)] * 2 + [blocks_of(c) for c in counts],
        in_specs=[hbm()] * 3,
        out_specs=[hbm()] * (2 + len(counts)),
        scratch_shapes=[
            pltpu.SMEM((2, pair_dev), jnp.int32),
            pltpu.SMEM((groups * per_owner + 1,), jnp.int32),
            pltpu.SMEM((groups * per_owner + 1,), jnp.int32),
            pltpu.SMEM((groups + 1,), jnp.int32),
            pltpu.VMEM((own_rows, enc_width), BF16),
            pltpu.VMEM((enc_width, width), BF16),
            pltpu.VMEM((own_rows, width), BF16),
            pltpu.VMEM((own_rows, width), BF16),
            pltpu.VMEM((len(steps) * tall, LANES), BF16),
            pltpu.SemaphoreType.DMA((3,)),
            pltpu.SemaphoreType.DMA((2 + len(counts),)),
        ],
        compiler_params=large,
        cost_estimate=LITTLE,
        name="embed",
    )(pair_list.T, enc_tokens.reshape(own_rows, enc_width), w_embed)

    queries = pl.pallas_call(
        functools.partial(query_kernel, 1.0 / math.sqrt(width // HEADS)),
        out_shape=jax.ShapeDtypeStruct((own_rows, width), BF16),
        in_specs=[vmem(), vmem()],
        out_specs=vmem(),
        compiler_params=params,
        cost_estimate=LITTLE,
        name="queries",
    )(normed, w_query)

    def decode(operands, parts, totals, last_call):
        count = span * len(parts)
        first_call = totals is None
        totals_shape = (own_rows, channels)
        scratch = [pltpu.VMEM((count, width), BF16)] * 2
        scratch.append(pltpu.VMEM((len(parts) * TILE, LANES), jnp.int32))
        scratch.append(pltpu.SMEM((len(parts) * TILE, LANES), jnp.int32))
        scratch.append(pltpu.SemaphoreType.DMA)
        if last_call:
            shapes = [(LOGIT, patches, img_dev), (channels - 1 - LOGIT, patches, img_dev), (patches, img_dev)]
            out_shape = [jax.ShapeDtypeStruct(s, F32) for s in shapes]
            out_specs = [vmem()] * 3
            scratch.append(pltpu.VMEM(totals_shape, F32))
        else:
            out_shape, out_specs = jax.ShapeDtypeStruct(totals_shape, F32), vmem()
        inputs = [queries, embedded, w_key, w_value, w_out, w_head.T]
        inputs += ([] if first_call else [totals]) + operands
        return pl.pallas_call(
            functools.partial(decode_kernel, parts, per_owner, patches, first_call, last_call),
            out_shape=out_shape,
            in_specs=[vmem()] * len(inputs),
            out_specs=out_specs,
            scratch_shapes=scratch,
            compiler_params=params,
            cost_estimate=LITTLE,
            name="decode",
        )(*inputs)

    if by_permute:

        def permute(block, step):
            return lax.ppermute(block, "img", [(i, i ^ step) for i in range(groups)])

        mate = permute(sends[1], 1)
        own, queries = lax.optimization_barrier((sends[0], queries))
        copies = []
        for n, t in enumerate(far + near):
            copies.append((0, n * tall, n, 0, tall))
            copies.append((1, t * tall, n, tall, tall))
        joined = pl.pallas_call(
            functools.partial(join_kernel, copies),
            out_shape=[blocks_of(2)] * (chips - 1),
            in_specs=[vmem()] * 2,
            out_specs=[pl.BlockSpec(memory_space=pl.ANY)] * (chips - 1),
            scratch_shapes=[pltpu.SemaphoreType.DMA((len(copies),))],
            compiler_params=params,
            cost_estimate=LITTLE,
            name="join",
        )(own, mate)
        both = dict(zip(far + near, joined))
        got = {t: permute(both[t], 2 * t) for t in far[:-1] + near}
        totals = decode([mate, got[near[0]]], [(0, 0), (1, 0), (1, 1)], None, False)
        for k in range(1, len(near), 2):
            pair = near[k : k + 2]
            parts = [(n, m) for n in range(len(pair)) for m in (0, 1)]
            totals = decode([got[t] for t in pair], parts, totals, False)
        last = far[-1]
        block, got[far[0]], totals = lax.optimization_barrier((both[last], got[far[0]], totals))
        got[last] = permute(block, 2 * last)
        for pair in (far[:2], far[2:-1], [last]):
            parts = [(n, m) for n in range(len(pair)) for m in (0, 1)]
            totals = decode([got[t] for t in pair], parts, totals, pair == [last])
    else:
        got = lax.all_to_all(sends[0].reshape(groups, tall, LANES), "img", 0, 0, tiled=True)
        some = math.gcd(groups, max(1, LANES // span))

        def decode_some(k, totals, last_call):
            block = lax.dynamic_slice_in_dim(got, k * some, some).reshape(some * tall, LANES)
            return decode([block], [(0, n) for n in range(some)], totals, last_call)

        totals = lax.fori_loop(
            0,
            groups // some - 1,
            lambda k, totals: decode_some(k, totals, False),
            jnp.zeros((own_rows, channels), F32),
        )
        totals = decode_some(groups // some - 1, totals, True)
    points, descriptors, confidence = totals
    return (
        jnp.transpose(points, (2, 0, 1)),
        jnp.transpose(descriptors, (2, 0, 1)),
        jnp.transpose(confidence),
    )


def solution(mesh):
    rows = P(("scene", "img"))
    return jax.shard_map(
        per_device,
        mesh=mesh,
        in_specs=(rows, rows, P(), P(), P(), P(), P(), P()),
        out_specs=(rows, rows, rows),
        check_vma=False,
    )
```

time: 96.5 us -> 66.6 us (0.69)
  local copies, waits for them, and re-layouts: 30.2 us -> 2.33 us
  waiting for transfers between devices: 0.04 us -> 19.5 us
  blocking collectives: 9.88 us -> 0 us
  starting transfers between devices: 25.7 us -> 16.9 us
  other arithmetic: 2.36 us -> 0 us
    unnamed x83 -> x16, local copies, waits for them, and re-layouts: 27 us -> 2.33 us
    ppermute x15 -> x8, waiting for transfers between devices: 0.04 us -> 19.5 us  [permute(): return lax.ppermute(block, 'img', [(i, i ^ step) for i in range(groups)])]
    unnamed x1 -> x0, blocking collectives: 9.88 us -> none
    ppermute x15 -> x8, starting transfers between devices: 25.7 us -> 16.9 us  [permute(): return lax.ppermute(block, 'img', [(i, i ^ step) for i in range(groups)])]
    reshape x2 -> x0, local copies, waits for them, and re-layouts: 1.93 us -> none  [the longest x1 1.15 us: per_device(): totals.reshape(img_dev, patches, channels)]
    div x2 -> x0, other arithmetic: 1.31 us -> none  [per_device(): return (totals[:, 0:3, :] / divisor, totals[:, 4:, :] / divisor, confidence)]
    gather x1 -> x0, local copies, waits for them, and re-layouts: 1.15 us -> none  [per_device(): table[source_of(jnp.arange(groups, dtype=jnp.int32), position, groups)]]
    pallas_call x8 -> x6, Pallas kernels: 20.2 us -> 20.5 us  [the longest x5 18.1 us: decode(): pl.pallas_call(functools.partial(decode_kernel, parts, per_owner, patches...]
  transfers between devices with their start and end apart: 15 -> 8, of which waited for: 0 -> 5; matrix products, arithmetic and copies ran while one was open for 5% -> 0% of each run, Pallas kernels for 20% -> 23%
where the time goes in v2:
time: 66.6 us; the launch traced here: 65.5 us
  Pallas kernels  26 us (39%)
  waiting for transfers between devices  19.5 us (29%)
  starting transfers between devices  16.9 us (25%)
  local copies, waits for them, and re-layouts  2.33 us (3%)
  between operations  0.76 us (1%)
    ppermute x8, waiting for transfers between devices, permute(): return lax.ppermute(block, 'img', [(i, i ^ step) for i in range(groups)])  19.5 us
    pallas_call x5, Pallas kernels, decode(): pl.pallas_call(functools.partial(decode_kernel, parts, per_owner, patches...  18.1 us
    ppermute x8, starting transfers between devices, permute(): return lax.ppermute(block, 'img', [(i, i ^ step) for i in range(groups)])  16.9 us
    pallas_call x1, Pallas kernels, per_device(): pl.pallas_call(functools.partial(embed_kernel, groups, per_owner, patches...  4.71 us
    pallas_call x1, Pallas kernels, per_device(): pl.pallas_call(functools.partial(join_kernel, copies), out_shape=[blocks_...  2.4 us
    unnamed x16, local copies, waits for them, and re-layouts  2.33 us
  transfers between devices with their start and end apart: 8, of which 5 were waited for; matrix products, arithmetic and copies ran while one was open for 0% of the time, Pallas kernels for 23%

profile of v2, /device:TPU:0, one launch (start us, length us, event | category | flops | bytes accessed | tf_op | source)
XLA Modules:
  0.0 65.5 jit_solution(12728942507352599695)
XLA Ops:
  0.6 0.0 copy-start.5
  0.6 4.7 %embed.1 = (bf16[512,768]{1,0:T(8,128)(2,1)}, bf16[512,768]{1,0:T(8,128)(2,1)}, bf16[3472,128]{1,0:T(8,128)(2,1)}, bf16[3968,128]{1,0:T(8,128)(2,1)}) custom-call(s32[2,64]{1,0:T(2,128)} %bitcast.12, bf16[512,1024]{1,0:T(8,128)(2,1)} %bitcast.11, bf16[1024,768]{1,0:T(8,128)(2,1)} %w_hbm.1), custom_call_target="tpu_custom_call" | custom-call | flops 1 | bytes 1 | tf_op jit(solution)/shard_map/embed/pallas_call | solution.py:252
  5.4 0.5 collective-permute-start
  5.9 0.0 copy-done.5
  5.9 0.0 copy-start.7
  5.9 1.1 %copy-done.7 = bf16[512,768]{1,0:T(8,128)(2,1)S(1)} copy-done((bf16[512,768]{1,0:T(8,128)(2,1)S(1)}, bf16[512,768]{1,0:T(8,128)(2,1)}, u32[]{:S(2)}) %copy-start.7) | copy-done | bytes 786456
  7.0 0.0 copy-start.1
  7.0 0.0 copy-start.2
  7.0 0.0 copy-start.3
  7.0 0.8 %queries.1.query_ref = bf16[512,768]{1,0:T(8,128)(2,1)S(1)} custom-call(bf16[512,768]{1,0:T(8,128)(2,1)S(1)} %copy-done.7, bf16[768,768]{1,0:T(8,128)(2,1)S(1)} %copy-done.5), custom_call_target="tpu_custom_call" | custom-call | flops 1 | bytes 1 | tf_op jit(solution)/shard_map/queries/pallas_call | solution.py:275
  7.8 0.0 copy-start
  7.8 0.0 copy-start.4
  7.8 0.5 collective-permute-done.refs_1_.rest_0_
  8.3 0.0 copy-start.6
  8.3 1.2 %copy-done.6 = bf16[3472,128]{1,0:T(8,128)(2,1)S(1)} copy-done((bf16[3472,128]{1,0:T(8,128)(2,1)S(1)}, bf16[3472,128]{1,0:T(8,128)(2,1)}, u32[]{:S(2)}) %copy-start.6) | copy-done | bytes 888856
  9.5 2.4 %join.1 = (bf16[992,128]{1,0:T(8,128)(2,1)S(1)}, bf16[992,128]{1,0:T(8,128)(2,1)S(1)}, bf16[992,128]{1,0:T(8,128)(2,1)S(1)}, bf16[992,128]{1,0:T(8,128)(2,1)S(1)...) custom-call(bf16[3472,128]{1,0:T(8,128)(2,1)S(1)} %copy-done.6, ...), custom_call_target="tpu_custom_call" | custom-call | flops 1 | bytes 1 | tf_op jit(solution)/shard_map/join/pallas_call | solution.py:324
  11.9 3.0 %collective-permute-start.2 = (bf16[992,128]{1,0:T(8,128)(2,1)S(1)}, bf16[992,128]{1,0:T(8,128)(2,1)S(1)}, u32[]{:S(2)}, u32[]{:S(2)}) collective-permute-start(bf16[992,128]{1,0:T(8,128)(2,1)S(1)} %get-tuple-element.30), channel_id=1, source_target_pairs={{0,2},{1,3},{2,0},{3,1},{4,6},{5,7},{6,4},{7,5},{8,10},{9,11},{10,... | collective-permute-start | bytes 761864 | tf_op jit(solution)/shard_map/ppermute | solution.py:316
  14.9 1.6 %collective-permute-start.3 = (bf16[992,128]{1,0:T(8,128)(2,1)S(1)}, bf16[992,128]{1,0:T(8,128)(2,1)S(1)}, u32[]{:S(2)}, u32[]{:S(2)}) collective-permute-start(bf16[992,128]{1,0:T(8,128)(2,1)S(1)} %get-tuple-element.31), channel_id=1, source_target_pairs={{0,4},{1,5},{2,6},{3,7},{4,0},{5,1},{6,2},{7,3},{8,12},{9,13},{10,... | collective-permute-start | bytes 761864 | tf_op jit(solution)/shard_map/ppermute | solution.py:316
  16.4 0.0 collective-permute-start.4
  16.4 3.0 %collective-permute-start.1 = (bf16[992,128]{1,0:T(8,128)(2,1)S(1)}, bf16[992,128]{1,0:T(8,128)(2,1)S(1)}, u32[]{:S(2)}, u32[]{:S(2)}) collective-permute-start(bf16[992,128]{1,0:T(8,128)(2,1)S(1)} %get-tuple-element.29), channel_id=1, source_target_pairs={{0,8},{1,9},{2,10},{3,11},{4,12},{5,13},{6,14},{7,15},{8,0},{9,1},... | collective-permute-start | bytes 761864 | tf_op jit(solution)/shard_map/ppermute | solution.py:316
  19.4 1.3 %collective-permute-start.5 = (bf16[992,128]{1,0:T(8,128)(2,1)S(1)}, bf16[992,128]{1,0:T(8,128)(2,1)S(1)}, u32[]{:S(2)}, u32[]{:S(2)}) collective-permute-start(bf16[992,128]{1,0:T(8,128)(2,1)S(1)} %get-tuple-element.35), channel_id=1, source_target_pairs={{0,10},{1,11},{2,8},{3,9},{4,14},{5,15},{6,12},{7,13},{8,2},{9,3},... | collective-permute-start | bytes 761864 | tf_op jit(solution)/shard_map/ppermute | solution.py:316
  20.7 0.6 collective-permute-done.2.rest_1_
  21.3 3.8 %collective-permute-start.6 = (bf16[992,128]{1,0:T(8,128)(2,1)S(1)}, bf16[992,128]{1,0:T(8,128)(2,1)S(1)}, u32[]{:S(2)}, u32[]{:S(2)}) collective-permute-start(bf16[992,128]{1,0:T(8,128)(2,1)S(1)} %get-tuple-element.36), channel_id=1, source_target_pairs={{0,12},{1,13},{2,14},{3,15},{4,8},{5,9},{6,10},{7,11},{8,4},{9,5},... | collective-permute-start | bytes 761864 | tf_op jit(solution)/shard_map/ppermute | solution.py:316
  25.1 0.0 copy-done.1
  25.1 0.0 copy-done.2
  25.1 0.0 copy-done.3
  25.1 0.0 copy-done
  25.1 0.0 copy-done.4
  25.1 3.4 %decode.5.rest_0_ = f32[512,28]{1,0:T(8,128)S(1)} custom-call(bf16[512,768]{1,0:T(8,128)(2,1)S(1)} %queries.1.query_ref, bf16[512,768]{1,0:T(8,128)(2,1)S(1)} %copy-done.3, bf16[768,768]{1,0:T(8,128)(2,1)S(1)} %copy-done, bf16[768,768]{1,0:T(8,128)(2,1)S(1)} %copy-done.1, bf16[768,768]{1,0:T(8,128)(2,1)S(1)} %copy-done.2, bf16[28,768]{1,0:T(8,128)(2,1)S(1)} %bitcast.6, ...), custom_call_target="tpu_custom_call" | custom-call | flops 1 | bytes 1 | tf_op jit(solution)/shard_map/decode/pallas_call | solution.py:302
  28.6 5.4 %collective-permute-done.3.rest_1_ = bf16[992,128]{1,0:T(8,128)(2,1)S(1)} collective-permute-done((bf16[992,128]{1,0:T(8,128)(2,1)S(1)}, bf16[992,128]{1,0:T(8,128)(2,1)S(1)}, u32[]{:S(2)}, u32[]{:S(2)}) %collective-permute-start.3) | collective-permute-done | bytes 253984 | tf_op jit(solution)/shard_map/ppermute | solution.py:316
  34.0 3.4 %collective-permute-done.4.rest_2_ = bf16[992,128]{1,0:T(8,128)(2,1)S(1)} collective-permute-done((bf16[992,128]{1,0:T(8,128)(2,1)S(1)}, bf16[992,128]{1,0:T(8,128)(2,1)S(1)}, u32[]{:S(2)}, u32[]{:S(2)}) %collective-permute-start.4) | collective-permute-done | bytes 253984 | tf_op jit(solution)/shard_map/ppermute | solution.py:316
  37.4 4.2 %decode.6.rest_0_ = f32[512,28]{1,0:T(8,128)S(1)} custom-call(bf16[512,768]{1,0:T(8,128)(2,1)S(1)} %queries.1.query_ref, bf16[512,768]{1,0:T(8,128)(2,1)S(1)} %copy-done.3, bf16[768,768]{1,0:T(8,128)(2,1)S(1)} %copy-done, bf16[768,768]{1,0:T(8,128)(2,1)S(1)} %copy-done.1, bf16[768,768]{1,0:T(8,128)(2,1)S(1)} %copy-done.2, bf16[28,768]{1,0:T(8,128)(2,1)S(1)} %bitcast.7, ...), custom_call_target="tpu_custom_call" | custom-call | flops 1 | bytes 1 | tf_op jit(solution)/shard_map/decode/pallas_call | solution.py:302
  41.6 0.0 collective-permute-done.1.rest_1_
  41.6 3.8 %collective-permute-start.7 = (bf16[992,128]{1,0:T(8,128)(2,1)S(1)}, bf16[992,128]{1,0:T(8,128)(2,1)S(1)}, u32[]{:S(2)}, u32[]{:S(2)}) collective-permute-start(bf16[992,128]{1,0:T(8,128)(2,1)S(1)} %get-tuple-element.37), channel_id=1, source_target_pairs={{0,14},{1,15},{2,12},{3,13},{4,10},{5,11},{6,8},{7,9},{8,6},{9,7},... | collective-permute-start | bytes 761864 | tf_op jit(solution)/shard_map/ppermute | solution.py:316
  45.4 9.6 %collective-permute-done.5.rest_2_ = bf16[992,128]{1,0:T(8,128)(2,1)S(1)} collective-permute-done((bf16[992,128]{1,0:T(8,128)(2,1)S(1)}, bf16[992,128]{1,0:T(8,128)(2,1)S(1)}, u32[]{:S(2)}, u32[]{:S(2)}) %collective-permute-start.5) | collective-permute-done | bytes 253984 | tf_op jit(solution)/shard_map/ppermute | solution.py:316
  55.0 4.2 %decode.7.rest_0_ = f32[512,28]{1,0:T(8,128)S(1)} custom-call(bf16[512,768]{1,0:T(8,128)(2,1)S(1)} %queries.1.query_ref, bf16[512,768]{1,0:T(8,128)(2,1)S(1)} %copy-done.3, bf16[768,768]{1,0:T(8,128)(2,1)S(1)} %copy-done, bf16[768,768]{1,0:T(8,128)(2,1)S(1)} %copy-done.1, bf16[768,768]{1,0:T(8,128)(2,1)S(1)} %copy-done.2, bf16[28,768]{1,0:T(8,128)(2,1)S(1)} %bitcast.8, ...), custom_call_target="tpu_custom_call" | custom-call | flops 1 | bytes 1 | tf_op jit(solution)/shard_map/decode/pallas_call | solution.py:302
  59.2 0.0 collective-permute-done.6.rest_1_
  59.2 2.7 %decode.8.rest_0_ = f32[512,28]{1,0:T(8,128)S(1)} custom-call(bf16[512,768]{1,0:T(8,128)(2,1)S(1)} %queries.1.query_ref, bf16[512,768]{1,0:T(8,128)(2,1)S(1)} %copy-done.3, bf16[768,768]{1,0:T(8,128)(2,1)S(1)} %copy-done, bf16[768,768]{1,0:T(8,128)(2,1)S(1)} %copy-done.1, bf16[768,768]{1,0:T(8,128)(2,1)S(1)} %copy-done.2, bf16[28,768]{1,0:T(8,128)(2,1)S(1)} %bitcast.9, ...), custom_call_target="tpu_custom_call" | custom-call | flops 1 | bytes 1 | tf_op jit(solution)/shard_map/decode/pallas_call | solution.py:302
  61.9 0.0 collective-permute-done.7.rest_1_
  61.9 3.6 %decode.9 = (f32[3,16,32]{2,1,0:T(8,128)}, f32[24,16,32]{2,1,0:T(8,128)}, f32[16,32]{1,0:T(8,128)}) custom-call(bf16[512,768]{1,0:T(8,128)(2,1)S(1)} %queries.1.query_ref, bf16[512,768]{1,0:T(8,128)(2,1)S(1)} %copy-done.3, bf16[768,768]{1,0:T(8,128)(2,1)S(1)} %copy-done, bf16[768,768]{1,0:T(8,128)(2,1)S(1)} %copy-done.1, bf16[768,768]{1,0:T(8,128)(2,1)S(1)} %copy-done.2, ...), custom_call_target="tpu_custom_call" | custom-call | flops 1 | bytes 1 | tf_op jit(solution)/shard_map/decode/pallas_call | solution.py:302
Async XLA Ops:
  0.6 5.2 %copy-start.5 = (bf16[768,768]{1,0:T(8,128)(2,1)S(1)}, bf16[768,768]{1,0:T(8,128)(2,1)}, u32[]{:S(2)}) copy-start(bf16[768,768]{1,0:T(8,128)(2,1)} %w_ref.1) | copy-start | bytes 3538948
  5.4 3.0 %collective-permute-start = (bf16[3968,128]{1,0:T(8,128)(2,1)}, bf16[3968,128]{1,0:T(8,128)(2,1)S(1)}, u32[]{:S(2)}, u32[]{:S(2)}) collective-permute-start(bf16[3968,128]{1,0:T(8,128)(2,1)} %get-tuple-element.27), channel_id=1, source_target_pairs={{0,1},{1,0},{2,3},{3,2},{4,5},{5,4},{6,7},{7,6},{8,9},{9,8},{10,11... | collective-permute-start | bytes 3047432 | tf_op jit(solution)/shard_map/ppermute | solution.py:316
  5.9 1.1 %copy-start.7 = (bf16[512,768]{1,0:T(8,128)(2,1)S(1)}, bf16[512,768]{1,0:T(8,128)(2,1)}, u32[]{:S(2)}) copy-start(bf16[512,768]{1,0:T(8,128)(2,1)} %get-tuple-element.23.normed_ref) | copy-start | bytes 2359300
  7.0 18.1 %copy-start.1 = (bf16[768,768]{1,0:T(8,128)(2,1)S(1)}, bf16[768,768]{1,0:T(8,128)(2,1)}, u32[]{:S(2)}) copy-start(bf16[768,768]{1,0:T(8,128)(2,1)} %wv_ref.9) | copy-start | bytes 3538948
  7.0 18.1 %copy-start.2 = (bf16[768,768]{1,0:T(8,128)(2,1)S(1)}, bf16[768,768]{1,0:T(8,128)(2,1)}, u32[]{:S(2)}) copy-start(bf16[768,768]{1,0:T(8,128)(2,1)} %wo_ref.9) | copy-start | bytes 3538948
  7.0 18.1 %copy-start.3 = (bf16[512,768]{1,0:T(8,128)(2,1)S(1)}, bf16[512,768]{1,0:T(8,128)(2,1)}, u32[]{:S(2)}) copy-start(bf16[512,768]{1,0:T(8,128)(2,1)} %get-tuple-element.25.emb_ref) | copy-start | bytes 2359300
  7.8 17.3 %copy-start = (bf16[768,768]{1,0:T(8,128)(2,1)S(1)}, bf16[768,768]{1,0:T(8,128)(2,1)}, u32[]{:S(2)}) copy-start(bf16[768,768]{1,0:T(8,128)(2,1)} %wk_ref.9) | copy-start | bytes 3538948
  7.8 17.3 %copy-start.4 = (bf16[768,28]{0,1:T(8,128)(2,1)S(1)}, bf16[768,28]{0,1:T(8,128)(2,1)}, u32[]{:S(2)}) copy-start(bf16[768,28]{0,1:T(8,128)(2,1)} %param.15) | copy-start | bytes 129028
  8.3 1.2 %copy-start.6 = (bf16[3472,128]{1,0:T(8,128)(2,1)S(1)}, bf16[3472,128]{1,0:T(8,128)(2,1)}, u32[]{:S(2)}) copy-start(bf16[3472,128]{1,0:T(8,128)(2,1)} %get-tuple-element.26.refs_0_) | copy-start | bytes 2666500
  11.9 9.4 %collective-permute-start.2 = (bf16[992,128]{1,0:T(8,128)(2,1)S(1)}, bf16[992,128]{1,0:T(8,128)(2,1)S(1)}, u32[]{:S(2)}, u32[]{:S(2)}) collective-permute-start(bf16[992,128]{1,0:T(8,128)(2,1)S(1)} %get-tuple-element.30), channel_id=1, source_target_pairs={{0,2},{1,3},{2,0},{3,1},{4,6},{5,7},{6,4},{7,5},{8,10},{9,11},{10,... | collective-permute-start | bytes 761864 | tf_op jit(solution)/shard_map/ppermute | solution.py:316
  14.9 19.1 %collective-permute-start.3 = (bf16[992,128]{1,0:T(8,128)(2,1)S(1)}, bf16[992,128]{1,0:T(8,128)(2,1)S(1)}, u32[]{:S(2)}, u32[]{:S(2)}) collective-permute-start(bf16[992,128]{1,0:T(8,128)(2,1)S(1)} %get-tuple-element.31), channel_id=1, source_target_pairs={{0,4},{1,5},{2,6},{3,7},{4,0},{5,1},{6,2},{7,3},{8,12},{9,13},{10,... | collective-permute-start | bytes 761864 | tf_op jit(solution)/shard_map/ppermute | solution.py:316
  16.4 21.0 %collective-permute-start.4 = (bf16[992,128]{1,0:T(8,128)(2,1)S(1)}, bf16[992,128]{1,0:T(8,128)(2,1)S(1)}, u32[]{:S(2)}, u32[]{:S(2)}) collective-permute-start(bf16[992,128]{1,0:T(8,128)(2,1)S(1)} %get-tuple-element.32), channel_id=1, source_target_pairs={{0,6},{1,7},{2,4},{3,5},{4,2},{5,3},{6,0},{7,1},{8,14},{9,15},{10,... | collective-permute-start | bytes 761864 | tf_op jit(solution)/shard_map/ppermute | solution.py:316
  16.4 25.2 %collective-permute-start.1 = (bf16[992,128]{1,0:T(8,128)(2,1)S(1)}, bf16[992,128]{1,0:T(8,128)(2,1)S(1)}, u32[]{:S(2)}, u32[]{:S(2)}) collective-permute-start(bf16[992,128]{1,0:T(8,128)(2,1)S(1)} %get-tuple-element.29), channel_id=1, source_target_pairs={{0,8},{1,9},{2,10},{3,11},{4,12},{5,13},{6,14},{7,15},{8,0},{9,1},... | collective-permute-start | bytes 761864 | tf_op jit(solution)/shard_map/ppermute | solution.py:316
  19.4 35.5 %collective-permute-start.5 = (bf16[992,128]{1,0:T(8,128)(2,1)S(1)}, bf16[992,128]{1,0:T(8,128)(2,1)S(1)}, u32[]{:S(2)}, u32[]{:S(2)}) collective-permute-start(bf16[992,128]{1,0:T(8,128)(2,1)S(1)} %get-tuple-element.35), channel_id=1, source_target_pairs={{0,10},{1,11},{2,8},{3,9},{4,14},{5,15},{6,12},{7,13},{8,2},{9,3},... | collective-permute-start | bytes 761864 | tf_op jit(solution)/shard_map/ppermute | solution.py:316
  21.3 37.9 %collective-permute-start.6 = (bf16[992,128]{1,0:T(8,128)(2,1)S(1)}, bf16[992,128]{1,0:T(8,128)(2,1)S(1)}, u32[]{:S(2)}, u32[]{:S(2)}) collective-permute-start(bf16[992,128]{1,0:T(8,128)(2,1)S(1)} %get-tuple-element.36), channel_id=1, source_target_pairs={{0,12},{1,13},{2,14},{3,15},{4,8},{5,9},{6,10},{7,11},{8,4},{9,5},... | collective-permute-start | bytes 761864 | tf_op jit(solution)/shard_map/ppermute | solution.py:316
  41.6 20.3 %collective-permute-start.7 = (bf16[992,128]{1,0:T(8,128)(2,1)S(1)}, bf16[992,128]{1,0:T(8,128)(2,1)S(1)}, u32[]{:S(2)}, u32[]{:S(2)}) collective-permute-start(bf16[992,128]{1,0:T(8,128)(2,1)S(1)} %get-tuple-element.37), channel_id=1, source_target_pairs={{0,14},{1,15},{2,12},{3,13},{4,10},{5,11},{6,8},{7,9},{8,6},{9,7},... | collective-permute-start | bytes 761864 | tf_op jit(solution)/shard_map/ppermute | solution.py:316

commit v3 on v2

--- a/solution.py
+++ b/solution.py
@@ -17,6 +17,7 @@
 MOST_GROUPS = 32
 LANES = 128
 TILE = 16
+MARK_BASE = 1024
 
 
 def layer_norm(field):
@@ -30,13 +31,31 @@
     return slots * patches * (width // LANES) + TILE
 
 
+def fill(filled, normed, table, steps, per_owner, patches):
+    width = normed.shape[1]
+    span = per_owner * patches
+    tall = block_rows(per_owner, patches, width)
+    tile_row = lax.broadcasted_iota(jnp.int32, (TILE, LANES), 0)
+    for block, step in enumerate(steps):
+        top = block * tall
+        marks = jnp.zeros((TILE, LANES), F32)
+        for rank in range(per_owner):
+            entry = table[step * per_owner + rank]
+            at = pl.multiple_of(lax.div(entry, MARK_BASE) * patches, patches)
+            image = normed[pl.ds(at, patches), :]
+            for f in range(width // LANES):
+                to = top + f * span + rank * patches
+                filled[to : to + patches, :] = image[:, f * LANES : (f + 1) * LANES]
+            marks = jnp.where(tile_row == rank, lax.rem(entry, MARK_BASE).astype(F32), marks)
+        filled[top + tall - TILE : top + tall, :] = marks.astype(BF16)
+
+
 def embed_kernel(
-    groups, per_owner, patches, steps, send_rows, pairs_hbm, enc_hbm, w_hbm, emb_hbm, normed_hbm, *rest
+    groups, per_owner, patches, by_distance, sets, pairs_hbm, enc_hbm, w_hbm, emb_hbm, normed_hbm, *rest
 ):
-    sends = rest[: len(send_rows)]
-    pairs, slots, ids, ranks, enc, w, emb, normed, filled, in_sem, out_sem = rest[len(send_rows) :]
+    sends = rest[: len(sets)]
+    pairs, table, ranks, enc, w, emb, normed, filled, in_sem, out_sem = rest[len(sets) :]
     img_dev = enc.shape[0] // patches
-    width = w.shape[1]
     loads = [
         pltpu.make_async_copy(pairs_hbm, pairs, in_sem.at[0]),
         pltpu.make_async_copy(w_hbm, w, in_sem.at[1]),
@@ -45,13 +64,12 @@
     for load in loads:
         load.start()
     position = lax.axis_index("img")
+    unused = groups * per_owner
     for owner in range(groups):
         ranks[owner] = 0
-        for rank in range(per_owner):
-            slots[owner * per_owner + rank] = 0
-            ids[owner * per_owner + rank] = 0
+    for slot in range(unused):
+        table[slot] = 0
     loads[0].wait()
-    unused = groups * per_owner
 
     @pl.loop(0, pairs.shape[1], unroll=4)
     def _(row):
@@ -60,10 +78,10 @@
         owner = jnp.where(live, lax.div(partner, img_dev), groups)
         rank = jnp.where(live, ranks[owner], 0)
         ranks[owner] = rank + 1
-        step = owner ^ position if len(send_rows) > 1 else owner
+        step = owner ^ position if by_distance else owner
         at = jnp.where(live, step * per_owner + rank, unused)
-        slots[at] = lax.rem(jnp.maximum(pairs[0, row], 0), img_dev) * patches
-        ids[at] = lax.rem(jnp.maximum(partner, 0), img_dev) + 1
+        image = lax.rem(jnp.maximum(pairs[0, row], 0), img_dev)
+        table[at] = image * MARK_BASE + lax.rem(jnp.maximum(partner, 0), img_dev) + 1
 
     loads[1].wait()
     loads[2].wait()
@@ -74,43 +92,27 @@
     normed[...] = layer_norm(embedded.astype(F32)).astype(BF16)
     stores.append(pltpu.make_async_copy(normed, normed_hbm, out_sem.at[1]))
     stores[-1].start()
-
-    span = per_owner * patches
-    tall = block_rows(per_owner, patches, width)
-    tile_row = lax.broadcasted_iota(jnp.int32, (TILE, LANES), 0)
-    place = {}
-    base = 0
-    for n, rows in enumerate(send_rows):
-        place[(base + rows) // tall - 1] = (n, base, rows)
-        base += rows
-    for block, step in enumerate(steps):
-        top = block * tall
-        marks = jnp.zeros((TILE, LANES), F32)
-        for rank in range(per_owner):
-            slot = step * per_owner + rank
-            image = normed[pl.ds(pl.multiple_of(slots[slot], patches), patches), :]
-            for f in range(width // LANES):
-                to = top + f * span + rank * patches
-                filled[to : to + patches, :] = image[:, f * LANES : (f + 1) * LANES]
-            marks = jnp.where(tile_row == rank, ids[slot].astype(F32), marks)
-        filled[top + tall - TILE : top + tall, :] = marks.astype(BF16)
-        if block in place:
-            n, base, rows = place[block]
-            stores.append(pltpu.make_async_copy(filled.at[pl.ds(base, rows)], sends[n], out_sem.at[2 + n]))
-            stores[-1].start()
+    row = 0
+    for n, steps in enumerate(sets):
+        rows = sends[n].shape[0]
+        part = filled.at[pl.ds(row, rows)]
+        fill(part, normed, table, steps, per_owner, patches)
+        stores.append(pltpu.make_async_copy(part, sends[n], out_sem.at[2 + n]))
+        stores[-1].start()
+        row += rows
     for store in stores:
         store.wait()
 
 
+def load_kernel(from_ref, to_ref, sem):
+    move = pltpu.make_async_copy(from_ref, to_ref, sem)
+    move.start()
+    move.wait()
+
+
 def join_kernel(copies, *refs):
-    *refs, sem = refs
-    moves = []
-    for n, (source, at, target, to, rows) in enumerate(copies):
-        part = refs[source].at[pl.ds(at, rows)]
-        moves.append(pltpu.make_async_copy(part, refs[2 + target].at[pl.ds(to, rows)], sem.at[n]))
-        moves[-1].start()
-    for move in moves:
-        move.wait()
+    for source, at, target, to, rows in copies:
+        refs[2 + target][to : to + rows, :] = refs[source][at : at + rows, :]
 
 
 def query_kernel(scale, normed_ref, w_ref, out_ref):
@@ -187,11 +189,9 @@
     terms = jnp.where(column == LOGIT, weight, weight * head_out)
     totals_ref[...] = jnp.zeros(totals_ref.shape, F32) if first_call else totals_in[...]
     for n, mark in enumerate(slots):
-
-        @pl.when(mark > 0)
-        def _():
-            at = pl.ds(pl.multiple_of((mark - 1) * patches, patches), patches)
-            totals_ref[at, :] = totals_ref[at, :] + terms[n * patches : (n + 1) * patches, :]
+        at = pl.ds(pl.multiple_of(jnp.maximum(mark - 1, 0) * patches, patches), patches)
+        term = terms[n * patches : (n + 1) * patches, :]
+        totals_ref[at, :] = totals_ref[at, :] + jnp.where(mark > 0, term, 0.0)
 
     if last_call:
         img_dev = confidence_ref.shape[1]
@@ -200,10 +200,9 @@
             confidence = rows[LOGIT : LOGIT + 1]
             ratio = rows / (1.0 + confidence)
             confidence_ref[token : token + 1, :] = confidence
-            for channel in range(LOGIT):
-                points_ref[channel, token : token + 1, :] = ratio[channel : channel + 1]
-            for channel in range(LOGIT + 1, rows.shape[0]):
-                descriptors_ref[channel - LOGIT - 1, token : token + 1, :] = ratio[channel : channel + 1]
+            points_ref[pl.ds(token, LOGIT, stride=patches), :] = ratio[:LOGIT]
+            count = rows.shape[0] - LOGIT - 1
+            descriptors_ref[pl.ds(token, count, stride=patches), :] = ratio[LOGIT + 1 :]
 
 
 def vmem():
@@ -244,28 +243,26 @@
     chips = groups // 2
     far, near = list(range(chips // 2, chips)), list(range(1, chips // 2))
     if by_permute:
-        steps = [2 * t for t in far + near] + [2 * t + 1 for t in range(chips)]
-        counts = [chips - 1, chips]
+        sets = [[2 * t + 1 for t in [0] + far], [2 * far[0]], [2 * t for t in far[1:]]]
+        sets += [[2 * t + 1 for t in near], [2 * t for t in near]]
     else:
-        steps = list(range(groups))
-        counts = [groups]
+        sets = [list(range(groups))]
     embedded, normed, *sends = pl.pallas_call(
-        functools.partial(embed_kernel, groups, per_owner, patches, steps, [c * tall for c in counts]),
-        out_shape=[rows_of(own_rows)] * 2 + [blocks_of(c) for c in counts],
+        functools.partial(embed_kernel, groups, per_owner, patches, by_permute, sets),
+        out_shape=[rows_of(own_rows)] * 2 + [blocks_of(len(steps)) for steps in sets],
         in_specs=[hbm()] * 3,
-        out_specs=[hbm()] * (2 + len(counts)),
+        out_specs=[hbm()] * (2 + len(sets)),
         scratch_shapes=[
             pltpu.SMEM((2, pair_dev), jnp.int32),
-            pltpu.SMEM((groups * per_owner + 1,), jnp.int32),
             pltpu.SMEM((groups * per_owner + 1,), jnp.int32),
             pltpu.SMEM((groups + 1,), jnp.int32),
             pltpu.VMEM((own_rows, enc_width), BF16),
             pltpu.VMEM((enc_width, width), BF16),
             pltpu.VMEM((own_rows, width), BF16),
             pltpu.VMEM((own_rows, width), BF16),
-            pltpu.VMEM((len(steps) * tall, LANES), BF16),
+            pltpu.VMEM((sum(len(steps) for steps in sets) * tall, LANES), BF16),
             pltpu.SemaphoreType.DMA((3,)),
-            pltpu.SemaphoreType.DMA((2 + len(counts),)),
+            pltpu.SemaphoreType.DMA((2 + len(sets),)),
         ],
         compiler_params=large,
         cost_estimate=LITTLE,
@@ -274,8 +271,8 @@
 
     queries = pl.pallas_call(
         functools.partial(query_kernel, 1.0 / math.sqrt(width // HEADS)),
-        out_shape=jax.ShapeDtypeStruct((own_rows, width), BF16),
-        in_specs=[vmem(), vmem()],
+        out_shape=rows_of(own_rows),
+        in_specs=[vmem()] * 2,
         out_specs=vmem(),
         compiler_params=params,
         cost_estimate=LITTLE,
@@ -291,7 +288,7 @@
         scratch.append(pltpu.SMEM((len(parts) * TILE, LANES), jnp.int32))
         scratch.append(pltpu.SemaphoreType.DMA)
         if last_call:
-            shapes = [(LOGIT, patches, img_dev), (channels - 1 - LOGIT, patches, img_dev), (patches, img_dev)]
+            shapes = [(LOGIT * patches, img_dev), ((channels - 1 - LOGIT) * patches, img_dev), (patches, img_dev)]
             out_shape = [jax.ShapeDtypeStruct(s, F32) for s in shapes]
             out_specs = [vmem()] * 3
             scratch.append(pltpu.VMEM(totals_shape, F32))
@@ -315,35 +312,60 @@
         def permute(block, step):
             return lax.ppermute(block, "img", [(i, i ^ step) for i in range(groups)])
 
-        mate = permute(sends[1], 1)
-        own, queries = lax.optimization_barrier((sends[0], queries))
-        copies = []
-        for n, t in enumerate(far + near):
-            copies.append((0, n * tall, n, 0, tall))
-            copies.append((1, t * tall, n, tall, tall))
-        joined = pl.pallas_call(
-            functools.partial(join_kernel, copies),
-            out_shape=[blocks_of(2)] * (chips - 1),
-            in_specs=[vmem()] * 2,
-            out_specs=[pl.BlockSpec(memory_space=pl.ANY)] * (chips - 1),
-            scratch_shapes=[pltpu.SemaphoreType.DMA((len(copies),))],
+        mate_far, mate_near = permute(sends[0], 1), permute(sends[3], 1)
+        first = permute(sends[1], 2 * far[0])
+        own_far = pl.pallas_call(
+            load_kernel,
+            out_shape=blocks_of(len(far) - 1),
+            in_specs=[hbm()],
+            out_specs=vmem(),
+            scratch_shapes=[pltpu.SemaphoreType.DMA],
             compiler_params=params,
             cost_estimate=LITTLE,
-            name="join",
-        )(own, mate)
-        both = dict(zip(far + near, joined))
-        got = {t: permute(both[t], 2 * t) for t in far[:-1] + near}
-        totals = decode([mate, got[near[0]]], [(0, 0), (1, 0), (1, 1)], None, False)
-        for k in range(1, len(near), 2):
-            pair = near[k : k + 2]
+            name="load",
+        )(sends[2])
+
+        def join(own, mate, counts, copies):
+            copies = [(n, at * tall, target, to * tall, tall) for n, at, target, to in copies]
+            return pl.pallas_call(
+                functools.partial(join_kernel, copies),
+                out_shape=[blocks_of(c) for c in counts],
+                in_specs=[vmem()] * 2,
+                out_specs=[vmem()] * len(counts),
+                compiler_params=params,
+                cost_estimate=LITTLE,
+                name="join",
+            )(own, mate)
+
+        copies = []
+        for n in range(len(far) - 1):
+            copies += [(0, n, n, 0), (1, n + 2, n, 1)]
+        copies.append((1, 1, len(far) - 1, 0))
+        *both, late = join(own_far, mate_far, [2] * (len(far) - 1) + [1], copies)
+        both = dict(zip(far[1:], both))
+        copies = []
+        for n in range(len(near)):
+            copies += [(0, n, n, 0), (1, n, n, 1)]
+        both.update(zip(near, join(sends[4], mate_near, [2] * len(near), copies)))
+
+        got = {far[1]: permute(both[far[1]], 2 * far[1])}
+        for t in near:
+            got[t] = permute(both[t], 2 * t)
+        totals = decode([mate_far], [(0, 0)], None, False)
+        block, first, totals = lax.optimization_barrier((both[far[2]], first, totals))
+        got[far[2]] = permute(block, 2 * far[2])
+        totals = decode([first], [(0, 0)], totals, False)
+        for n in range(3, len(far)):
+            block, got[far[n - 2]], totals = lax.optimization_barrier((both[far[n]], got[far[n - 2]], totals))
+            got[far[n]] = permute(block, 2 * far[n])
+        totals = decode([got[far[1]]], [(0, 0), (0, 1)], totals, False)
+        late, got[far[-2]], totals = lax.optimization_barrier((late, got[far[-2]], totals))
+        last = permute(late, 2 * far[0])
+        plan = [near[:2], near[2:]] + [[t] for t in far[2:]]
+        for pair in plan:
             parts = [(n, m) for n in range(len(pair)) for m in (0, 1)]
             totals = decode([got[t] for t in pair], parts, totals, False)
-        last = far[-1]
-        block, got[far[0]], totals = lax.optimization_barrier((both[last], got[far[0]], totals))
-        got[last] = permute(block, 2 * last)
-        for pair in (far[:2], far[2:-1], [last]):
-            parts = [(n, m) for n in range(len(pair)) for m in (0, 1)]
-            totals = decode([got[t] for t in pair], parts, totals, pair == [last])
+        totals = decode([last], [(0, 0)], totals, True)
     else:
         got = lax.all_to_all(sends[0].reshape(groups, tall, LANES), "img", 0, 0, tiled=True)
         some = math.gcd(groups, max(1, LANES // span))
@@ -361,8 +383,8 @@
         totals = decode_some(groups // some - 1, totals, True)
     points, descriptors, confidence = totals
     return (
-        jnp.transpose(points, (2, 0, 1)),
-        jnp.transpose(descriptors, (2, 0, 1)),
+        jnp.transpose(points.reshape(LOGIT, patches, img_dev), (2, 0, 1)),
+        jnp.transpose(descriptors.reshape(channels - 1 - LOGIT, patches, img_dev), (2, 0, 1)),
         jnp.transpose(confidence),
     )
 

time: 66.6 us -> 60.7 us (0.911); the launches traced: 65.5 us -> 60.5 us
  waiting for transfers between devices: 19.5 us -> 12.2 us
  Pallas kernels: 26 us -> 28 us
    ppermute x8 -> x10, waiting for transfers between devices: 19.5 us -> 12.2 us  [permute(): return lax.ppermute(block, 'img', [(i, i ^ step) for i in range(groups)])]
    pallas_call x5 -> x8, Pallas kernels: 18.1 us -> 22.2 us  [decode(): pl.pallas_call(functools.partial(decode_kernel, parts, per_owner, patches...]
    pallas_call x1 -> x3, Pallas kernels: 2.4 us -> 0.29 us  [the longest x1 0.18 us: per_device(): pl.pallas_call(load_kernel, out_shape=blocks_of(len(far) - 1), in_specs=[...]
    unnamed x16 -> x18, local copies, waits for them, and re-layouts: 2.33 us -> 2.96 us
    ppermute x8 -> x10, starting transfers between devices: 16.9 us -> 16.5 us  [permute(): return lax.ppermute(block, 'img', [(i, i ^ step) for i in range(groups)])]
  transfers between devices with their start and end apart: 8 -> 10, of which waited for: 5 -> 3; matrix products, arithmetic and copies ran while one was open for 0% -> 0% of each run, Pallas kernels for 23% -> 33%
where the time goes in v3:
time: 60.7 us; the launch traced here: 60.5 us
  Pallas kernels  28 us (46%)
  starting transfers between devices  16.5 us (27%)
  waiting for transfers between devices  12.2 us (20%)
  local copies, waits for them, and re-layouts  2.96 us (5%)
  between operations  0.8 us (1%)
    pallas_call x8, Pallas kernels, decode(): pl.pallas_call(functools.partial(decode_kernel, parts, per_owner, patches...  22.2 us
    ppermute x10, starting transfers between devices, permute(): return lax.ppermute(block, 'img', [(i, i ^ step) for i in range(groups)])  16.5 us
    ppermute x10, waiting for transfers between devices, permute(): return lax.ppermute(block, 'img', [(i, i ^ step) for i in range(groups)])  12.2 us
    pallas_call x1, Pallas kernels, per_device(): pl.pallas_call(functools.partial(embed_kernel, groups, per_owner, patches...  4.74 us
    unnamed x18, local copies, waits for them, and re-layouts  2.96 us
  transfers between devices with their start and end apart: 10, of which 3 were waited for; matrix products, arithmetic and copies ran while one was open for 0% of the time, Pallas kernels for 33%

profile of v3, /device:TPU:0, one launch (start us, length us, event | category | flops | bytes accessed | tf_op | source)
XLA Modules:
  0.0 60.5 jit_solution(15324377790600612863)
XLA Ops:
  0.6 0.0 copy-start.5
  0.6 4.7 %embed.1 = (bf16[512,768]{1,0:T(8,128)(2,1)}, bf16[512,768]{1,0:T(8,128)(2,1)}, bf16[2480,128]{1,0:T(8,128)(2,1)}, bf16[496,128]{1,0:T(8,128)(2,1)}, bf16[1488,1...) custom-call(s32[2,64]{1,0:T(2,128)} %bitcast.19, bf16[512,1024]{1,0:T(8,128)(2,1)} %bitcast.18, ...), custom_call_target="tpu_custom_call" | custom-call | flops 1 | bytes 1 | tf_op jit(solution)/shard_map/embed/pallas_call | solution.py:250
  5.4 0.5 collective-permute-start
  5.9 0.1 collective-permute-start.4
  6.0 4.0 %collective-permute-start.1 = (bf16[496,128]{1,0:T(8,128)(2,1)}, bf16[496,128]{1,0:T(8,128)(2,1)S(1)}, u32[]{:S(2)}, u32[]{:S(2)}) collective-permute-start(bf16[496,128]{1,0:T(8,128)(2,1)} %get-tuple-element.35), channel_id=1, source_target_pairs={{0,8},{1,9},{2,10},{3,11},{4,12},{5,13},{6,14},{7,15},{8,0},{9,1},... | collective-permute-start | bytes 380936 | tf_op jit(solution)/shard_map/ppermute | solution.py:313
  10.0 0.0 copy-start.8
  10.0 1.0 %copy-done.8 = bf16[1488,128]{1,0:T(8,128)(2,1)S(1)} copy-done((bf16[1488,128]{1,0:T(8,128)(2,1)S(1)}, bf16[1488,128]{1,0:T(8,128)(2,1)}, u32[]{:S(2)}) %copy-start.8) | copy-done | bytes 380952
  11.0 0.0 copy-start.3
  11.0 0.2 load.1.refs_0_
  11.2 0.0 collective-permute-done.refs_1_.rest_0_
  11.2 0.0 copy-start.2
  11.2 0.1 join.2
  11.3 1.6 %collective-permute-start.3 = (bf16[992,128]{1,0:T(8,128)(2,1)S(1)}, bf16[992,128]{1,0:T(8,128)(2,1)S(1)}, u32[]{:S(2)}, u32[]{:S(2)}) collective-permute-start(bf16[992,128]{1,0:T(8,128)(2,1)S(1)} %get-tuple-element.38), channel_id=1, source_target_pairs={{0,10},{1,11},{2,8},{3,9},{4,14},{5,15},{6,12},{7,13},{8,2},{9,3},... | collective-permute-start | bytes 761864 | tf_op jit(solution)/shard_map/ppermute | solution.py:313
  12.9 0.0 copy-done.5
  12.9 0.0 copy-start.6
  12.9 1.1 %copy-done.6 = bf16[512,768]{1,0:T(8,128)(2,1)S(1)} copy-done((bf16[512,768]{1,0:T(8,128)(2,1)S(1)}, bf16[512,768]{1,0:T(8,128)(2,1)}, u32[]{:S(2)}) %copy-start.6) | copy-done | bytes 786456
  14.0 0.0 copy-start
  14.0 0.8 %queries.1.query_ref = bf16[512,768]{1,0:T(8,128)(2,1)S(1)} custom-call(bf16[512,768]{1,0:T(8,128)(2,1)S(1)} %copy-done.6, bf16[768,768]{1,0:T(8,128)(2,1)S(1)} %copy-done.5), custom_call_target="tpu_custom_call" | custom-call | flops 1 | bytes 1 | tf_op jit(solution)/shard_map/queries/pallas_call | solution.py:272
  14.8 0.0 copy-done.3
  14.8 0.0 copy-done.2
  14.8 0.5 copy-done
  15.3 0.4 copy-done.1
  15.6 0.0 copy-done.4
  15.6 2.3 %decode.8.rest_0_ = f32[512,28]{1,0:T(8,128)S(1)} custom-call(bf16[512,768]{1,0:T(8,128)(2,1)S(1)} %queries.1.query_ref, bf16[512,768]{1,0:T(8,128)(2,1)S(1)} %copy-done.3, bf16[768,768]{1,0:T(8,128)(2,1)S(1)} %copy-done, bf16[768,768]{1,0:T(8,128)(2,1)S(1)} %copy-done.1, bf16[768,768]{1,0:T(8,128)(2,1)S(1)} %copy-done.2, bf16[28,768]{1,0:T(8,128)(2,1)S(1)} %bitcast.10, ...), custom_call_target="tpu_custom_call" | custom-call | flops 1 | bytes 1 | tf_op jit(solution)/shard_map/decode/pallas_call | solution.py:299
  17.9 4.7 %collective-permute-done.1.rest_1_ = bf16[496,128]{1,0:T(8,128)(2,1)S(1)} collective-permute-done((bf16[496,128]{1,0:T(8,128)(2,1)}, bf16[496,128]{1,0:T(8,128)(2,1)S(1)}, u32[]{:S(2)}, u32[]{:S(2)}) %collective-permute-start.1) | collective-permute-done | bytes 127008 | tf_op jit(solution)/shard_map/ppermute | solution.py:313
  22.6 3.1 %collective-permute-start.2 = (bf16[992,128]{1,0:T(8,128)(2,1)S(1)}, bf16[992,128]{1,0:T(8,128)(2,1)S(1)}, u32[]{:S(2)}, u32[]{:S(2)}) collective-permute-start(bf16[992,128]{1,0:T(8,128)(2,1)S(1)} %get-tuple-element.36), channel_id=1, source_target_pairs={{0,12},{1,13},{2,14},{3,15},{4,8},{5,9},{6,10},{7,11},{8,4},{9,5},... | collective-permute-start | bytes 761864 | tf_op jit(solution)/shard_map/ppermute | solution.py:313
  25.7 0.0 collective-permute-done.4.refs_1_
  25.7 0.0 copy-done.7
  25.7 0.1 join.3
  25.7 1.6 %collective-permute-start.5 = (bf16[992,128]{1,0:T(8,128)(2,1)S(1)}, bf16[992,128]{1,0:T(8,128)(2,1)S(1)}, u32[]{:S(2)}, u32[]{:S(2)}) collective-permute-start(bf16[992,128]{1,0:T(8,128)(2,1)S(1)} %get-tuple-element.46), channel_id=1, source_target_pairs={{0,2},{1,3},{2,0},{3,1},{4,6},{5,7},{6,4},{7,5},{8,10},{9,11},{10,... | collective-permute-start | bytes 761864 | tf_op jit(solution)/shard_map/ppermute | solution.py:313
  27.3 0.0 collective-permute-start.6
  27.3 2.0 %collective-permute-start.7 = (bf16[992,128]{1,0:T(8,128)(2,1)S(1)}, bf16[992,128]{1,0:T(8,128)(2,1)S(1)}, u32[]{:S(2)}, u32[]{:S(2)}) collective-permute-start(bf16[992,128]{1,0:T(8,128)(2,1)S(1)} %get-tuple-element.48), channel_id=1, source_target_pairs={{0,6},{1,7},{2,4},{3,5},{4,2},{5,3},{6,0},{7,1},{8,14},{9,15},{10,... | collective-permute-start | bytes 761864 | tf_op jit(solution)/shard_map/ppermute | solution.py:313
  29.3 2.3 %decode.9.rest_0_ = f32[512,28]{1,0:T(8,128)S(1)} custom-call(bf16[512,768]{1,0:T(8,128)(2,1)S(1)} %queries.1.query_ref, bf16[512,768]{1,0:T(8,128)(2,1)S(1)} %copy-done.3, bf16[768,768]{1,0:T(8,128)(2,1)S(1)} %copy-done, bf16[768,768]{1,0:T(8,128)(2,1)S(1)} %copy-done.1, bf16[768,768]{1,0:T(8,128)(2,1)S(1)} %copy-done.2, bf16[28,768]{1,0:T(8,128)(2,1)S(1)} %bitcast.11, ...), custom_call_target="tpu_custom_call" | custom-call | flops 1 | bytes 1 | tf_op jit(solution)/shard_map/decode/pallas_call | solution.py:299
  31.5 3.3 %collective-permute-done.3.rest_1_ = bf16[992,128]{1,0:T(8,128)(2,1)S(1)} collective-permute-done((bf16[992,128]{1,0:T(8,128)(2,1)S(1)}, bf16[992,128]{1,0:T(8,128)(2,1)S(1)}, u32[]{:S(2)}, u32[]{:S(2)}) %collective-permute-start.3) | collective-permute-done | bytes 253984 | tf_op jit(solution)/shard_map/ppermute | solution.py:313
  34.8 2.6 %collective-permute-start.8 = (bf16[992,128]{1,0:T(8,128)(2,1)S(1)}, bf16[992,128]{1,0:T(8,128)(2,1)S(1)}, u32[]{:S(2)}, u32[]{:S(2)}) collective-permute-start(bf16[992,128]{1,0:T(8,128)(2,1)S(1)} %get-tuple-element.50), channel_id=1, source_target_pairs={{0,14},{1,15},{2,12},{3,13},{4,10},{5,11},{6,8},{7,9},{8,6},{9,7},... | collective-permute-start | bytes 761864 | tf_op jit(solution)/shard_map/ppermute | solution.py:313
  37.5 2.6 %decode.10.rest_0_ = f32[512,28]{1,0:T(8,128)S(1)} custom-call(bf16[512,768]{1,0:T(8,128)(2,1)S(1)} %queries.1.query_ref, bf16[512,768]{1,0:T(8,128)(2,1)S(1)} %copy-done.3, bf16[768,768]{1,0:T(8,128)(2,1)S(1)} %copy-done, bf16[768,768]{1,0:T(8,128)(2,1)S(1)} %copy-done.1, bf16[768,768]{1,0:T(8,128)(2,1)S(1)} %copy-done.2, bf16[28,768]{1,0:T(8,128)(2,1)S(1)} %bitcast.12, ...), custom_call_target="tpu_custom_call" | custom-call | flops 1 | bytes 1 | tf_op jit(solution)/shard_map/decode/pallas_call | solution.py:299
  40.1 0.0 collective-permute-done.2.rest_1_
  40.1 1.0 %collective-permute-start.9 = (bf16[496,128]{1,0:T(8,128)(2,1)S(1)}, bf16[496,128]{1,0:T(8,128)(2,1)S(1)}, u32[]{:S(2)}, u32[]{:S(2)}) collective-permute-start(bf16[496,128]{1,0:T(8,128)(2,1)S(1)} %get-tuple-element.51), channel_id=1, source_target_pairs={{0,8},{1,9},{2,10},{3,11},{4,12},{5,13},{6,14},{7,15},{8,0},{9,1},... | collective-permute-start | bytes 380936 | tf_op jit(solution)/shard_map/ppermute | solution.py:313
  41.1 0.0 collective-permute-done.5.rest_1_
  41.1 0.0 collective-permute-done.6.rest_2_
  41.1 4.0 %decode.11.rest_0_ = f32[512,28]{1,0:T(8,128)S(1)} custom-call(bf16[512,768]{1,0:T(8,128)(2,1)S(1)} %queries.1.query_ref, bf16[512,768]{1,0:T(8,128)(2,1)S(1)} %copy-done.3, bf16[768,768]{1,0:T(8,128)(2,1)S(1)} %copy-done, bf16[768,768]{1,0:T(8,128)(2,1)S(1)} %copy-done.1, bf16[768,768]{1,0:T(8,128)(2,1)S(1)} %copy-done.2, bf16[28,768]{1,0:T(8,128)(2,1)S(1)} %bitcast.13, ...), custom_call_target="tpu_custom_call" | custom-call | flops 1 | bytes 1 | tf_op jit(solution)/shard_map/decode/pallas_call | solution.py:299
  45.1 4.2 %collective-permute-done.7.rest_1_ = bf16[992,128]{1,0:T(8,128)(2,1)S(1)} collective-permute-done((bf16[992,128]{1,0:T(8,128)(2,1)S(1)}, bf16[992,128]{1,0:T(8,128)(2,1)S(1)}, u32[]{:S(2)}, u32[]{:S(2)}) %collective-permute-start.7) | collective-permute-done | bytes 253984 | tf_op jit(solution)/shard_map/ppermute | solution.py:313
  49.4 2.6 %decode.12.rest_0_ = f32[512,28]{1,0:T(8,128)S(1)} custom-call(bf16[512,768]{1,0:T(8,128)(2,1)S(1)} %queries.1.query_ref, bf16[512,768]{1,0:T(8,128)(2,1)S(1)} %copy-done.3, bf16[768,768]{1,0:T(8,128)(2,1)S(1)} %copy-done, bf16[768,768]{1,0:T(8,128)(2,1)S(1)} %copy-done.1, bf16[768,768]{1,0:T(8,128)(2,1)S(1)} %copy-done.2, bf16[28,768]{1,0:T(8,128)(2,1)S(1)} %bitcast.14, ...), custom_call_target="tpu_custom_call" | custom-call | flops 1 | bytes 1 | tf_op jit(solution)/shard_map/decode/pallas_call | solution.py:299
  52.0 2.6 %decode.13.rest_0_ = f32[512,28]{1,0:T(8,128)S(1)} custom-call(bf16[512,768]{1,0:T(8,128)(2,1)S(1)} %queries.1.query_ref, bf16[512,768]{1,0:T(8,128)(2,1)S(1)} %copy-done.3, bf16[768,768]{1,0:T(8,128)(2,1)S(1)} %copy-done, bf16[768,768]{1,0:T(8,128)(2,1)S(1)} %copy-done.1, bf16[768,768]{1,0:T(8,128)(2,1)S(1)} %copy-done.2, bf16[28,768]{1,0:T(8,128)(2,1)S(1)} %bitcast.15, ...), custom_call_target="tpu_custom_call" | custom-call | flops 1 | bytes 1 | tf_op jit(solution)/shard_map/decode/pallas_call | solution.py:299
  54.7 0.0 collective-permute-done.8.rest_1_
  54.7 2.6 %decode.14.rest_0_ = f32[512,28]{1,0:T(8,128)S(1)} custom-call(bf16[512,768]{1,0:T(8,128)(2,1)S(1)} %queries.1.query_ref, bf16[512,768]{1,0:T(8,128)(2,1)S(1)} %copy-done.3, bf16[768,768]{1,0:T(8,128)(2,1)S(1)} %copy-done, bf16[768,768]{1,0:T(8,128)(2,1)S(1)} %copy-done.1, bf16[768,768]{1,0:T(8,128)(2,1)S(1)} %copy-done.2, bf16[28,768]{1,0:T(8,128)(2,1)S(1)} %bitcast.16, ...), custom_call_target="tpu_custom_call" | custom-call | flops 1 | bytes 1 | tf_op jit(solution)/shard_map/decode/pallas_call | solution.py:299
  57.3 0.0 collective-permute-done.9.rest_1_
  57.3 3.2 %decode.15 = (f32[48,32]{1,0:T(8,128)}, f32[384,32]{1,0:T(8,128)}, f32[16,32]{1,0:T(8,128)}) custom-call(bf16[512,768]{1,0:T(8,128)(2,1)S(1)} %queries.1.query_ref, bf16[512,768]{1,0:T(8,128)(2,1)S(1)} %copy-done.3, bf16[768,768]{1,0:T(8,128)(2,1)S(1)} %copy-done, bf16[768,768]{1,0:T(8,128)(2,1)S(1)} %copy-done.1, bf16[768,768]{1,0:T(8,128)(2,1)S(1)} %copy-done.2, ...), custom_call_target="tpu_custom_call" | custom-call | flops 1 | bytes 1 | tf_op jit(solution)/shard_map/decode/pallas_call | solution.py:299
  (3 shorter events, 0.0 us)
Async XLA Ops:
  0.6 12.2 %copy-start.5 = (bf16[768,768]{1,0:T(8,128)(2,1)S(1)}, bf16[768,768]{1,0:T(8,128)(2,1)}, u32[]{:S(2)}) copy-start(bf16[768,768]{1,0:T(8,128)(2,1)} %w_ref.1) | copy-start | bytes 3538948
  5.4 5.8 %collective-permute-start = (bf16[2480,128]{1,0:T(8,128)(2,1)}, bf16[2480,128]{1,0:T(8,128)(2,1)S(1)}, u32[]{:S(2)}, u32[]{:S(2)}) collective-permute-start(bf16[2480,128]{1,0:T(8,128)(2,1)} %get-tuple-element.32), channel_id=1, source_target_pairs={{0,1},{1,0},{2,3},{3,2},{4,5},{5,4},{6,7},{7,6},{8,9},{9,8},{10,11... | collective-permute-start | bytes 1904648 | tf_op jit(solution)/shard_map/ppermute | solution.py:313
  5.9 19.7 %collective-permute-start.4 = (bf16[1488,128]{1,0:T(8,128)(2,1)}, bf16[1488,128]{1,0:T(8,128)(2,1)S(1)}, u32[]{:S(2)}, u32[]{:S(2)}) collective-permute-start(bf16[1488,128]{1,0:T(8,128)(2,1)} %get-tuple-element.45), channel_id=1, source_target_pairs={{0,1},{1,0},{2,3},{3,2},{4,5},{5,4},{6,7},{7,6},{8,9},{9,8},{10,11... | collective-permute-start | bytes 1142792 | tf_op jit(solution)/shard_map/ppermute | solution.py:313
  6.0 16.6 %collective-permute-start.1 = (bf16[496,128]{1,0:T(8,128)(2,1)}, bf16[496,128]{1,0:T(8,128)(2,1)S(1)}, u32[]{:S(2)}, u32[]{:S(2)}) collective-permute-start(bf16[496,128]{1,0:T(8,128)(2,1)} %get-tuple-element.35), channel_id=1, source_target_pairs={{0,8},{1,9},{2,10},{3,11},{4,12},{5,13},{6,14},{7,15},{8,0},{9,1},... | collective-permute-start | bytes 380936 | tf_op jit(solution)/shard_map/ppermute | solution.py:313
  10.0 1.0 %copy-start.8 = (bf16[1488,128]{1,0:T(8,128)(2,1)S(1)}, bf16[1488,128]{1,0:T(8,128)(2,1)}, u32[]{:S(2)}) copy-start(bf16[1488,128]{1,0:T(8,128)(2,1)} %get-tuple-element.31.from_ref) | copy-start | bytes 1142788
  11.0 3.8 %copy-start.3 = (bf16[512,768]{1,0:T(8,128)(2,1)S(1)}, bf16[512,768]{1,0:T(8,128)(2,1)}, u32[]{:S(2)}) copy-start(bf16[512,768]{1,0:T(8,128)(2,1)} %get-tuple-element.30.emb_ref) | copy-start | bytes 2359300
  11.2 3.6 %copy-start.2 = (bf16[768,768]{1,0:T(8,128)(2,1)S(1)}, bf16[768,768]{1,0:T(8,128)(2,1)}, u32[]{:S(2)}) copy-start(bf16[768,768]{1,0:T(8,128)(2,1)} %wo_ref.15) | copy-start | bytes 3538948
  11.3 23.6 %collective-permute-start.3 = (bf16[992,128]{1,0:T(8,128)(2,1)S(1)}, bf16[992,128]{1,0:T(8,128)(2,1)S(1)}, u32[]{:S(2)}, u32[]{:S(2)}) collective-permute-start(bf16[992,128]{1,0:T(8,128)(2,1)S(1)} %get-tuple-element.38), channel_id=1, source_target_pairs={{0,10},{1,11},{2,8},{3,9},{4,14},{5,15},{6,12},{7,13},{8,2},{9,3},... | collective-permute-start | bytes 761864 | tf_op jit(solution)/shard_map/ppermute | solution.py:313
  12.9 1.1 %copy-start.6 = (bf16[512,768]{1,0:T(8,128)(2,1)S(1)}, bf16[512,768]{1,0:T(8,128)(2,1)}, u32[]{:S(2)}) copy-start(bf16[512,768]{1,0:T(8,128)(2,1)} %get-tuple-element.29.normed_ref) | copy-start | bytes 2359300
  14.0 1.3 %copy-start = (bf16[768,768]{1,0:T(8,128)(2,1)S(1)}, bf16[768,768]{1,0:T(8,128)(2,1)}, u32[]{:S(2)}) copy-start(bf16[768,768]{1,0:T(8,128)(2,1)} %wk_ref.15) | copy-start | bytes 3538948
  14.0 1.6 %copy-start.1 = (bf16[768,768]{1,0:T(8,128)(2,1)S(1)}, bf16[768,768]{1,0:T(8,128)(2,1)}, u32[]{:S(2)}) copy-start(bf16[768,768]{1,0:T(8,128)(2,1)} %wv_ref.15) | copy-start | bytes 3538948
  14.0 1.6 %copy-start.4 = (bf16[768,28]{0,1:T(8,128)(2,1)S(1)}, bf16[768,28]{0,1:T(8,128)(2,1)}, u32[]{:S(2)}) copy-start(bf16[768,28]{0,1:T(8,128)(2,1)} %param.15) | copy-start | bytes 129028
  15.6 10.0 %copy-start.7 = (bf16[1488,128]{1,0:T(8,128)(2,1)S(1)}, bf16[1488,128]{1,0:T(8,128)(2,1)}, u32[]{:S(2)}) copy-start(bf16[1488,128]{1,0:T(8,128)(2,1)} %get-tuple-element.44.refs_0_) | copy-start | bytes 1142788
  22.6 17.5 %collective-permute-start.2 = (bf16[992,128]{1,0:T(8,128)(2,1)S(1)}, bf16[992,128]{1,0:T(8,128)(2,1)S(1)}, u32[]{:S(2)}, u32[]{:S(2)}) collective-permute-start(bf16[992,128]{1,0:T(8,128)(2,1)S(1)} %get-tuple-element.36), channel_id=1, source_target_pairs={{0,12},{1,13},{2,14},{3,15},{4,8},{5,9},{6,10},{7,11},{8,4},{9,5},... | collective-permute-start | bytes 761864 | tf_op jit(solution)/shard_map/ppermute | solution.py:313
  25.7 15.4 %collective-permute-start.5 = (bf16[992,128]{1,0:T(8,128)(2,1)S(1)}, bf16[992,128]{1,0:T(8,128)(2,1)S(1)}, u32[]{:S(2)}, u32[]{:S(2)}) collective-permute-start(bf16[992,128]{1,0:T(8,128)(2,1)S(1)} %get-tuple-element.46), channel_id=1, source_target_pairs={{0,2},{1,3},{2,0},{3,1},{4,6},{5,7},{6,4},{7,5},{8,10},{9,11},{10,... | collective-permute-start | bytes 761864 | tf_op jit(solution)/shard_map/ppermute | solution.py:313
  27.3 13.8 %collective-permute-start.6 = (bf16[992,128]{1,0:T(8,128)(2,1)S(1)}, bf16[992,128]{1,0:T(8,128)(2,1)S(1)}, u32[]{:S(2)}, u32[]{:S(2)}) collective-permute-start(bf16[992,128]{1,0:T(8,128)(2,1)S(1)} %get-tuple-element.47), channel_id=1, source_target_pairs={{0,4},{1,5},{2,6},{3,7},{4,0},{5,1},{6,2},{7,3},{8,12},{9,13},{10,... | collective-permute-start | bytes 761864 | tf_op jit(solution)/shard_map/ppermute | solution.py:313
  27.3 22.1 %collective-permute-start.7 = (bf16[992,128]{1,0:T(8,128)(2,1)S(1)}, bf16[992,128]{1,0:T(8,128)(2,1)S(1)}, u32[]{:S(2)}, u32[]{:S(2)}) collective-permute-start(bf16[992,128]{1,0:T(8,128)(2,1)S(1)} %get-tuple-element.48), channel_id=1, source_target_pairs={{0,6},{1,7},{2,4},{3,5},{4,2},{5,3},{6,0},{7,1},{8,14},{9,15},{10,... | collective-permute-start | bytes 761864 | tf_op jit(solution)/shard_map/ppermute | solution.py:313
  34.8 19.8 %collective-permute-start.8 = (bf16[992,128]{1,0:T(8,128)(2,1)S(1)}, bf16[992,128]{1,0:T(8,128)(2,1)S(1)}, u32[]{:S(2)}, u32[]{:S(2)}) collective-permute-start(bf16[992,128]{1,0:T(8,128)(2,1)S(1)} %get-tuple-element.50), channel_id=1, source_target_pairs={{0,14},{1,15},{2,12},{3,13},{4,10},{5,11},{6,8},{7,9},{8,6},{9,7},... | collective-permute-start | bytes 761864 | tf_op jit(solution)/shard_map/ppermute | solution.py:313
  40.1 17.2 %collective-permute-start.9 = (bf16[496,128]{1,0:T(8,128)(2,1)S(1)}, bf16[496,128]{1,0:T(8,128)(2,1)S(1)}, u32[]{:S(2)}, u32[]{:S(2)}) collective-permute-start(bf16[496,128]{1,0:T(8,128)(2,1)S(1)} %get-tuple-element.51), channel_id=1, source_target_pairs={{0,8},{1,9},{2,10},{3,11},{4,12},{5,13},{6,14},{7,15},{8,0},{9,1},... | collective-permute-start | bytes 380936 | tf_op jit(solution)/shard_map/ppermute | solution.py:313

commit v4 on v3

--- a/solution.py
+++ b/solution.py
@@ -349,8 +349,11 @@
         both.update(zip(near, join(sends[4], mate_near, [2] * len(near), copies)))
 
         got = {far[1]: permute(both[far[1]], 2 * far[1])}
-        for t in near:
-            got[t] = permute(both[t], 2 * t)
+        for n, t in enumerate(near):
+            block = both[t]
+            if n > 1:
+                block, got[near[n - 2]] = lax.optimization_barrier((block, got[near[n - 2]]))
+            got[t] = permute(block, 2 * t)
         totals = decode([mate_far], [(0, 0)], None, False)
         block, first, totals = lax.optimization_barrier((both[far[2]], first, totals))
         got[far[2]] = permute(block, 2 * far[2])
@@ -361,7 +364,7 @@
         totals = decode([got[far[1]]], [(0, 0), (0, 1)], totals, False)
         late, got[far[-2]], totals = lax.optimization_barrier((late, got[far[-2]], totals))
         last = permute(late, 2 * far[0])
-        plan = [near[:2], near[2:]] + [[t] for t in far[2:]]
+        plan = [near[:2], far[2:3], near[2:]] + [[t] for t in far[3:]]
         for pair in plan:
             parts = [(n, m) for n in range(len(pair)) for m in (0, 1)]
             totals = decode([got[t] for t in pair], parts, totals, False)

time: 60.7 us -> 59.2 us (0.975)
  waiting for transfers between devices: 12.2 us -> 10.6 us
    ppermute x10, waiting for transfers between devices: 12.2 us -> 10.6 us  [permute(): return lax.ppermute(block, 'img', [(i, i ^ step) for i in range(groups)])]
  transfers between devices with their start and end apart: 10 -> 10, of which waited for: 3 -> 2; matrix products, arithmetic and copies ran while one was open for 0% -> 0% of each run, Pallas kernels for 33% -> 34%
where the time goes in v4:
time: 59.2 us; the launch traced here: 59 us
  Pallas kernels  28 us (47%)
  starting transfers between devices  16.7 us (28%)
  waiting for transfers between devices  10.6 us (18%)
  local copies, waits for them, and re-layouts  2.81 us (5%)
  between operations  0.83 us (1%)
    pallas_call x8, Pallas kernels, decode(): pl.pallas_call(functools.partial(decode_kernel, parts, per_owner, patches...  22.2 us
    ppermute x10, starting transfers between devices, permute(): return lax.ppermute(block, 'img', [(i, i ^ step) for i in range(groups)])  16.7 us
    ppermute x10, waiting for transfers between devices, permute(): return lax.ppermute(block, 'img', [(i, i ^ step) for i in range(groups)])  10.6 us
    pallas_call x1, Pallas kernels, per_device(): pl.pallas_call(functools.partial(embed_kernel, groups, per_owner, patches...  4.74 us
    unnamed x18, local copies, waits for them, and re-layouts  2.81 us
  transfers between devices with their start and end apart: 10, of which 2 were waited for; matrix products, arithmetic and copies ran while one was open for 0% of the time, Pallas kernels for 34%

profile of v4, /device:TPU:0, one launch (start us, length us, event | category | flops | bytes accessed | tf_op | source)
XLA Modules:
  0.0 59.0 jit_solution(17723194377015380624)
XLA Ops:
  0.6 0.0 copy-start.5
  0.6 4.7 %embed.1 = (bf16[512,768]{1,0:T(8,128)(2,1)}, bf16[512,768]{1,0:T(8,128)(2,1)}, bf16[2480,128]{1,0:T(8,128)(2,1)}, bf16[496,128]{1,0:T(8,128)(2,1)}, bf16[1488,1...) custom-call(s32[2,64]{1,0:T(2,128)} %bitcast.19, bf16[512,1024]{1,0:T(8,128)(2,1)} %bitcast.18, ...), custom_call_target="tpu_custom_call" | custom-call | flops 1 | bytes 1 | tf_op jit(solution)/shard_map/embed/pallas_call | solution.py:250
  5.4 0.5 collective-permute-start
  5.9 0.1 collective-permute-start.4
  6.0 4.0 %collective-permute-start.1 = (bf16[496,128]{1,0:T(8,128)(2,1)}, bf16[496,128]{1,0:T(8,128)(2,1)S(1)}, u32[]{:S(2)}, u32[]{:S(2)}) collective-permute-start(bf16[496,128]{1,0:T(8,128)(2,1)} %get-tuple-element.37), channel_id=1, source_target_pairs={{0,8},{1,9},{2,10},{3,11},{4,12},{5,13},{6,14},{7,15},{8,0},{9,1},... | collective-permute-start | bytes 380936 | tf_op jit(solution)/shard_map/ppermute | solution.py:313
  10.0 0.0 collective-permute-done.4.refs_1_
  10.0 0.0 copy-start.8
  10.0 1.0 %copy-done.8 = bf16[1488,128]{1,0:T(8,128)(2,1)S(1)} copy-done((bf16[1488,128]{1,0:T(8,128)(2,1)S(1)}, bf16[1488,128]{1,0:T(8,128)(2,1)}, u32[]{:S(2)}) %copy-start.8) | copy-done | bytes 380952
  11.0 0.0 copy-start.6
  11.0 0.1 join.3
  11.1 1.6 %collective-permute-start.5 = (bf16[992,128]{1,0:T(8,128)(2,1)S(1)}, bf16[992,128]{1,0:T(8,128)(2,1)S(1)}, u32[]{:S(2)}, u32[]{:S(2)}) collective-permute-start(bf16[992,128]{1,0:T(8,128)(2,1)S(1)} %get-tuple-element.49), channel_id=1, source_target_pairs={{0,2},{1,3},{2,0},{3,1},{4,6},{5,7},{6,4},{7,5},{8,10},{9,11},{10,... | collective-permute-start | bytes 761864 | tf_op jit(solution)/shard_map/ppermute | solution.py:313
  12.6 0.0 copy-start.7
  12.6 1.0 %copy-done.7 = bf16[1488,128]{1,0:T(8,128)(2,1)S(1)} copy-done((bf16[1488,128]{1,0:T(8,128)(2,1)S(1)}, bf16[1488,128]{1,0:T(8,128)(2,1)}, u32[]{:S(2)}) %copy-start.7) | copy-done | bytes 380952
  13.6 0.2 load.1.refs_0_
  13.8 0.0 collective-permute-done.refs_1_.rest_0_
  13.8 0.0 copy-start.2
  13.8 0.1 join.2
  13.9 2.3 %collective-permute-start.3 = (bf16[992,128]{1,0:T(8,128)(2,1)S(1)}, bf16[992,128]{1,0:T(8,128)(2,1)S(1)}, u32[]{:S(2)}, u32[]{:S(2)}) collective-permute-start(bf16[992,128]{1,0:T(8,128)(2,1)S(1)} %get-tuple-element.40), channel_id=1, source_target_pairs={{0,10},{1,11},{2,8},{3,9},{4,14},{5,15},{6,12},{7,13},{8,2},{9,3},... | collective-permute-start | bytes 761864 | tf_op jit(solution)/shard_map/ppermute | solution.py:313
  16.2 0.0 copy-done.5
  16.2 0.0 copy-done.6
  16.2 0.0 copy-start.4
  16.3 0.8 %queries.1.query_ref = bf16[512,768]{1,0:T(8,128)(2,1)S(1)} custom-call(bf16[512,768]{1,0:T(8,128)(2,1)S(1)} %copy-done.6, bf16[768,768]{1,0:T(8,128)(2,1)S(1)} %copy-done.5), custom_call_target="tpu_custom_call" | custom-call | flops 1 | bytes 1 | tf_op jit(solution)/shard_map/queries/pallas_call | solution.py:272
  17.0 0.0 copy-done.3
  17.1 0.0 copy-done.2
  17.1 0.4 copy-done
  17.5 0.4 copy-done.1
  17.9 0.0 copy-done.4
  17.9 2.3 %decode.8.rest_0_ = f32[512,28]{1,0:T(8,128)S(1)} custom-call(bf16[512,768]{1,0:T(8,128)(2,1)S(1)} %queries.1.query_ref, bf16[512,768]{1,0:T(8,128)(2,1)S(1)} %copy-done.3, bf16[768,768]{1,0:T(8,128)(2,1)S(1)} %copy-done, bf16[768,768]{1,0:T(8,128)(2,1)S(1)} %copy-done.1, bf16[768,768]{1,0:T(8,128)(2,1)S(1)} %copy-done.2, bf16[28,768]{1,0:T(8,128)(2,1)S(1)} %bitcast.10, ...), custom_call_target="tpu_custom_call" | custom-call | flops 1 | bytes 1 | tf_op jit(solution)/shard_map/decode/pallas_call | solution.py:299
  20.1 0.0 collective-permute-done.1.rest_1_
  20.1 1.8 %collective-permute-start.2 = (bf16[992,128]{1,0:T(8,128)(2,1)S(1)}, bf16[992,128]{1,0:T(8,128)(2,1)S(1)}, u32[]{:S(2)}, u32[]{:S(2)}) collective-permute-start(bf16[992,128]{1,0:T(8,128)(2,1)S(1)} %get-tuple-element.38), channel_id=1, source_target_pairs={{0,12},{1,13},{2,14},{3,15},{4,8},{5,9},{6,10},{7,11},{8,4},{9,5},... | collective-permute-start | bytes 761864 | tf_op jit(solution)/shard_map/ppermute | solution.py:313
  22.0 0.0 collective-permute-start.6
  22.0 2.3 %decode.9.rest_0_ = f32[512,28]{1,0:T(8,128)S(1)} custom-call(bf16[512,768]{1,0:T(8,128)(2,1)S(1)} %queries.1.query_ref, bf16[512,768]{1,0:T(8,128)(2,1)S(1)} %copy-done.3, bf16[768,768]{1,0:T(8,128)(2,1)S(1)} %copy-done, bf16[768,768]{1,0:T(8,128)(2,1)S(1)} %copy-done.1, bf16[768,768]{1,0:T(8,128)(2,1)S(1)} %copy-done.2, bf16[28,768]{1,0:T(8,128)(2,1)S(1)} %bitcast.11, ...), custom_call_target="tpu_custom_call" | custom-call | flops 1 | bytes 1 | tf_op jit(solution)/shard_map/decode/pallas_call | solution.py:299
  24.3 0.0 collective-permute-done.5.rest_1_
  24.3 2.9 %collective-permute-start.7 = (bf16[992,128]{1,0:T(8,128)(2,1)S(1)}, bf16[992,128]{1,0:T(8,128)(2,1)S(1)}, u32[]{:S(2)}, u32[]{:S(2)}) collective-permute-start(bf16[992,128]{1,0:T(8,128)(2,1)S(1)} %get-tuple-element.53), channel_id=1, source_target_pairs={{0,6},{1,7},{2,4},{3,5},{4,2},{5,3},{6,0},{7,1},{8,14},{9,15},{10,... | collective-permute-start | bytes 761864 | tf_op jit(solution)/shard_map/ppermute | solution.py:313
  27.2 8.3 %collective-permute-done.3.rest_1_ = bf16[992,128]{1,0:T(8,128)(2,1)S(1)} collective-permute-done((bf16[992,128]{1,0:T(8,128)(2,1)S(1)}, bf16[992,128]{1,0:T(8,128)(2,1)S(1)}, u32[]{:S(2)}, u32[]{:S(2)}) %collective-permute-start.3) | collective-permute-done | bytes 253984 | tf_op jit(solution)/shard_map/ppermute | solution.py:313
  35.5 2.4 %collective-permute-start.8 = (bf16[992,128]{1,0:T(8,128)(2,1)S(1)}, bf16[992,128]{1,0:T(8,128)(2,1)S(1)}, u32[]{:S(2)}, u32[]{:S(2)}) collective-permute-start(bf16[992,128]{1,0:T(8,128)(2,1)S(1)} %get-tuple-element.54), channel_id=1, source_target_pairs={{0,14},{1,15},{2,12},{3,13},{4,10},{5,11},{6,8},{7,9},{8,6},{9,7},... | collective-permute-start | bytes 761864 | tf_op jit(solution)/shard_map/ppermute | solution.py:313
  37.8 2.6 %decode.10.rest_0_ = f32[512,28]{1,0:T(8,128)S(1)} custom-call(bf16[512,768]{1,0:T(8,128)(2,1)S(1)} %queries.1.query_ref, bf16[512,768]{1,0:T(8,128)(2,1)S(1)} %copy-done.3, bf16[768,768]{1,0:T(8,128)(2,1)S(1)} %copy-done, bf16[768,768]{1,0:T(8,128)(2,1)S(1)} %copy-done.1, bf16[768,768]{1,0:T(8,128)(2,1)S(1)} %copy-done.2, bf16[28,768]{1,0:T(8,128)(2,1)S(1)} %bitcast.12, ...), custom_call_target="tpu_custom_call" | custom-call | flops 1 | bytes 1 | tf_op jit(solution)/shard_map/decode/pallas_call | solution.py:299
  40.5 0.0 collective-permute-done.2.rest_1_
  40.5 1.1 %collective-permute-start.9 = (bf16[496,128]{1,0:T(8,128)(2,1)S(1)}, bf16[496,128]{1,0:T(8,128)(2,1)S(1)}, u32[]{:S(2)}, u32[]{:S(2)}) collective-permute-start(bf16[496,128]{1,0:T(8,128)(2,1)S(1)} %get-tuple-element.55), channel_id=1, source_target_pairs={{0,8},{1,9},{2,10},{3,11},{4,12},{5,13},{6,14},{7,15},{8,0},{9,1},... | collective-permute-start | bytes 380936 | tf_op jit(solution)/shard_map/ppermute | solution.py:313
  41.6 0.0 collective-permute-done.6.rest_2_
  41.6 4.0 %decode.11.rest_0_ = f32[512,28]{1,0:T(8,128)S(1)} custom-call(bf16[512,768]{1,0:T(8,128)(2,1)S(1)} %queries.1.query_ref, bf16[512,768]{1,0:T(8,128)(2,1)S(1)} %copy-done.3, bf16[768,768]{1,0:T(8,128)(2,1)S(1)} %copy-done, bf16[768,768]{1,0:T(8,128)(2,1)S(1)} %copy-done.1, bf16[768,768]{1,0:T(8,128)(2,1)S(1)} %copy-done.2, bf16[28,768]{1,0:T(8,128)(2,1)S(1)} %bitcast.13, ...), custom_call_target="tpu_custom_call" | custom-call | flops 1 | bytes 1 | tf_op jit(solution)/shard_map/decode/pallas_call | solution.py:299
  45.6 2.6 %decode.12.rest_0_ = f32[512,28]{1,0:T(8,128)S(1)} custom-call(bf16[512,768]{1,0:T(8,128)(2,1)S(1)} %queries.1.query_ref, bf16[512,768]{1,0:T(8,128)(2,1)S(1)} %copy-done.3, bf16[768,768]{1,0:T(8,128)(2,1)S(1)} %copy-done, bf16[768,768]{1,0:T(8,128)(2,1)S(1)} %copy-done.1, bf16[768,768]{1,0:T(8,128)(2,1)S(1)} %copy-done.2, bf16[28,768]{1,0:T(8,128)(2,1)S(1)} %bitcast.14, ...), custom_call_target="tpu_custom_call" | custom-call | flops 1 | bytes 1 | tf_op jit(solution)/shard_map/decode/pallas_call | solution.py:299
  48.3 2.3 %collective-permute-done.7.rest_1_ = bf16[992,128]{1,0:T(8,128)(2,1)S(1)} collective-permute-done((bf16[992,128]{1,0:T(8,128)(2,1)S(1)}, bf16[992,128]{1,0:T(8,128)(2,1)S(1)}, u32[]{:S(2)}, u32[]{:S(2)}) %collective-permute-start.7) | collective-permute-done | bytes 253984 | tf_op jit(solution)/shard_map/ppermute | solution.py:313
  50.5 2.6 %decode.13.rest_0_ = f32[512,28]{1,0:T(8,128)S(1)} custom-call(bf16[512,768]{1,0:T(8,128)(2,1)S(1)} %queries.1.query_ref, bf16[512,768]{1,0:T(8,128)(2,1)S(1)} %copy-done.3, bf16[768,768]{1,0:T(8,128)(2,1)S(1)} %copy-done, bf16[768,768]{1,0:T(8,128)(2,1)S(1)} %copy-done.1, bf16[768,768]{1,0:T(8,128)(2,1)S(1)} %copy-done.2, bf16[28,768]{1,0:T(8,128)(2,1)S(1)} %bitcast.15, ...), custom_call_target="tpu_custom_call" | custom-call | flops 1 | bytes 1 | tf_op jit(solution)/shard_map/decode/pallas_call | solution.py:299
  53.2 0.0 collective-permute-done.8.rest_1_
  53.2 2.6 %decode.14.rest_0_ = f32[512,28]{1,0:T(8,128)S(1)} custom-call(bf16[512,768]{1,0:T(8,128)(2,1)S(1)} %queries.1.query_ref, bf16[512,768]{1,0:T(8,128)(2,1)S(1)} %copy-done.3, bf16[768,768]{1,0:T(8,128)(2,1)S(1)} %copy-done, bf16[768,768]{1,0:T(8,128)(2,1)S(1)} %copy-done.1, bf16[768,768]{1,0:T(8,128)(2,1)S(1)} %copy-done.2, bf16[28,768]{1,0:T(8,128)(2,1)S(1)} %bitcast.16, ...), custom_call_target="tpu_custom_call" | custom-call | flops 1 | bytes 1 | tf_op jit(solution)/shard_map/decode/pallas_call | solution.py:299
  55.8 0.0 collective-permute-done.9.rest_1_
  55.9 3.2 %decode.15 = (f32[48,32]{1,0:T(8,128)}, f32[384,32]{1,0:T(8,128)}, f32[16,32]{1,0:T(8,128)}) custom-call(bf16[512,768]{1,0:T(8,128)(2,1)S(1)} %queries.1.query_ref, bf16[512,768]{1,0:T(8,128)(2,1)S(1)} %copy-done.3, bf16[768,768]{1,0:T(8,128)(2,1)S(1)} %copy-done, bf16[768,768]{1,0:T(8,128)(2,1)S(1)} %copy-done.1, bf16[768,768]{1,0:T(8,128)(2,1)S(1)} %copy-done.2, ...), custom_call_target="tpu_custom_call" | custom-call | flops 1 | bytes 1 | tf_op jit(solution)/shard_map/decode/pallas_call | solution.py:299
  (3 shorter events, 0.0 us)
Async XLA Ops:
  0.6 15.6 %copy-start.5 = (bf16[768,768]{1,0:T(8,128)(2,1)S(1)}, bf16[768,768]{1,0:T(8,128)(2,1)}, u32[]{:S(2)}) copy-start(bf16[768,768]{1,0:T(8,128)(2,1)} %w_ref.1) | copy-start | bytes 3538948
  5.4 8.4 %collective-permute-start = (bf16[2480,128]{1,0:T(8,128)(2,1)}, bf16[2480,128]{1,0:T(8,128)(2,1)S(1)}, u32[]{:S(2)}, u32[]{:S(2)}) collective-permute-start(bf16[2480,128]{1,0:T(8,128)(2,1)} %get-tuple-element.34), channel_id=1, source_target_pairs={{0,1},{1,0},{2,3},{3,2},{4,5},{5,4},{6,7},{7,6},{8,9},{9,8},{10,11... | collective-permute-start | bytes 1904648 | tf_op jit(solution)/shard_map/ppermute | solution.py:313
  5.9 4.1 %collective-permute-start.4 = (bf16[1488,128]{1,0:T(8,128)(2,1)}, bf16[1488,128]{1,0:T(8,128)(2,1)S(1)}, u32[]{:S(2)}, u32[]{:S(2)}) collective-permute-start(bf16[1488,128]{1,0:T(8,128)(2,1)} %get-tuple-element.47), channel_id=1, source_target_pairs={{0,1},{1,0},{2,3},{3,2},{4,5},{5,4},{6,7},{7,6},{8,9},{9,8},{10,11... | collective-permute-start | bytes 1142792 | tf_op jit(solution)/shard_map/ppermute | solution.py:313
  6.0 14.1 %collective-permute-start.1 = (bf16[496,128]{1,0:T(8,128)(2,1)}, bf16[496,128]{1,0:T(8,128)(2,1)S(1)}, u32[]{:S(2)}, u32[]{:S(2)}) collective-permute-start(bf16[496,128]{1,0:T(8,128)(2,1)} %get-tuple-element.37), channel_id=1, source_target_pairs={{0,8},{1,9},{2,10},{3,11},{4,12},{5,13},{6,14},{7,15},{8,0},{9,1},... | collective-permute-start | bytes 380936 | tf_op jit(solution)/shard_map/ppermute | solution.py:313
  10.0 1.0 %copy-start.8 = (bf16[1488,128]{1,0:T(8,128)(2,1)S(1)}, bf16[1488,128]{1,0:T(8,128)(2,1)}, u32[]{:S(2)}) copy-start(bf16[1488,128]{1,0:T(8,128)(2,1)} %get-tuple-element.46.refs_0_) | copy-start | bytes 1142788
  11.0 5.2 %copy-start.6 = (bf16[512,768]{1,0:T(8,128)(2,1)S(1)}, bf16[512,768]{1,0:T(8,128)(2,1)}, u32[]{:S(2)}) copy-start(bf16[512,768]{1,0:T(8,128)(2,1)} %get-tuple-element.31.normed_ref) | copy-start | bytes 2359300
  11.1 13.2 %collective-permute-start.5 = (bf16[992,128]{1,0:T(8,128)(2,1)S(1)}, bf16[992,128]{1,0:T(8,128)(2,1)S(1)}, u32[]{:S(2)}, u32[]{:S(2)}) collective-permute-start(bf16[992,128]{1,0:T(8,128)(2,1)S(1)} %get-tuple-element.49), channel_id=1, source_target_pairs={{0,2},{1,3},{2,0},{3,1},{4,6},{5,7},{6,4},{7,5},{8,10},{9,11},{10,... | collective-permute-start | bytes 761864 | tf_op jit(solution)/shard_map/ppermute | solution.py:313
  12.6 1.0 %copy-start.7 = (bf16[1488,128]{1,0:T(8,128)(2,1)S(1)}, bf16[1488,128]{1,0:T(8,128)(2,1)}, u32[]{:S(2)}) copy-start(bf16[1488,128]{1,0:T(8,128)(2,1)} %get-tuple-element.33.from_ref) | copy-start | bytes 1142788
  13.6 3.4 %copy-start.3 = (bf16[512,768]{1,0:T(8,128)(2,1)S(1)}, bf16[512,768]{1,0:T(8,128)(2,1)}, u32[]{:S(2)}) copy-start(bf16[512,768]{1,0:T(8,128)(2,1)} %get-tuple-element.32.emb_ref) | copy-start | bytes 2359300
  13.8 3.2 %copy-start.2 = (bf16[768,768]{1,0:T(8,128)(2,1)S(1)}, bf16[768,768]{1,0:T(8,128)(2,1)}, u32[]{:S(2)}) copy-start(bf16[768,768]{1,0:T(8,128)(2,1)} %wo_ref.15) | copy-start | bytes 3538948
  13.9 21.6 %collective-permute-start.3 = (bf16[992,128]{1,0:T(8,128)(2,1)S(1)}, bf16[992,128]{1,0:T(8,128)(2,1)S(1)}, u32[]{:S(2)}, u32[]{:S(2)}) collective-permute-start(bf16[992,128]{1,0:T(8,128)(2,1)S(1)} %get-tuple-element.40), channel_id=1, source_target_pairs={{0,10},{1,11},{2,8},{3,9},{4,14},{5,15},{6,12},{7,13},{8,2},{9,3},... | collective-permute-start | bytes 761864 | tf_op jit(solution)/shard_map/ppermute | solution.py:313
  16.2 1.3 %copy-start = (bf16[768,768]{1,0:T(8,128)(2,1)S(1)}, bf16[768,768]{1,0:T(8,128)(2,1)}, u32[]{:S(2)}) copy-start(bf16[768,768]{1,0:T(8,128)(2,1)} %wk_ref.15) | copy-start | bytes 3538948
  16.2 1.6 %copy-start.1 = (bf16[768,768]{1,0:T(8,128)(2,1)S(1)}, bf16[768,768]{1,0:T(8,128)(2,1)}, u32[]{:S(2)}) copy-start(bf16[768,768]{1,0:T(8,128)(2,1)} %wv_ref.15) | copy-start | bytes 3538948
  16.2 1.6 %copy-start.4 = (bf16[768,28]{0,1:T(8,128)(2,1)S(1)}, bf16[768,28]{0,1:T(8,128)(2,1)}, u32[]{:S(2)}) copy-start(bf16[768,28]{0,1:T(8,128)(2,1)} %param.15) | copy-start | bytes 129028
  20.1 20.3 %collective-permute-start.2 = (bf16[992,128]{1,0:T(8,128)(2,1)S(1)}, bf16[992,128]{1,0:T(8,128)(2,1)S(1)}, u32[]{:S(2)}, u32[]{:S(2)}) collective-permute-start(bf16[992,128]{1,0:T(8,128)(2,1)S(1)} %get-tuple-element.38), channel_id=1, source_target_pairs={{0,12},{1,13},{2,14},{3,15},{4,8},{5,9},{6,10},{7,11},{8,4},{9,5},... | collective-permute-start | bytes 761864 | tf_op jit(solution)/shard_map/ppermute | solution.py:313
  22.0 19.6 %collective-permute-start.6 = (bf16[992,128]{1,0:T(8,128)(2,1)S(1)}, bf16[992,128]{1,0:T(8,128)(2,1)S(1)}, u32[]{:S(2)}, u32[]{:S(2)}) collective-permute-start(bf16[992,128]{1,0:T(8,128)(2,1)S(1)} %get-tuple-element.51), channel_id=1, source_target_pairs={{0,4},{1,5},{2,6},{3,7},{4,0},{5,1},{6,2},{7,3},{8,12},{9,13},{10,... | collective-permute-start | bytes 761864 | tf_op jit(solution)/shard_map/ppermute | solution.py:313
  24.3 26.3 %collective-permute-start.7 = (bf16[992,128]{1,0:T(8,128)(2,1)S(1)}, bf16[992,128]{1,0:T(8,128)(2,1)S(1)}, u32[]{:S(2)}, u32[]{:S(2)}) collective-permute-start(bf16[992,128]{1,0:T(8,128)(2,1)S(1)} %get-tuple-element.53), channel_id=1, source_target_pairs={{0,6},{1,7},{2,4},{3,5},{4,2},{5,3},{6,0},{7,1},{8,14},{9,15},{10,... | collective-permute-start | bytes 761864 | tf_op jit(solution)/shard_map/ppermute | solution.py:313
  35.5 17.7 %collective-permute-start.8 = (bf16[992,128]{1,0:T(8,128)(2,1)S(1)}, bf16[992,128]{1,0:T(8,128)(2,1)S(1)}, u32[]{:S(2)}, u32[]{:S(2)}) collective-permute-start(bf16[992,128]{1,0:T(8,128)(2,1)S(1)} %get-tuple-element.54), channel_id=1, source_target_pairs={{0,14},{1,15},{2,12},{3,13},{4,10},{5,11},{6,8},{7,9},{8,6},{9,7},... | collective-permute-start | bytes 761864 | tf_op jit(solution)/shard_map/ppermute | solution.py:313
  40.5 15.3 %collective-permute-start.9 = (bf16[496,128]{1,0:T(8,128)(2,1)S(1)}, bf16[496,128]{1,0:T(8,128)(2,1)S(1)}, u32[]{:S(2)}, u32[]{:S(2)}) collective-permute-start(bf16[496,128]{1,0:T(8,128)(2,1)S(1)} %get-tuple-element.55), channel_id=1, source_target_pairs={{0,8},{1,9},{2,10},{3,11},{4,12},{5,13},{6,14},{7,15},{8,0},{9,1},... | collective-permute-start | bytes 380936 | tf_op jit(solution)/shard_map/ppermute | solution.py:313

commit v5 on v4

--- a/solution.py
+++ b/solution.py
@@ -241,7 +241,7 @@
         return jax.ShapeDtypeStruct((count * tall, LANES), BF16)
 
     chips = groups // 2
-    far, near = list(range(chips // 2, chips)), list(range(1, chips // 2))
+    far, near = list(range(chips - 1, chips // 2 - 1, -1)), list(range(1, chips // 2))
     if by_permute:
         sets = [[2 * t + 1 for t in [0] + far], [2 * far[0]], [2 * t for t in far[1:]]]
         sets += [[2 * t + 1 for t in near], [2 * t for t in near]]
@@ -364,11 +364,11 @@
         totals = decode([got[far[1]]], [(0, 0), (0, 1)], totals, False)
         late, got[far[-2]], totals = lax.optimization_barrier((late, got[far[-2]], totals))
         last = permute(late, 2 * far[0])
-        plan = [near[:2], far[2:3], near[2:]] + [[t] for t in far[3:]]
+        plan = [near[:2], far[2:3], near[2:]] + [[t] for t in far[3:-1]]
         for pair in plan:
             parts = [(n, m) for n in range(len(pair)) for m in (0, 1)]
             totals = decode([got[t] for t in pair], parts, totals, False)
-        totals = decode([last], [(0, 0)], totals, True)
+        totals = decode([got[far[-1]], last], [(0, 0), (0, 1), (1, 0)], totals, True)
     else:
         got = lax.all_to_all(sends[0].reshape(groups, tall, LANES), "img", 0, 0, tiled=True)
         some = math.gcd(groups, max(1, LANES // span))

time: 59.2 us -> 58.1 us (0.981)
  starting transfers between devices: 16.7 us -> 25.6 us
  waiting for transfers between devices: 10.6 us -> 2.17 us
  Pallas kernels: 28 us -> 26.4 us
    ppermute x10, starting transfers between devices: 16.7 us -> 25.6 us  [permute(): return lax.ppermute(block, 'img', [(i, i ^ step) for i in range(groups)])]
    ppermute x10, waiting for transfers between devices: 10.6 us -> 2.17 us  [permute(): return lax.ppermute(block, 'img', [(i, i ^ step) for i in range(groups)])]
    pallas_call x8 -> x7, Pallas kernels: 22.2 us -> 20.6 us  [decode(): pl.pallas_call(functools.partial(decode_kernel, parts, per_owner, patches...]
  transfers between devices with their start and end apart: 10 -> 10, of which waited for: 2 -> 2; matrix products, arithmetic and copies ran while one was open for 0% -> 0% of each run, Pallas kernels for 34% -> 30%
where the time goes in v5:
time: 58.1 us; the launch traced here: 57.9 us
  Pallas kernels  26.4 us (45%)
  starting transfers between devices  25.6 us (44%)
  local copies, waits for them, and re-layouts  2.81 us (5%)
  waiting for transfers between devices  2.17 us (4%)
  between operations  0.83 us (1%)
    ppermute x10, starting transfers between devices, permute(): return lax.ppermute(block, 'img', [(i, i ^ step) for i in range(groups)])  25.6 us
    pallas_call x7, Pallas kernels, decode(): pl.pallas_call(functools.partial(decode_kernel, parts, per_owner, patches...  20.6 us
    pallas_call x1, Pallas kernels, per_device(): pl.pallas_call(functools.partial(embed_kernel, groups, per_owner, patches...  4.74 us
    unnamed x18, local copies, waits for them, and re-layouts  2.81 us
    ppermute x10, waiting for transfers between devices, permute(): return lax.ppermute(block, 'img', [(i, i ^ step) for i in range(groups)])  2.17 us
  transfers between devices with their start and end apart: 10, of which 2 were waited for; matrix products, arithmetic and copies ran while one was open for 0% of the time, Pallas kernels for 30%

profile of v5, /device:TPU:0, one launch (start us, length us, event | category | flops | bytes accessed | tf_op | source)
XLA Modules:
  0.0 57.9 jit_solution(4160238674290063162)
XLA Ops:
  0.6 0.0 copy-start.5
  0.6 4.7 %embed.1 = (bf16[512,768]{1,0:T(8,128)(2,1)}, bf16[512,768]{1,0:T(8,128)(2,1)}, bf16[2480,128]{1,0:T(8,128)(2,1)}, bf16[496,128]{1,0:T(8,128)(2,1)}, bf16[1488,1...) custom-call(s32[2,64]{1,0:T(2,128)} %bitcast.18, bf16[512,1024]{1,0:T(8,128)(2,1)} %bitcast.17, ...), custom_call_target="tpu_custom_call" | custom-call | flops 1 | bytes 1 | tf_op jit(solution)/shard_map/embed/pallas_call | solution.py:250
  5.4 0.5 collective-permute-start
  5.9 0.1 collective-permute-start.4
  6.0 6.0 %collective-permute-start.1 = (bf16[496,128]{1,0:T(8,128)(2,1)}, bf16[496,128]{1,0:T(8,128)(2,1)S(1)}, u32[]{:S(2)}, u32[]{:S(2)}) collective-permute-start(bf16[496,128]{1,0:T(8,128)(2,1)} %get-tuple-element.37), channel_id=1, source_target_pairs={{0,14},{1,15},{2,12},{3,13},{4,10},{5,11},{6,8},{7,9},{8,6},{9,7},... | collective-permute-start | bytes 380936 | tf_op jit(solution)/shard_map/ppermute | solution.py:313
  12.0 0.0 collective-permute-done.4.refs_1_
  12.0 0.0 copy-start.8
  12.0 1.0 %copy-done.8 = bf16[1488,128]{1,0:T(8,128)(2,1)S(1)} copy-done((bf16[1488,128]{1,0:T(8,128)(2,1)S(1)}, bf16[1488,128]{1,0:T(8,128)(2,1)}, u32[]{:S(2)}) %copy-start.8) | copy-done | bytes 380952
  13.0 0.0 copy-start.6
  13.0 0.1 join.3
  13.0 0.6 collective-permute-start.5
  13.6 0.0 copy-start.7
  13.6 1.0 %copy-done.7 = bf16[1488,128]{1,0:T(8,128)(2,1)S(1)} copy-done((bf16[1488,128]{1,0:T(8,128)(2,1)S(1)}, bf16[1488,128]{1,0:T(8,128)(2,1)}, u32[]{:S(2)}) %copy-start.7) | copy-done | bytes 380952
  14.6 0.0 copy-start.3
  14.6 0.2 load.1.refs_0_
  14.8 0.0 collective-permute-done.refs_1_.rest_0_
  14.8 0.0 copy-start.2
  14.8 0.1 join.2
  14.9 2.4 %collective-permute-start.3 = (bf16[992,128]{1,0:T(8,128)(2,1)S(1)}, bf16[992,128]{1,0:T(8,128)(2,1)S(1)}, u32[]{:S(2)}, u32[]{:S(2)}) collective-permute-start(bf16[992,128]{1,0:T(8,128)(2,1)S(1)} %get-tuple-element.40), channel_id=1, source_target_pairs={{0,12},{1,13},{2,14},{3,15},{4,8},{5,9},{6,10},{7,11},{8,4},{9,5},... | collective-permute-start | bytes 761864 | tf_op jit(solution)/shard_map/ppermute | solution.py:313
  17.3 0.0 copy-done.5
  17.3 0.0 copy-done.6
  17.3 0.0 copy-start.4
  17.3 0.8 %queries.1.query_ref = bf16[512,768]{1,0:T(8,128)(2,1)S(1)} custom-call(bf16[512,768]{1,0:T(8,128)(2,1)S(1)} %copy-done.6, bf16[768,768]{1,0:T(8,128)(2,1)S(1)} %copy-done.5), custom_call_target="tpu_custom_call" | custom-call | flops 1 | bytes 1 | tf_op jit(solution)/shard_map/queries/pallas_call | solution.py:272
  18.1 0.0 copy-done.3
  18.1 0.0 copy-done.2
  18.1 0.4 copy-done
  18.6 0.4 copy-done.1
  18.9 0.0 copy-done.4
  18.9 2.3 %decode.7.rest_0_ = f32[512,28]{1,0:T(8,128)S(1)} custom-call(bf16[512,768]{1,0:T(8,128)(2,1)S(1)} %queries.1.query_ref, bf16[512,768]{1,0:T(8,128)(2,1)S(1)} %copy-done.3, bf16[768,768]{1,0:T(8,128)(2,1)S(1)} %copy-done, bf16[768,768]{1,0:T(8,128)(2,1)S(1)} %copy-done.1, bf16[768,768]{1,0:T(8,128)(2,1)S(1)} %copy-done.2, bf16[28,768]{1,0:T(8,128)(2,1)S(1)} %bitcast.10, ...), custom_call_target="tpu_custom_call" | custom-call | flops 1 | bytes 1 | tf_op jit(solution)/shard_map/decode/pallas_call | solution.py:299
  21.2 0.0 collective-permute-done.1.rest_1_
  21.2 0.1 collective-permute-start.2
  21.3 3.0 %collective-permute-start.6 = (bf16[992,128]{1,0:T(8,128)(2,1)S(1)}, bf16[992,128]{1,0:T(8,128)(2,1)S(1)}, u32[]{:S(2)}, u32[]{:S(2)}) collective-permute-start(bf16[992,128]{1,0:T(8,128)(2,1)S(1)} %get-tuple-element.51), channel_id=1, source_target_pairs={{0,4},{1,5},{2,6},{3,7},{4,0},{5,1},{6,2},{7,3},{8,12},{9,13},{10,... | collective-permute-start | bytes 761864 | tf_op jit(solution)/shard_map/ppermute | solution.py:313
  24.3 2.3 %decode.8.rest_0_ = f32[512,28]{1,0:T(8,128)S(1)} custom-call(bf16[512,768]{1,0:T(8,128)(2,1)S(1)} %queries.1.query_ref, bf16[512,768]{1,0:T(8,128)(2,1)S(1)} %copy-done.3, bf16[768,768]{1,0:T(8,128)(2,1)S(1)} %copy-done, bf16[768,768]{1,0:T(8,128)(2,1)S(1)} %copy-done.1, bf16[768,768]{1,0:T(8,128)(2,1)S(1)} %copy-done.2, bf16[28,768]{1,0:T(8,128)(2,1)S(1)} %bitcast.11, ...), custom_call_target="tpu_custom_call" | custom-call | flops 1 | bytes 1 | tf_op jit(solution)/shard_map/decode/pallas_call | solution.py:299
  26.5 0.0 collective-permute-done.5.rest_1_
  26.5 0.1 collective-permute-start.7
  26.6 0.0 collective-permute-done.3.rest_1_
  26.6 9.5 %collective-permute-start.8 = (bf16[992,128]{1,0:T(8,128)(2,1)S(1)}, bf16[992,128]{1,0:T(8,128)(2,1)S(1)}, u32[]{:S(2)}, u32[]{:S(2)}) collective-permute-start(bf16[992,128]{1,0:T(8,128)(2,1)S(1)} %get-tuple-element.54), channel_id=1, source_target_pairs={{0,8},{1,9},{2,10},{3,11},{4,12},{5,13},{6,14},{7,15},{8,0},{9,1},... | collective-permute-start | bytes 761864 | tf_op jit(solution)/shard_map/ppermute | solution.py:313
  36.2 2.6 %decode.9.rest_0_ = f32[512,28]{1,0:T(8,128)S(1)} custom-call(bf16[512,768]{1,0:T(8,128)(2,1)S(1)} %queries.1.query_ref, bf16[512,768]{1,0:T(8,128)(2,1)S(1)} %copy-done.3, bf16[768,768]{1,0:T(8,128)(2,1)S(1)} %copy-done, bf16[768,768]{1,0:T(8,128)(2,1)S(1)} %copy-done.1, bf16[768,768]{1,0:T(8,128)(2,1)S(1)} %copy-done.2, bf16[28,768]{1,0:T(8,128)(2,1)S(1)} %bitcast.12, ...), custom_call_target="tpu_custom_call" | custom-call | flops 1 | bytes 1 | tf_op jit(solution)/shard_map/decode/pallas_call | solution.py:299
  38.8 1.5 %collective-permute-done.2.rest_1_ = bf16[992,128]{1,0:T(8,128)(2,1)S(1)} collective-permute-done((bf16[992,128]{1,0:T(8,128)(2,1)S(1)}, bf16[992,128]{1,0:T(8,128)(2,1)S(1)}, u32[]{:S(2)}, u32[]{:S(2)}) %collective-permute-start.2) | collective-permute-done | bytes 253984 | tf_op jit(solution)/shard_map/ppermute | solution.py:313
  40.3 3.4 %collective-permute-start.9 = (bf16[496,128]{1,0:T(8,128)(2,1)S(1)}, bf16[496,128]{1,0:T(8,128)(2,1)S(1)}, u32[]{:S(2)}, u32[]{:S(2)}) collective-permute-start(bf16[496,128]{1,0:T(8,128)(2,1)S(1)} %get-tuple-element.55), channel_id=1, source_target_pairs={{0,14},{1,15},{2,12},{3,13},{4,10},{5,11},{6,8},{7,9},{8,6},{9,7},... | collective-permute-start | bytes 380936 | tf_op jit(solution)/shard_map/ppermute | solution.py:313
  43.7 0.0 collective-permute-done.6.rest_2_
  43.8 4.0 %decode.10.rest_0_ = f32[512,28]{1,0:T(8,128)S(1)} custom-call(bf16[512,768]{1,0:T(8,128)(2,1)S(1)} %queries.1.query_ref, bf16[512,768]{1,0:T(8,128)(2,1)S(1)} %copy-done.3, bf16[768,768]{1,0:T(8,128)(2,1)S(1)} %copy-done, bf16[768,768]{1,0:T(8,128)(2,1)S(1)} %copy-done.1, bf16[768,768]{1,0:T(8,128)(2,1)S(1)} %copy-done.2, bf16[28,768]{1,0:T(8,128)(2,1)S(1)} %bitcast.13, ...), custom_call_target="tpu_custom_call" | custom-call | flops 1 | bytes 1 | tf_op jit(solution)/shard_map/decode/pallas_call | solution.py:299
  47.8 2.6 %decode.11.rest_0_ = f32[512,28]{1,0:T(8,128)S(1)} custom-call(bf16[512,768]{1,0:T(8,128)(2,1)S(1)} %queries.1.query_ref, bf16[512,768]{1,0:T(8,128)(2,1)S(1)} %copy-done.3, bf16[768,768]{1,0:T(8,128)(2,1)S(1)} %copy-done, bf16[768,768]{1,0:T(8,128)(2,1)S(1)} %copy-done.1, bf16[768,768]{1,0:T(8,128)(2,1)S(1)} %copy-done.2, bf16[28,768]{1,0:T(8,128)(2,1)S(1)} %bitcast.14, ...), custom_call_target="tpu_custom_call" | custom-call | flops 1 | bytes 1 | tf_op jit(solution)/shard_map/decode/pallas_call | solution.py:299
  50.4 0.0 collective-permute-done.7.rest_1_
  50.4 2.6 %decode.12.rest_0_ = f32[512,28]{1,0:T(8,128)S(1)} custom-call(bf16[512,768]{1,0:T(8,128)(2,1)S(1)} %queries.1.query_ref, bf16[512,768]{1,0:T(8,128)(2,1)S(1)} %copy-done.3, bf16[768,768]{1,0:T(8,128)(2,1)S(1)} %copy-done, bf16[768,768]{1,0:T(8,128)(2,1)S(1)} %copy-done.1, bf16[768,768]{1,0:T(8,128)(2,1)S(1)} %copy-done.2, bf16[28,768]{1,0:T(8,128)(2,1)S(1)} %bitcast.15, ...), custom_call_target="tpu_custom_call" | custom-call | flops 1 | bytes 1 | tf_op jit(solution)/shard_map/decode/pallas_call | solution.py:299
  53.1 0.0 collective-permute-done.9.rest_2_
  53.1 0.6 %collective-permute-done.8.rest_1_ = bf16[992,128]{1,0:T(8,128)(2,1)S(1)} collective-permute-done((bf16[992,128]{1,0:T(8,128)(2,1)S(1)}, bf16[992,128]{1,0:T(8,128)(2,1)S(1)}, u32[]{:S(2)}, u32[]{:S(2)}) %collective-permute-start.8) | collective-permute-done | bytes 253984 | tf_op jit(solution)/shard_map/ppermute | solution.py:313
  53.7 4.2 %decode.13 = (f32[48,32]{1,0:T(8,128)}, f32[384,32]{1,0:T(8,128)}, f32[16,32]{1,0:T(8,128)}) custom-call(bf16[512,768]{1,0:T(8,128)(2,1)S(1)} %queries.1.query_ref, bf16[512,768]{1,0:T(8,128)(2,1)S(1)} %copy-done.3, bf16[768,768]{1,0:T(8,128)(2,1)S(1)} %copy-done, bf16[768,768]{1,0:T(8,128)(2,1)S(1)} %copy-done.1, bf16[768,768]{1,0:T(8,128)(2,1)S(1)} %copy-done.2, ...), custom_call_target="tpu_custom_call" | custom-call | flops 1 | bytes 1 | tf_op jit(solution)/shard_map/decode/pallas_call | solution.py:299
  (2 shorter events, 0.0 us)
Async XLA Ops:
  0.6 16.7 %copy-start.5 = (bf16[768,768]{1,0:T(8,128)(2,1)S(1)}, bf16[768,768]{1,0:T(8,128)(2,1)}, u32[]{:S(2)}) copy-start(bf16[768,768]{1,0:T(8,128)(2,1)} %w_ref.1) | copy-start | bytes 3538948
  5.4 9.4 %collective-permute-start = (bf16[2480,128]{1,0:T(8,128)(2,1)}, bf16[2480,128]{1,0:T(8,128)(2,1)S(1)}, u32[]{:S(2)}, u32[]{:S(2)}) collective-permute-start(bf16[2480,128]{1,0:T(8,128)(2,1)} %get-tuple-element.34), channel_id=1, source_target_pairs={{0,1},{1,0},{2,3},{3,2},{4,5},{5,4},{6,7},{7,6},{8,9},{9,8},{10,11... | collective-permute-start | bytes 1904648 | tf_op jit(solution)/shard_map/ppermute | solution.py:313
  5.9 6.1 %collective-permute-start.4 = (bf16[1488,128]{1,0:T(8,128)(2,1)}, bf16[1488,128]{1,0:T(8,128)(2,1)S(1)}, u32[]{:S(2)}, u32[]{:S(2)}) collective-permute-start(bf16[1488,128]{1,0:T(8,128)(2,1)} %get-tuple-element.47), channel_id=1, source_target_pairs={{0,1},{1,0},{2,3},{3,2},{4,5},{5,4},{6,7},{7,6},{8,9},{9,8},{10,11... | collective-permute-start | bytes 1142792 | tf_op jit(solution)/shard_map/ppermute | solution.py:313
  6.0 15.2 %collective-permute-start.1 = (bf16[496,128]{1,0:T(8,128)(2,1)}, bf16[496,128]{1,0:T(8,128)(2,1)S(1)}, u32[]{:S(2)}, u32[]{:S(2)}) collective-permute-start(bf16[496,128]{1,0:T(8,128)(2,1)} %get-tuple-element.37), channel_id=1, source_target_pairs={{0,14},{1,15},{2,12},{3,13},{4,10},{5,11},{6,8},{7,9},{8,6},{9,7},... | collective-permute-start | bytes 380936 | tf_op jit(solution)/shard_map/ppermute | solution.py:313
  12.0 1.0 %copy-start.8 = (bf16[1488,128]{1,0:T(8,128)(2,1)S(1)}, bf16[1488,128]{1,0:T(8,128)(2,1)}, u32[]{:S(2)}) copy-start(bf16[1488,128]{1,0:T(8,128)(2,1)} %get-tuple-element.46.refs_0_) | copy-start | bytes 1142788
  13.0 4.3 %copy-start.6 = (bf16[512,768]{1,0:T(8,128)(2,1)S(1)}, bf16[512,768]{1,0:T(8,128)(2,1)}, u32[]{:S(2)}) copy-start(bf16[512,768]{1,0:T(8,128)(2,1)} %get-tuple-element.31.normed_ref) | copy-start | bytes 2359300
  13.0 13.5 %collective-permute-start.5 = (bf16[992,128]{1,0:T(8,128)(2,1)S(1)}, bf16[992,128]{1,0:T(8,128)(2,1)S(1)}, u32[]{:S(2)}, u32[]{:S(2)}) collective-permute-start(bf16[992,128]{1,0:T(8,128)(2,1)S(1)} %get-tuple-element.49), channel_id=1, source_target_pairs={{0,2},{1,3},{2,0},{3,1},{4,6},{5,7},{6,4},{7,5},{8,10},{9,11},{10,... | collective-permute-start | bytes 761864 | tf_op jit(solution)/shard_map/ppermute | solution.py:313
  13.6 1.0 %copy-start.7 = (bf16[1488,128]{1,0:T(8,128)(2,1)S(1)}, bf16[1488,128]{1,0:T(8,128)(2,1)}, u32[]{:S(2)}) copy-start(bf16[1488,128]{1,0:T(8,128)(2,1)} %get-tuple-element.33.from_ref) | copy-start | bytes 1142788
  14.6 3.5 %copy-start.3 = (bf16[512,768]{1,0:T(8,128)(2,1)S(1)}, bf16[512,768]{1,0:T(8,128)(2,1)}, u32[]{:S(2)}) copy-start(bf16[512,768]{1,0:T(8,128)(2,1)} %get-tuple-element.32.emb_ref) | copy-start | bytes 2359300
  14.8 3.3 %copy-start.2 = (bf16[768,768]{1,0:T(8,128)(2,1)S(1)}, bf16[768,768]{1,0:T(8,128)(2,1)}, u32[]{:S(2)}) copy-start(bf16[768,768]{1,0:T(8,128)(2,1)} %wo_ref.13) | copy-start | bytes 3538948
  14.9 11.8 %collective-permute-start.3 = (bf16[992,128]{1,0:T(8,128)(2,1)S(1)}, bf16[992,128]{1,0:T(8,128)(2,1)S(1)}, u32[]{:S(2)}, u32[]{:S(2)}) collective-permute-start(bf16[992,128]{1,0:T(8,128)(2,1)S(1)} %get-tuple-element.40), channel_id=1, source_target_pairs={{0,12},{1,13},{2,14},{3,15},{4,8},{5,9},{6,10},{7,11},{8,4},{9,5},... | collective-permute-start | bytes 761864 | tf_op jit(solution)/shard_map/ppermute | solution.py:313
  17.3 1.3 %copy-start = (bf16[768,768]{1,0:T(8,128)(2,1)S(1)}, bf16[768,768]{1,0:T(8,128)(2,1)}, u32[]{:S(2)}) copy-start(bf16[768,768]{1,0:T(8,128)(2,1)} %wk_ref.13) | copy-start | bytes 3538948
  17.3 1.6 %copy-start.1 = (bf16[768,768]{1,0:T(8,128)(2,1)S(1)}, bf16[768,768]{1,0:T(8,128)(2,1)}, u32[]{:S(2)}) copy-start(bf16[768,768]{1,0:T(8,128)(2,1)} %wv_ref.13) | copy-start | bytes 3538948
  17.3 1.6 %copy-start.4 = (bf16[768,28]{0,1:T(8,128)(2,1)S(1)}, bf16[768,28]{0,1:T(8,128)(2,1)}, u32[]{:S(2)}) copy-start(bf16[768,28]{0,1:T(8,128)(2,1)} %param.15) | copy-start | bytes 129028
  21.2 19.1 %collective-permute-start.2 = (bf16[992,128]{1,0:T(8,128)(2,1)S(1)}, bf16[992,128]{1,0:T(8,128)(2,1)S(1)}, u32[]{:S(2)}, u32[]{:S(2)}) collective-permute-start(bf16[992,128]{1,0:T(8,128)(2,1)S(1)} %get-tuple-element.38), channel_id=1, source_target_pairs={{0,10},{1,11},{2,8},{3,9},{4,14},{5,15},{6,12},{7,13},{8,2},{9,3},... | collective-permute-start | bytes 761864 | tf_op jit(solution)/shard_map/ppermute | solution.py:313
  21.3 22.5 %collective-permute-start.6 = (bf16[992,128]{1,0:T(8,128)(2,1)S(1)}, bf16[992,128]{1,0:T(8,128)(2,1)S(1)}, u32[]{:S(2)}, u32[]{:S(2)}) collective-permute-start(bf16[992,128]{1,0:T(8,128)(2,1)S(1)} %get-tuple-element.51), channel_id=1, source_target_pairs={{0,4},{1,5},{2,6},{3,7},{4,0},{5,1},{6,2},{7,3},{8,12},{9,13},{10,... | collective-permute-start | bytes 761864 | tf_op jit(solution)/shard_map/ppermute | solution.py:313
  26.5 23.9 %collective-permute-start.7 = (bf16[992,128]{1,0:T(8,128)(2,1)S(1)}, bf16[992,128]{1,0:T(8,128)(2,1)S(1)}, u32[]{:S(2)}, u32[]{:S(2)}) collective-permute-start(bf16[992,128]{1,0:T(8,128)(2,1)S(1)} %get-tuple-element.53), channel_id=1, source_target_pairs={{0,6},{1,7},{2,4},{3,5},{4,2},{5,3},{6,0},{7,1},{8,14},{9,15},{10,... | collective-permute-start | bytes 761864 | tf_op jit(solution)/shard_map/ppermute | solution.py:313
  26.6 27.1 %collective-permute-start.8 = (bf16[992,128]{1,0:T(8,128)(2,1)S(1)}, bf16[992,128]{1,0:T(8,128)(2,1)S(1)}, u32[]{:S(2)}, u32[]{:S(2)}) collective-permute-start(bf16[992,128]{1,0:T(8,128)(2,1)S(1)} %get-tuple-element.54), channel_id=1, source_target_pairs={{0,8},{1,9},{2,10},{3,11},{4,12},{5,13},{6,14},{7,15},{8,0},{9,1},... | collective-permute-start | bytes 761864 | tf_op jit(solution)/shard_map/ppermute | solution.py:313
  40.3 12.7 %collective-permute-start.9 = (bf16[496,128]{1,0:T(8,128)(2,1)S(1)}, bf16[496,128]{1,0:T(8,128)(2,1)S(1)}, u32[]{:S(2)}, u32[]{:S(2)}) collective-permute-start(bf16[496,128]{1,0:T(8,128)(2,1)S(1)} %get-tuple-element.55), channel_id=1, source_target_pairs={{0,14},{1,15},{2,12},{3,13},{4,10},{5,11},{6,8},{7,9},{8,6},{9,7},... | collective-permute-start | bytes 380936 | tf_op jit(solution)/shard_map/ppermute | solution.py:313
